TPU v7x, 256 devices: a whole 4x4x8 slice. The times are simulated.
256 devices in a mesh: group: 16 (over z, y_hi), node: 16 (over x, y_lo, core).
Axes of the slice: x: 4, y: 4 (y_hi: 2, y_lo: 2; y = y_hi * 2 + y_lo), z: 8, core: 2. Of those that a mesh axis runs over, the one named last changes fastest.
Arguments:
- grads: bfloat16 [256, 4194304], P(('group', 'node')), may hold values from -24 to 24
- master: float32 [4194304], P(('group', 'node')), may hold values from -6 to 6
- moment: float32 [4194304], P(('group', 'node')), may hold values from -6 to 6
- second: float32 [4194304], P(('group', 'node')), may hold values from 1 to 400
Outputs:
- master_out: float32 [4194304], P(('group', 'node'))
- moment_out: float32 [4194304], P(('group', 'node'))
- second_out: float32 [4194304], P(('group', 'node'))
All inputs are finite; a program needn't handle non-finite values.
Results may differ from a plain program's by a relative error of at most 0.0012.
Values may be sent and summed in bfloat16 or wider, within the bound.
No kernel may reach another device: no remote copies, remote signals or barrier semaphores. Data moves between devices by JAX's collectives and lax.ppermute only.
A program may use at most 128 MiB of HBM per device.

v0:
```python
import jax
import jax.numpy as jnp
from jax import lax
from jax.sharding import PartitionSpec as P

BLOCK = 512


def quantize(values):
    block_peak = jnp.max(jnp.abs(values), axis=-1)
    scales = jnp.full(block_peak.shape, 2.0 ** (-24), jnp.float32)
    for exponent in range(-24, 17):
        scales = jnp.where(
            block_peak > 127.0 * 2.0**exponent, jnp.float32(2.0 ** (exponent + 1)), scales
        )
    codes = jnp.floor(values / scales[..., None] + 0.5).astype(jnp.bfloat16)
    return (codes, scales.astype(jnp.bfloat16))


def dequantize(codes, scales):
    return codes.astype(jnp.float32) * scales.astype(jnp.float32)[..., None]


def body(grads, master, moment, second):
    group_count = lax.axis_size("group")
    node_count = lax.axis_size("node")
    shard_len = master.shape[0]
    block_count = shard_len // BLOCK
    local = grads.reshape(group_count, node_count, block_count, BLOCK).astype(jnp.float32)
    first_quant, first_scale = quantize(local)
    recv_quant, recv_scale = (
        lax.all_to_all(first_quant, "node", split_axis=1, concat_axis=1, tiled=True),
        lax.all_to_all(first_scale, "node", split_axis=1, concat_axis=1, tiled=True),
    )
    partial_value = jnp.sum(dequantize(recv_quant, recv_scale), axis=1)
    second_quant, second_scale = quantize(partial_value)
    owned_quant, owned_scale = (
        lax.all_to_all(second_quant, "group", split_axis=0, concat_axis=0, tiled=True),
        lax.all_to_all(second_scale, "group", split_axis=0, concat_axis=0, tiled=True),
    )
    summed = jnp.sum(dequantize(owned_quant, owned_scale), axis=0)
    gradient = summed.reshape(shard_len)
    moment_out = 0.9 * moment + 0.1 * gradient
    second_out = 0.95 * second + 0.05 * gradient * gradient
    master_out = master - 0.02 * (moment_out / (jnp.sqrt(second_out) + 1e-08) + 0.1 * master)
    return (master_out, moment_out, second_out)


def solution(mesh):
    in_specs = (
        P(("group", "node"), None),
        P(("group", "node")),
        P(("group", "node")),
        P(("group", "node")),
    )
    out_specs = (P(("group", "node")), P(("group", "node")), P(("group", "node")))
    return jax.shard_map(body, mesh=mesh, in_specs=in_specs, out_specs=out_specs, check_vma=False)
```

profile of v0, /device:TPU:12, one launch (start us, length us, event | category | flops | bytes accessed | tf_op | source)
XLA Modules:
  0.0 384.8 jit_solution(5889862293639260206)
XLA Ops:
  0.6 146.1 %convert_reduce_fusion = f32[4194304]{0:T(1024)} fusion(bf16[1,4194304]{1,0:T(2,128)(2,1)} %param.4), kind=kLoop, calls=%fused_computation | loop fusion | flops 4194304 | bytes 25165824 | tf_op jit(solution)/shard_map/convert_element_type | solution.py:29
  146.7 18.2 %reshape.533 = f32[16,16,32,512]{3,2,1,0:T(8,128)} reshape(f32[4194304]{0:T(1024)} %convert_reduce_fusion) | data formatting | bytes 33554432 | tf_op jit(solution)/shard_map/convert_element_type | solution.py:29
  164.8 7.2 %abs_reduce_fusion = f32[16,16,32]{2,1,0:T(8,128)S(1)} fusion(f32[16,16,32,512]{3,2,1,0:T(8,128)} %reshape.533), kind=kLoop, calls=%fused_computation.3 | loop fusion | flops 8380416 | bytes 16809984 | tf_op jit(solution)/shard_map/reduce_max | solution.py:10
  172.0 0.4 fusion.21
  172.4 0.7 reshape.566
  173.2 5.7 %all-to-all-start.1 = ((bf16[16,2,256]{2,1,0:T(2,128)(2,1)}), bf16[16,2,256]{2,1,0:T(2,128)(2,1)S(1)}, u32[]{:S(2)}, u32[]{:S(2)}) async-start(bf16[16,2,256]{2,1,0:T(2,128)(2,1)} %reshape.566), calls=%async_computation.1 | async-start | bytes 32768 | tf_op jit(solution)/shard_map/all_to_all | solution.py:33
  178.9 9.8 %floor_convert_fusion = bf16[16,16,32,512]{3,2,1,0:T(8,128)(2,1)} fusion(f32[16,16,32,512]{3,2,1,0:T(8,128)} %reshape.533, f32[16,16,32]{2,1,0:T(8,128)S(1)} %get-tuple-element.34), kind=kLoop, calls=%fused_computation.2 | loop fusion | flops 16777216 | bytes 25198592 | tf_op jit(solution)/shard_map/convert_element_type | solution.py:16
  188.6 8.3 %copy.89 = bf16[16,16,32,512]{3,2,0,1:T(8,128)(2,1)} copy(bf16[16,16,32,512]{3,2,1,0:T(8,128)(2,1)} %floor_convert_fusion) | data formatting | bytes 16777216 | tf_op jit(solution)/shard_map/convert_element_type | solution.py:16
  196.9 0.0 copy-start
  196.9 0.0 copy-start.1
  196.9 0.0 copy-start.2
  196.9 0.0 all-to-all-done.1
  196.9 5.9 %all-to-all-start = ((bf16[16,16,32,512]{3,2,0,1:T(8,128)(2,1)}), bf16[16,16,32,512]{3,2,0,1:T(8,128)(2,1)}, u32[]{:S(2)}, u32[]{:S(2)}) async-start(bf16[16,16,32,512]{3,2,0,1:T(8,128)(2,1)} %copy.89), calls=%async_computation | async-start | bytes 16777216 | tf_op jit(solution)/shard_map/all_to_all | solution.py:32
  202.8 0.1 reshape.567
  202.9 133.1 %all-to-all-done = bf16[16,16,32,512]{3,2,0,1:T(8,128)(2,1)} async-done(((bf16[16,16,32,512]{3,2,0,1:T(8,128)(2,1)}), bf16[16,16,32,512]{3,2,0,1:T(8,128)(2,1)}, u32[]{:S(2)}, u32[]{:S(2)}) %all-to-all-start) | async-done | bytes 8388640 | tf_op jit(solution)/shard_map/all_to_all | solution.py:32
  336.0 5.0 %multiply_reduce_fusion = f32[16,32,512]{2,1,0:T(8,128)S(1)} fusion(bf16[16,16,32,512]{3,2,0,1:T(8,128)(2,1)} %all-to-all-done, f32[16,16,32]{2,0,1:T(8,128)S(1)} %bitcast_convert_fusion), kind=kLoop, calls=%fused_computation.1 | loop fusion | flops 12320768 | bytes 9469952 | tf_op jit(solution)/shard_map/reduce_sum | solution.py:35
  341.1 0.2 abs_reduce_fusion.1
  341.2 0.1 select_convert_fusion
  341.3 0.6 copy.91
  341.9 10.3 %all-to-all-start.3 = ((bf16[16,1,32]{2,1,0:T(2,128)(2,1)}), bf16[16,1,32]{2,1,0:T(2,128)(2,1)S(1)}, u32[]{:S(2)}, u32[]{:S(2)}) async-start(bf16[16,1,32]{2,1,0:T(2,128)(2,1)} %copy.91), calls=%async_computation.3 | async-start | bytes 16384 | tf_op jit(solution)/shard_map/all_to_all | solution.py:39
  352.3 1.0 floor_convert_fusion.1
  353.3 8.9 %all-to-all-done.3 = bf16[16,1,32]{2,1,0:T(2,128)(2,1)S(1)} async-done(((bf16[16,1,32]{2,1,0:T(2,128)(2,1)}), bf16[16,1,32]{2,1,0:T(2,128)(2,1)S(1)}, u32[]{:S(2)}, u32[]{:S(2)}) %all-to-all-start.3) | async-done | bytes 1056 | tf_op jit(solution)/shard_map/all_to_all | solution.py:39
  362.2 3.6 all-to-all-start.2
  365.8 18.1 %all-to-all-done.2 = bf16[16,32,512]{2,1,0:T(8,128)(2,1)S(1)} async-done(((bf16[16,32,512]{2,1,0:T(8,128)(2,1)}), bf16[16,32,512]{2,1,0:T(8,128)(2,1)S(1)}, u32[]{:S(2)}, u32[]{:S(2)}) %all-to-all-start.2) | async-done | bytes 524320 | tf_op jit(solution)/shard_map/all_to_all | solution.py:38
  383.9 0.2 multiply_reduce_fusion.1
  384.1 0.0 copy-done
  384.1 0.0 copy-done.1
  384.1 0.0 copy-done.2
  384.1 0.7 multiply_subtract_fusion
  (5 shorter events, 0.1 us)
Async XLA Ops:
  173.2 23.8 %all-to-all-start.1 = ((bf16[16,2,256]{2,1,0:T(2,128)(2,1)}), bf16[16,2,256]{2,1,0:T(2,128)(2,1)S(1)}, u32[]{:S(2)}, u32[]{:S(2)}) async-start(bf16[16,2,256]{2,1,0:T(2,128)(2,1)} %reshape.566), calls=%async_computation.1 | async-start | bytes 32768 | tf_op jit(solution)/shard_map/all_to_all | solution.py:33
  196.9 187.2 %copy-start = (f32[16384]{0:T(1024)S(1)}, f32[16384]{0:T(1024)}, u32[]{:S(2)}) copy-start(f32[16384]{0:T(1024)} %param.5) | copy-start | bytes 196612
  196.9 187.2 %copy-start.1 = (f32[16384]{0:T(1024)S(1)}, f32[16384]{0:T(1024)}, u32[]{:S(2)}) copy-start(f32[16384]{0:T(1024)} %param.7) | copy-start | bytes 196612
  196.9 187.2 %copy-start.2 = (f32[16384]{0:T(1024)S(1)}, f32[16384]{0:T(1024)}, u32[]{:S(2)}) copy-start(f32[16384]{0:T(1024)} %param.6) | copy-start | bytes 196612
  196.9 139.1 %all-to-all-start = ((bf16[16,16,32,512]{3,2,0,1:T(8,128)(2,1)}), bf16[16,16,32,512]{3,2,0,1:T(8,128)(2,1)}, u32[]{:S(2)}, u32[]{:S(2)}) async-start(bf16[16,16,32,512]{3,2,0,1:T(8,128)(2,1)} %copy.89), calls=%async_computation | async-start | bytes 16777216 | tf_op jit(solution)/shard_map/all_to_all | solution.py:32
  341.9 20.2 %all-to-all-start.3 = ((bf16[16,1,32]{2,1,0:T(2,128)(2,1)}), bf16[16,1,32]{2,1,0:T(2,128)(2,1)S(1)}, u32[]{:S(2)}, u32[]{:S(2)}) async-start(bf16[16,1,32]{2,1,0:T(2,128)(2,1)} %copy.91), calls=%async_computation.3 | async-start | bytes 16384 | tf_op jit(solution)/shard_map/all_to_all | solution.py:39
  362.2 21.7 %all-to-all-start.2 = ((bf16[16,32,512]{2,1,0:T(8,128)(2,1)}), bf16[16,32,512]{2,1,0:T(8,128)(2,1)S(1)}, u32[]{:S(2)}, u32[]{:S(2)}) async-start(bf16[16,32,512]{2,1,0:T(8,128)(2,1)} %floor_convert_fusion.1), calls=%async_computation.2 | async-start | bytes 1048576 | tf_op jit(solution)/shard_map/all_to_all | solution.py:38
where the time goes:
time: 386 us; the launch traced here: 385 us
  other arithmetic  171 us (44%)
  waiting for transfers between devices  160 us (41%)
  local copies, waits for them, and re-layouts  27.9 us (7%)
  starting transfers between devices  25.5 us (7%)
    convert_element_type x1, other arithmetic, body(): grads.reshape(group_count, node_count, block_count, BLOCK)  146 us
    all_to_all x1, waiting for transfers between devices, body(): lax.all_to_all(first_quant, 'node', split_axis=1, concat_axis=1, tiled=True)  133 us
    convert_element_type x1, local copies, waits for them, and re-layouts, body(): grads.reshape(group_count, node_count, block_count, BLOCK)  18.2 us
    all_to_all x1, waiting for transfers between devices, body(): lax.all_to_all(second_quant, 'group', split_axis=0, concat_axis=0, tiled=...  18.1 us
    convert_element_type x2, other arithmetic, quantize(): codes = jnp.floor(values / scales[..., None] + 0.5).astype(jnp.bfloat16)  10.8 us
    all_to_all x1, starting transfers between devices, body(): lax.all_to_all(second_scale, 'group', split_axis=0, concat_axis=0, tiled=...  10.3 us
    all_to_all x1, waiting for transfers between devices, body(): lax.all_to_all(second_scale, 'group', split_axis=0, concat_axis=0, tiled=...  8.87 us
    convert_element_type x1, local copies, waits for them, and re-layouts, quantize(): codes = jnp.floor(values / scales[..., None] + 0.5).astype(jnp.bfloat16)  8.26 us
  transfers between devices with their start and end apart: 4, of which 3 were waited for; matrix products, arithmetic and copies ran while one was open for 5% of the time, Pallas kernels for 0%

commit v1 on v0

v1 whole, which is shorter than its diff:
```python
import jax
import jax.numpy as jnp
from jax import lax
from jax.experimental import pallas as pl
from jax.experimental.pallas import tpu as pltpu
from jax.sharding import PartitionSpec as P

BLOCK = 512
LANES = 128
ROWS = BLOCK // LANES
GROUP_ROWS = 8 * ROWS
GROUP = GROUP_ROWS * LANES


def scale_of(peak):
    scale = jnp.full(peak.shape, 2.0**-24, jnp.float32)
    inverse = jnp.full(peak.shape, 2.0**24, jnp.float32)
    for k in (16, 8, 4, 2, 1):
        above = peak > scale * (127.0 * 2.0 ** (k - 1))
        scale = jnp.where(above, scale * 2.0**k, scale)
        inverse = jnp.where(above, inverse * 2.0**-k, inverse)
    return scale, inverse


def requantized(parts):
    peak = jnp.abs(parts[0])
    for part in parts[1:]:
        peak = jnp.maximum(peak, jnp.abs(part))
    peak = jnp.max(peak, axis=1, keepdims=True)
    scale, inverse = scale_of(jnp.broadcast_to(peak, parts[0].shape))
    return [jnp.floor(part * inverse + 0.5) * scale for part in parts]


def first_kernel(nodes, groups, x_ref, o_ref, scratch):
    def step(n, carry):
        for k in range(groups):
            at = pl.multiple_of((n * groups + k) * GROUP, GROUP)
            scratch[k] = x_ref[0:1, pl.ds(at, GROUP)].astype(jnp.float32).reshape(GROUP_ROWS, LANES)
        for k in range(groups):
            parts = [scratch[k, pl.ds(s, 8, stride=ROWS), :] for s in range(ROWS)]
            done = jnp.concatenate(requantized(parts), axis=0)
            o_ref[n, 0, k * GROUP_ROWS : (k + 1) * GROUP_ROWS, :] = done.astype(jnp.bfloat16)
        return carry

    lax.fori_loop(0, nodes, step, 0, unroll=2)


def second_kernel(nodes, groups, r_ref, o_ref):
    for k in range(groups):
        rows = slice(k * GROUP_ROWS, (k + 1) * GROUP_ROWS)
        total = r_ref[0, 0, rows, :].astype(jnp.float32)
        for n in range(1, nodes):
            total = total + r_ref[n, 0, rows, :].astype(jnp.float32)
        parts = [total[8 * s : 8 * s + 8] for s in range(ROWS)]
        done = jnp.concatenate(requantized(parts), axis=0)
        o_ref[0, rows, :] = done.astype(jnp.bfloat16)


def update_kernel(replicas, groups, r_ref, p_ref, m_ref, v_ref, po_ref, mo_ref, vo_ref, scratch):
    for k in range(groups):
        rows = slice(k * GROUP_ROWS, (k + 1) * GROUP_ROWS)
        total = r_ref[0, rows, :].astype(jnp.float32)
        for g in range(1, replicas):
            total = total + r_ref[g, rows, :].astype(jnp.float32)
        for s in range(ROWS):
            scratch[pl.ds(k * GROUP_ROWS + s, 8, stride=ROWS), :] = total[8 * s : 8 * s + 8]
    gradient = scratch[...]
    master = p_ref[...]
    moment = 0.9 * m_ref[...] + 0.1 * gradient
    second = 0.95 * v_ref[...] + 0.05 * gradient * gradient
    mo_ref[...] = moment
    vo_ref[...] = second
    po_ref[...] = master - 0.02 * (moment / (jnp.sqrt(second) + 1e-08) + 0.1 * master)


def body(grads, master, moment, second):
    replicas = lax.axis_size("group")
    nodes = lax.axis_size("node")
    shard = master.shape[0]
    rows = shard // LANES
    groups = shard // GROUP
    params = pltpu.CompilerParams(vmem_limit_bytes=32 << 20)
    first = pl.pallas_call(
        lambda *refs: first_kernel(nodes, groups, *refs),
        name="first_quantize",
        grid=(replicas,),
        in_specs=[pl.BlockSpec((1, nodes * shard), lambda g: (0, g))],
        out_specs=pl.BlockSpec((nodes, 1, rows, LANES), lambda g: (0, g, 0, 0)),
        out_shape=jax.ShapeDtypeStruct((nodes, replicas, rows, LANES), jnp.bfloat16),
        scratch_shapes=[pltpu.VMEM((groups, GROUP_ROWS, LANES), jnp.float32)],
        compiler_params=params,
    )(grads)
    received = lax.all_to_all(first, "node", split_axis=0, concat_axis=0, tiled=True)
    partial = pl.pallas_call(
        lambda *refs: second_kernel(nodes, groups, *refs),
        name="sum_and_requantize",
        grid=(replicas,),
        in_specs=[pl.BlockSpec((nodes, 1, rows, LANES), lambda g: (0, g, 0, 0))],
        out_specs=pl.BlockSpec((1, rows, LANES), lambda g: (g, 0, 0)),
        out_shape=jax.ShapeDtypeStruct((replicas, rows, LANES), jnp.bfloat16),
        compiler_params=params,
    )(received)
    owned = lax.all_to_all(partial, "group", split_axis=0, concat_axis=0, tiled=True)
    state = jax.ShapeDtypeStruct((rows, LANES), jnp.float32)
    outs = pl.pallas_call(
        lambda *refs: update_kernel(replicas, groups, *refs),
        name="adamw_update",
        out_shape=(state, state, state),
        scratch_shapes=[pltpu.VMEM((rows, LANES), jnp.float32)],
        compiler_params=params,
    )(owned, *(a.reshape(rows, LANES) for a in (master, moment, second)))
    return tuple(a.reshape(shard) for a in outs)


def solution(mesh):
    split = P(("group", "node"))
    in_specs = (P(("group", "node"), None), split, split, split)
    return jax.shard_map(
        body, mesh=mesh, in_specs=in_specs, out_specs=(split, split, split), check_vma=False
    )
```

time: 386 us -> 163 us (0.42)
  the two profiles are of different devices: /device:TPU:12 before, /device:TPU:2 now
where the time goes in v1:
time: 163 us; the launch traced here: 162 us
  blocking collectives  129 us (79%)
  Pallas kernels  33 us (20%)
    all_to_all x1, blocking collectives, body(): lax.all_to_all(first, 'node', split_axis=0, concat_axis=0, tiled=True)  98.4 us
    all_to_all x1, blocking collectives, body(): lax.all_to_all(partial, 'group', split_axis=0, concat_axis=0, tiled=True)  30.1 us
    pallas_call x1, Pallas kernels, body(): pl.pallas_call(lambda *refs: first_kernel(nodes, groups, *refs), name='fi...  28.9 us
    pallas_call x1, Pallas kernels, body(): pl.pallas_call(lambda *refs: second_kernel(nodes, groups, *refs), name='s...  3.34 us

profile of v1, /device:TPU:2, one launch (start us, length us, event | category | flops | bytes accessed | tf_op | source)
XLA Modules:
  0.0 162.2 jit_solution(8320451422768548258)
XLA Ops:
  0.6 28.9 %first_quantize.1 = bf16[16,16,128,128]{3,2,1,0:T(8,128)(2,1)S(1)} custom-call(bf16[1,4194304]{1,0:T(2,128)(2,1)} %refs_0_.1), custom_call_target="tpu_custom_call" | custom-call | tf_op jit(solution)/shard_map/first_quantize/pallas_call | solution.py:83
  29.5 98.4 %all_to_all.10.refs_0_ = bf16[16,16,128,128]{3,2,1,0:T(8,128)(2,1)S(1)} all-to-all(bf16[16,16,128,128]{3,2,1,0:T(8,128)(2,1)S(1)} %first_quantize.1), channel_id=1, replica_groups=mesh['group'=16,'node'=16] {'node'}, dimensions={0} | all-to-all | bytes 16777216 | tf_op jit(solution)/shard_map/all_to_all | solution.py:93
  128.0 0.0 copy-start
  128.0 0.0 copy-start.1
  128.0 0.0 copy-start.2
  128.0 3.3 %sum_and_requantize.1 = bf16[16,128,128]{2,1,0:T(8,128)(2,1)S(1)} custom-call(bf16[16,16,128,128]{3,2,1,0:T(8,128)(2,1)S(1)} %all_to_all.10.refs_0_), custom_call_target="tpu_custom_call" | custom-call | tf_op jit(solution)/shard_map/sum_and_requantize/pallas_call | solution.py:94
  131.3 30.1 %all_to_all.11.refs_0_ = bf16[16,128,128]{2,1,0:T(8,128)(2,1)S(1)} all-to-all(bf16[16,128,128]{2,1,0:T(8,128)(2,1)S(1)} %sum_and_requantize.1), channel_id=1, replica_groups=mesh['group'=16,'node'=16] {'group'}, dimensions={0} | all-to-all | bytes 1048576 | tf_op jit(solution)/shard_map/all_to_all | solution.py:103
  161.4 0.0 copy-done
  161.4 0.0 copy-done.1
  161.4 0.0 copy-done.2
  161.4 0.8 adamw_update.1
Async XLA Ops:
  128.0 33.5 %copy-start = (f32[16384]{0:T(1024)S(1)}, f32[16384]{0:T(1024)}, u32[]{:S(2)}) copy-start(f32[16384]{0:T(1024)} %param.5) | copy-start | bytes 196612
  128.0 33.5 %copy-start.1 = (f32[16384]{0:T(1024)S(1)}, f32[16384]{0:T(1024)}, u32[]{:S(2)}) copy-start(f32[16384]{0:T(1024)} %param.6) | copy-start | bytes 196612
  128.0 33.5 %copy-start.2 = (f32[16384]{0:T(1024)S(1)}, f32[16384]{0:T(1024)}, u32[]{:S(2)}) copy-start(f32[16384]{0:T(1024)} %param.7) | copy-start | bytes 196612

commit v2 on v1

v2 whole, which is shorter than its diff:
```python
import jax
import jax.numpy as jnp
from jax import lax
from jax.experimental import pallas as pl
from jax.experimental.pallas import tpu as pltpu
from jax.sharding import Mesh
from jax.sharding import PartitionSpec as P

BLOCK = 512
LANES = 128
ROWS = BLOCK // LANES
GROUP_ROWS = 8 * ROWS
GROUP = GROUP_ROWS * LANES
SEND_LANE = 64
AUX_ROWS = 16

RATIO = 64.0
STEPS = 72.0
OFFSET = 113.0

PARTS = (3, 5, 8)
PARAMS = pltpu.CompilerParams(vmem_limit_bytes=48 << 20)


def scale_of(peak):
    scale = jnp.full(peak.shape, 2.0**-24, jnp.float32)
    inverse = jnp.full(peak.shape, 2.0**24, jnp.float32)
    for k in (16, 8, 4, 2, 1):
        above = peak > scale * (127.0 * 2.0 ** (k - 1))
        scale = jnp.where(above, scale * 2.0**k, scale)
        inverse = jnp.where(above, inverse * 2.0**-k, inverse)
    return scale, inverse


def peak_of(parts):
    peak = jnp.abs(parts[0])
    for part in parts[1:]:
        peak = jnp.maximum(peak, jnp.abs(part))
    return jnp.max(peak, axis=1, keepdims=True)


def requantized(parts):
    scale, inverse = scale_of(jnp.broadcast_to(peak_of(parts), parts[0].shape))
    return [jnp.floor(part * inverse + 0.5) * scale for part in parts]


def pair_kernel(chips, groups, core_ref, x_ref, after_ref, own_ref, send_ref, scale_ref, scratch):
    del after_ref
    core = core_ref[0]
    lane = lax.broadcasted_iota(jnp.int32, (8, LANES), 1)
    where = [(d, half, k) for d in range(chips) for half in range(2) for k in range(groups)]

    for d, half, k in where:
        node = 2 * d + (core if half == 0 else 1 - core)
        at = pl.multiple_of((node * groups + k) * GROUP, GROUP)
        rows = x_ref[0:1, pl.ds(at, GROUP)].astype(jnp.float32).reshape(GROUP_ROWS, LANES)
        scratch[d, half * groups + k] = rows

    def parts_of(d, half, k):
        return [scratch[d, half * groups + k, pl.ds(s, 8, stride=ROWS), :] for s in range(ROWS)]

    tiles = [jnp.zeros((8, LANES), jnp.float32)] * groups
    for d, half, k in where:
        column = lane == half * SEND_LANE + d * groups + k
        tiles[k] = jnp.where(column, peak_of(parts_of(d, half, k)), tiles[k])
    tile = tiles[0]
    for k in range(1, groups):
        tile = jnp.maximum(tile, tiles[k])
    scale, inverse = scale_of(tile)
    scale_ref[0] = jnp.where(tile > 0, scale, 0.0)

    for d, half, k in where:
        at = half * SEND_LANE + d * groups + k
        s_col = jnp.broadcast_to(scale[:, at : at + 1], (8, LANES))
        i_col = jnp.broadcast_to(inverse[:, at : at + 1], (8, LANES))
        done = [jnp.floor(part * i_col + 0.5) * s_col for part in parts_of(d, half, k)]
        o_ref = send_ref if half else own_ref
        at = slice(k * GROUP_ROWS, (k + 1) * GROUP_ROWS)
        o_ref[d, 0, at, :] = jnp.concatenate(done, axis=0).astype(jnp.bfloat16)


def encode_kernel(
    chips, groups, count, own_ref, peer_ref, mine_ref, theirs_ref, before_ref, m_ref, flag_ref,
    buffer, aux, packed, bad, sems, aux_sem,
):
    g = pl.program_id(0)
    slot = lax.rem(g, 2)
    rows = groups * GROUP_ROWS
    lane = lax.broadcasted_iota(jnp.int32, (8, LANES), 1)

    def copy(step, at):
        where = m_ref.at[:, pl.ds(pl.multiple_of(step * rows, rows), rows), :]
        return pltpu.make_async_copy(buffer.at[at], where, sems.at[at])

    @pl.when(g == 0)
    def _():
        bad[...] = before_ref[...]
        packed[...] = jnp.ones_like(packed)

    @pl.when(g >= 2)
    def _():
        copy(g - 2, slot).wait()

    mine, theirs = mine_ref[0], pltpu.roll(theirs_ref[0], SEND_LANE, 1)
    high, low = jnp.maximum(mine, theirs), jnp.minimum(mine, theirs)
    bad[...] = jnp.where((low > 0) & (high > RATIO * low), 1.0, bad[...])
    scale, inverse = scale_of(127.0 * high)
    weight = inverse * (RATIO / STEPS)

    for d in range(chips):
        tile = packed[d]
        for k in range(groups):
            column = slice(d * groups + k, d * groups + k + 1)
            tile = jnp.where(lane == g * groups + k, scale[:, column], tile)
            w_col = jnp.broadcast_to(weight[:, column], (8, LANES))
            at = slice(k * GROUP_ROWS, (k + 1) * GROUP_ROWS)
            total = own_ref[d, 0, at, :].astype(jnp.float32) + peer_ref[d, 0, at, :].astype(jnp.float32)
            out = []
            for s in range(ROWS):
                part = total[8 * s : 8 * s + 8]
                code = jnp.exp2(jnp.abs(part) * w_col - OFFSET)
                out.append(jnp.where(part < 0, -code, code))
            buffer[slot, d, at, :] = jnp.concatenate(out, axis=0).astype(jnp.bfloat16)
        packed[d] = tile
    copy(g, slot).start()

    @pl.when(g == count - 1)
    def _():
        flag = jnp.max(bad[...])
        flag_ref[...] = bad[...]
        for d in range(chips):
            unit = packed[d] * jnp.where(flag > 0, jnp.float32(jnp.nan), 1.0 / RATIO)
            aux[d] = jnp.concatenate([unit, unit], axis=0).astype(jnp.bfloat16)
        last = pltpu.make_async_copy(aux, m_ref.at[:, pl.ds(count * rows, AUX_ROWS), :], aux_sem)
        last.start()
        last.wait()
        if count >= 2:
            copy(g - 1, 1 - slot).wait()
        copy(g, slot).wait()


def decode_kernel(chips, groups, r_ref, aux_ref, o_ref, units):
    g = pl.program_id(0)

    @pl.when(g == 0)
    def _():
        for d in range(chips):
            units[d] = aux_ref[d].astype(jnp.float32)[0:8]

    rolled = [pltpu.roll(units[d], LANES - g * groups, 1) for d in range(chips)]
    for k in range(groups):
        at = slice(k * GROUP_ROWS, (k + 1) * GROUP_ROWS)
        total = [jnp.zeros((8, LANES), jnp.float32)] * ROWS
        for d in range(chips):
            unit = jnp.broadcast_to(rolled[d][:, k : k + 1], (8, LANES))
            code = r_ref[d, at, :].astype(jnp.float32)
            for s in range(ROWS):
                part = code[8 * s : 8 * s + 8]
                size = jnp.floor(jnp.log2(jnp.abs(part)) * STEPS + (OFFSET * STEPS + 0.5))
                total[s] = total[s] + size * jnp.where(part < 0, -unit, unit)
        o_ref[0, at, :] = jnp.concatenate(requantized(total), axis=0).astype(jnp.bfloat16)


def first_kernel(nodes, groups, after_ref, x_ref, o_ref, scratch):
    del after_ref

    def step(n, carry):
        for k in range(groups):
            at = pl.multiple_of((n * groups + k) * GROUP, GROUP)
            scratch[k] = x_ref[0:1, pl.ds(at, GROUP)].astype(jnp.float32).reshape(GROUP_ROWS, LANES)
        for k in range(groups):
            parts = [scratch[k, pl.ds(s, 8, stride=ROWS), :] for s in range(ROWS)]
            done = jnp.concatenate(requantized(parts), axis=0)
            o_ref[n, 0, k * GROUP_ROWS : (k + 1) * GROUP_ROWS, :] = done.astype(jnp.bfloat16)
        return carry

    lax.fori_loop(0, nodes, step, 0)


def second_kernel(nodes, groups, r_ref, o_ref):
    for k in range(groups):
        rows = slice(k * GROUP_ROWS, (k + 1) * GROUP_ROWS)
        total = r_ref[0, 0, rows, :].astype(jnp.float32)
        for n in range(1, nodes):
            total = total + r_ref[n, 0, rows, :].astype(jnp.float32)
        parts = [total[8 * s : 8 * s + 8] for s in range(ROWS)]
        o_ref[0, rows, :] = jnp.concatenate(requantized(parts), axis=0).astype(jnp.bfloat16)


def update_kernel(replicas, groups, r_ref, p_ref, m_ref, v_ref, po_ref, mo_ref, vo_ref, scratch):
    for k in range(groups):
        rows = slice(k * GROUP_ROWS, (k + 1) * GROUP_ROWS)
        total = r_ref[0, rows, :].astype(jnp.float32)
        for g in range(1, replicas):
            total = total + r_ref[g, rows, :].astype(jnp.float32)
        for s in range(ROWS):
            scratch[pl.ds(k * GROUP_ROWS + s, 8, stride=ROWS), :] = total[8 * s : 8 * s + 8]
    gradient = scratch[...]
    master = p_ref[...]
    moment = 0.9 * m_ref[...] + 0.1 * gradient
    second = 0.95 * v_ref[...] + 0.05 * gradient * gradient
    mo_ref[...] = moment
    vo_ref[...] = second
    po_ref[...] = master - 0.02 * (moment / (jnp.sqrt(second) + 1e-08) + 0.1 * master)


COST = pl.CostEstimate(flops=1, bytes_accessed=1, transcendentals=0)


def pair_sums(grads, start, count, replicas, chips, shard, before):
    rows, groups = shard // LANES, shard // GROUP
    nodes = 2 * chips
    core = lax.axis_index("core").astype(jnp.int32).reshape(1)
    half = jax.ShapeDtypeStruct((chips, count, rows, LANES), jnp.bfloat16)
    half_spec = pl.BlockSpec((chips, 1, rows, LANES), lambda g: (0, g, 0, 0))
    tile_spec = pl.BlockSpec((1, 8, LANES), lambda g: (g, 0, 0))
    own, send, scales = pl.pallas_call(
        lambda *refs: pair_kernel(chips, groups, *refs),
        name="quantize",
        grid=(count,),
        in_specs=[
            pl.BlockSpec(memory_space=pltpu.SMEM),
            pl.BlockSpec((1, nodes * shard), lambda g: (0, g + start)),
            pl.BlockSpec(memory_space=pl.ANY),
        ],
        out_specs=[half_spec, half_spec, tile_spec],
        out_shape=[half, half, jax.ShapeDtypeStruct((count, 8, LANES), jnp.float32)],
        scratch_shapes=[pltpu.VMEM((chips, 2 * groups, GROUP_ROWS, LANES), jnp.float32)],
        compiler_params=PARAMS,
        cost_estimate=COST,
    )(core, grads, before)
    swap = [(0, 1), (1, 0)]
    peer_scales = lax.ppermute(scales, "core", swap)
    peer = lax.ppermute(send, "core", swap)
    flag = jax.ShapeDtypeStruct((8, LANES), jnp.float32)
    whole = pl.BlockSpec((8, LANES), lambda g: (0, 0))
    return pl.pallas_call(
        lambda *refs: encode_kernel(chips, groups, count, *refs),
        name="add_and_encode",
        grid=(count,),
        in_specs=[half_spec, half_spec, tile_spec, tile_spec, whole],
        out_specs=[pl.BlockSpec(memory_space=pl.ANY), whole],
        out_shape=[
            jax.ShapeDtypeStruct((chips, count * rows + AUX_ROWS, LANES), jnp.bfloat16), flag,
        ],
        scratch_shapes=[
            pltpu.VMEM((2, chips, rows, LANES), jnp.bfloat16),
            pltpu.VMEM((chips, AUX_ROWS, LANES), jnp.bfloat16),
            pltpu.VMEM((chips, 8, LANES), jnp.float32),
            pltpu.VMEM((8, LANES), jnp.float32),
            pltpu.SemaphoreType.DMA((2,)),
            pltpu.SemaphoreType.DMA,
        ],
        compiler_params=PARAMS,
        cost_estimate=COST,
    )(own, peer, scales, peer_scales, before)


def node_sums(received, count, chips, shard):
    rows, groups = shard // LANES, shard // GROUP
    return pl.pallas_call(
        lambda *refs: decode_kernel(chips, groups, *refs),
        name="decode_and_requantize",
        grid=(count,),
        in_specs=[
            pl.BlockSpec((chips, rows, LANES), lambda g: (0, g, 0)),
            pl.BlockSpec((chips, AUX_ROWS, LANES), lambda g: (0, count * rows // AUX_ROWS, 0)),
        ],
        out_specs=pl.BlockSpec((1, rows, LANES), lambda g: (g, 0, 0)),
        out_shape=jax.ShapeDtypeStruct((count, rows, LANES), jnp.bfloat16),
        scratch_shapes=[pltpu.VMEM((chips, 8, LANES), jnp.float32)],
        compiler_params=PARAMS,
        cost_estimate=COST,
    )(received, received)


def plain_sums(grads, after, replicas, nodes, shard):
    rows, groups = shard // LANES, shard // GROUP
    first = pl.pallas_call(
        lambda *refs: first_kernel(nodes, groups, *refs),
        name="plain_quantize",
        grid=(replicas,),
        in_specs=[
            pl.BlockSpec(memory_space=pltpu.SMEM),
            pl.BlockSpec((1, nodes * shard), lambda g: (0, g)),
        ],
        out_specs=pl.BlockSpec((nodes, 1, rows, LANES), lambda g: (0, g, 0, 0)),
        out_shape=jax.ShapeDtypeStruct((nodes, replicas, rows, LANES), jnp.bfloat16),
        scratch_shapes=[pltpu.VMEM((groups, GROUP_ROWS, LANES), jnp.float32)],
        compiler_params=PARAMS,
    )(after, grads)
    received = lax.all_to_all(first, ("chip", "core"), split_axis=0, concat_axis=0, tiled=True)
    partial = pl.pallas_call(
        lambda *refs: second_kernel(nodes, groups, *refs),
        name="plain_requantize",
        grid=(replicas,),
        in_specs=[pl.BlockSpec((nodes, 1, rows, LANES), lambda g: (0, g, 0, 0))],
        out_specs=pl.BlockSpec((1, rows, LANES), lambda g: (g, 0, 0)),
        out_shape=jax.ShapeDtypeStruct((replicas, rows, LANES), jnp.bfloat16),
        compiler_params=PARAMS,
    )(received)
    return lax.all_to_all(partial, "group", split_axis=0, concat_axis=0, tiled=True)


def update(owned, master, moment, second):
    replicas, rows = owned.shape[:2]
    state = jax.ShapeDtypeStruct((rows, LANES), jnp.float32)
    return pl.pallas_call(
        lambda *refs: update_kernel(replicas, rows // GROUP_ROWS, *refs),
        name="adamw_update",
        out_shape=(state, state, state),
        scratch_shapes=[pltpu.VMEM((rows, LANES), jnp.float32)],
        compiler_params=PARAMS,
    )(owned, master, moment, second)


def body(grads, master, moment, second):
    replicas = lax.axis_size("group")
    chips = lax.axis_size("chip")
    shard = master.shape[0]
    flag = jnp.zeros((8, LANES), jnp.float32)
    partials, start = [], 0
    for count in PARTS:
        message, flag = pair_sums(grads, start, count, replicas, chips, shard, flag)
        received = lax.all_to_all(message, "chip", split_axis=0, concat_axis=0, tiled=True)
        partials.append(node_sums(received, count, chips, shard))
        start += count
    partial = jnp.concatenate(partials, axis=0) + partials[-1][0, 0, 0] * 0
    owned = lax.all_to_all(partial, "group", split_axis=0, concat_axis=0, tiled=True)
    state = [a.reshape(shard // LANES, LANES) for a in (master, moment, second)]
    owned, _ = lax.while_loop(
        lambda carry: jnp.logical_and(carry[1] == 0, jnp.any(jnp.isnan(carry[0][:, 0, 0]))),
        lambda carry: (
            plain_sums(grads, carry[1].reshape(1), replicas, 2 * chips, shard), carry[1] + 1,
        ),
        (owned, jnp.int32(0)),
    )
    return tuple(a.reshape(shard) for a in update(owned, *state))


def solution(mesh):
    groups, nodes = mesh.devices.shape
    cores = Mesh(mesh.devices.reshape(groups, nodes // 2, 2), ("group", "chip", "core"))
    split = P(("group", "chip", "core"))
    in_specs = (P(("group", "chip", "core"), None), split, split, split)
    return jax.shard_map(
        body, mesh=cores, in_specs=in_specs, out_specs=(split, split, split), check_vma=False
    )
```

time: 163 us -> 149 us (0.914)
  blocking collectives: 129 us -> 18.2 us
  waiting for transfers between devices: 0 us -> 52.8 us
  starting transfers between devices: 0 us -> 22.3 us
  Pallas kernels: 33 us -> 44.7 us
  local copies, waits for them, and re-layouts: 0.01 us -> 4.9 us
  other arithmetic: 0 us -> 2.34 us
    all_to_all x2 -> x1, blocking collectives: 129 us -> 18.2 us  [body(): lax.all_to_all(message, 'chip', split_axis=0, concat_axis=0, tiled=True)]
    all_to_all x0 -> x3, waiting for transfers between devices: none -> 47.2 us  [the longest x2 29.9 us: body(): lax.all_to_all(message, 'chip', split_axis=0, concat_axis=0, tiled=True)]
    all_to_all x0 -> x3, starting transfers between devices: none -> 21 us  [the longest x1 10.9 us: body(): lax.all_to_all(partial, 'group', split_axis=0, concat_axis=0, tiled=True)]
    pallas_call x3 -> x10, Pallas kernels: 33 us -> 44.7 us  [the longest x3 24.9 us: pair_sums(): pl.pallas_call(lambda *refs: pair_kernel(chips, groups, *refs), name='qua...]
    ppermute x0 -> x6, waiting for transfers between devices: none -> 5.56 us  [the longest x3 5.55 us: pair_sums(): peer_scales = lax.ppermute(scales, 'core', swap)]
    unnamed x6 -> x20, local copies, waits for them, and re-layouts: 0.01 us -> 4.39 us
  transfers between devices with their start and end apart: 0 -> 9, of which waited for: 0 -> 6; matrix products, arithmetic and copies ran while one was open for 0% -> 0% of each run, Pallas kernels for 0% -> 7%
where the time goes in v2:
time: 149 us; the launch traced here: 147 us
  waiting for transfers between devices  52.8 us (35%)
  Pallas kernels  44.7 us (30%)
  starting transfers between devices  22.3 us (15%)
  blocking collectives  18.2 us (12%)
  local copies, waits for them, and re-layouts  4.9 us (3%)
  other arithmetic  2.34 us (2%)
    all_to_all x2, waiting for transfers between devices, body(): lax.all_to_all(message, 'chip', split_axis=0, concat_axis=0, tiled=True)  29.9 us
    pallas_call x3, Pallas kernels, pair_sums(): pl.pallas_call(lambda *refs: pair_kernel(chips, groups, *refs), name='qua...  24.9 us
    all_to_all x1, blocking collectives, body(): lax.all_to_all(message, 'chip', split_axis=0, concat_axis=0, tiled=True)  18.2 us
    all_to_all x1, waiting for transfers between devices, body(): lax.all_to_all(partial, 'group', split_axis=0, concat_axis=0, tiled=True)  17.3 us
    all_to_all x1, starting transfers between devices, body(): lax.all_to_all(partial, 'group', split_axis=0, concat_axis=0, tiled=True)  10.9 us
    pallas_call x3, Pallas kernels, pair_sums(): pl.pallas_call(lambda *refs: encode_kernel(chips, groups, count, *refs),...  10.8 us
    all_to_all x2, starting transfers between devices, body(): lax.all_to_all(message, 'chip', split_axis=0, concat_axis=0, tiled=True)  10.1 us
    pallas_call x3, Pallas kernels, node_sums(): pl.pallas_call(lambda *refs: decode_kernel(chips, groups, *refs), name='d...  7.17 us
  transfers between devices with their start and end apart: 9, of which 6 were waited for; matrix products, arithmetic and copies ran while one was open for 0% of the time, Pallas kernels for 7%

profile of v2, /device:TPU:2, one launch (start us, length us, event | category | flops | bytes accessed | tf_op | source)
XLA Modules:
  0.0 147.3 jit_solution(10039501593147781162)
XLA Ops:
  0.6 5.1 %quantize.3 = (bf16[8,3,128,128]{3,2,1,0:T(8,128)(2,1)S(1)}, bf16[8,3,128,128]{3,2,1,0:T(8,128)(2,1)S(1)}, f32[3,8,128]{2,1,0:T(8,128)S(1)}) custom-call(s32[1]{0:T(128)} %bitcast.1.refs_0_, bf16[1,4194304]{1,0:T(2,128)(2,1)} %refs_1_.5, f32[8,128]{1,0:T(8,128)S(1)} %broadcast_in_dim.3.refs_2_.refs_4_), custom_call_target="tpu_custom_call" | custom-call | flops 1 | bytes 1 | tf_op jit(solution)/shard_map/quantize/pallas_call | solution.py:217
  5.7 0.1 collective-permute-start
  5.8 0.5 collective-permute-start.1
  6.3 1.8 %collective-permute-done.1.refs_3_ = f32[3,8,128]{2,1,0:T(8,128)S(1)} collective-permute-done((f32[3,8,128]{2,1,0:T(8,128)S(1)}, f32[3,8,128]{2,1,0:T(8,128)S(1)}, u32[]{:S(2)}, u32[]{:S(2)}) %collective-permute-start.1) | collective-permute-done | bytes 12320 | tf_op jit(solution)/shard_map/ppermute | solution.py:233
  8.1 0.0 collective-permute-done.refs_1_
  8.1 1.4 add_and_encode.3
  9.5 7.6 %quantize.4 = (bf16[8,5,128,128]{3,2,1,0:T(8,128)(2,1)S(1)}, bf16[8,5,128,128]{3,2,1,0:T(8,128)(2,1)S(1)}, f32[5,8,128]{2,1,0:T(8,128)S(1)}) custom-call(s32[1]{0:T(128)} %bitcast.1.refs_0_, bf16[1,4194304]{1,0:T(2,128)(2,1)} %refs_1_.5, f32[8,128]{1,0:T(8,128)S(1)} %get-tuple-element.41.refs_2_.refs_4_), custom_call_target="tpu_custom_call" | custom-call | flops 1 | bytes 1 | tf_op jit(solution)/shard_map/quantize/pallas_call | solution.py:217
  17.1 0.2 collective-permute-start.2
  17.3 0.4 collective-permute-start.3
  17.7 2.6 %collective-permute-done.3.refs_3_ = f32[5,8,128]{2,1,0:T(8,128)S(1)} collective-permute-done((f32[5,8,128]{2,1,0:T(8,128)S(1)}, f32[5,8,128]{2,1,0:T(8,128)S(1)}, u32[]{:S(2)}, u32[]{:S(2)}) %collective-permute-start.3) | collective-permute-done | bytes 20512 | tf_op jit(solution)/shard_map/ppermute | solution.py:233
  20.3 0.0 collective-permute-done.2.refs_1_
  20.3 2.2 %add_and_encode.4 = (bf16[8,656,128]{2,1,0:T(8,128)(2,1)S(1)}, f32[8,128]{1,0:T(8,128)S(1)}) custom-call(bf16[8,5,128,128]{3,2,1,0:T(8,128)(2,1)S(1)} %get-tuple-element.42.refs_0_, bf16[8,5,128,128]{3,2,1,0:T(8,128)(2,1)S(1)} %collective-permute-done.2.refs_1_, f32[5,8,128]{2,1,0:T(8,128)S(1)} %get-tuple-element.44.refs_2_, ...), custom_call_target="tpu_custom_call" | custom-call | flops 1 | bytes 1 | tf_op jit(solution)/shard_map/add_and_encode/pallas_call | solution.py:237
  22.4 0.0 copy-start.1
  22.4 1.1 copy-done.1
  23.5 12.2 %quantize.5 = (bf16[8,8,128,128]{3,2,1,0:T(8,128)(2,1)S(1)}, bf16[8,8,128,128]{3,2,1,0:T(8,128)(2,1)}, f32[8,8,128]{2,1,0:T(8,128)S(1)}) custom-call(s32[1]{0:T(128)} %bitcast.1.refs_0_, bf16[1,4194304]{1,0:T(2,128)(2,1)} %refs_1_.5, f32[8,128]{1,0:T(8,128)S(1)} %get-tuple-element.46.refs_2_.refs_4_), custom_call_target="tpu_custom_call" | custom-call | flops 1 | bytes 1 | tf_op jit(solution)/shard_map/quantize/pallas_call | solution.py:217
  35.8 0.1 collective-permute-start.4
  35.9 18.2 %all_to_all.32.refs_0_.refs_1_ = bf16[8,400,128]{2,1,0:T(8,128)(2,1)} all-to-all(bf16[8,400,128]{2,1,0:T(8,128)(2,1)S(1)} %get-tuple-element.40), channel_id=1, replica_groups=mesh['group'=16,'chip'=8,'core'=2] {'chip'}, dimensions={0} | all-to-all | bytes 1638400 | tf_op jit(solution)/shard_map/all_to_all | solution.py:325
  54.1 4.9 %all-to-all-start.3 = ((bf16[8,656,128]{2,1,0:T(8,128)(2,1)}), bf16[8,656,128]{2,1,0:T(8,128)(2,1)S(1)}, u32[]{:S(2)}, u32[]{:S(2)}) async-start(bf16[8,656,128]{2,1,0:T(8,128)(2,1)} %copy-done.1), calls=%async_computation.3 | async-start | bytes 2686976 | tf_op jit(solution)/shard_map/all_to_all | solution.py:325
  59.1 0.0 collective-permute-start.5
  59.1 1.2 collective-permute-done.5.refs_3_
  60.3 0.0 collective-permute-done.4.refs_1_
  60.3 7.3 %add_and_encode.5 = (bf16[8,1040,128]{2,1,0:T(8,128)(2,1)}, f32[8,128]{1,0:T(8,128)}) custom-call(bf16[8,8,128,128]{3,2,1,0:T(8,128)(2,1)S(1)} %get-tuple-element.47.refs_0_, bf16[8,8,128,128]{3,2,1,0:T(8,128)(2,1)} %collective-permute-done.4.refs_1_, f32[8,8,128]{2,1,0:T(8,128)S(1)} %get-tuple-element.49.refs_2_, ...), custom_call_target="tpu_custom_call" | custom-call | flops 1 | bytes 1 | tf_op jit(solution)/shard_map/add_and_encode/pallas_call | solution.py:237
  67.6 8.7 %all-to-all-done.3.refs_0_.refs_1_ = bf16[8,656,128]{2,1,0:T(8,128)(2,1)S(1)} async-done(((bf16[8,656,128]{2,1,0:T(8,128)(2,1)}), bf16[8,656,128]{2,1,0:T(8,128)(2,1)S(1)}, u32[]{:S(2)}, u32[]{:S(2)}) %all-to-all-start.3) | async-done | bytes 1343520 | tf_op jit(solution)/shard_map/all_to_all | solution.py:325
  76.3 5.1 %all-to-all-start.4 = ((bf16[8,1040,128]{2,1,0:T(8,128)(2,1)}), bf16[8,1040,128]{2,1,0:T(8,128)(2,1)S(1)}, u32[]{:S(2)}, u32[]{:S(2)}) async-start(bf16[8,1040,128]{2,1,0:T(8,128)(2,1)} %get-tuple-element.50), calls=%async_computation.4 | async-start | bytes 4259840 | tf_op jit(solution)/shard_map/all_to_all | solution.py:325
  81.4 0.0 copy-start
  81.4 1.1 copy-done
  82.5 1.4 decode_and_requantize.3
  83.9 0.0 copy-start.4
  83.9 0.6 copy-done.4
  84.5 2.2 %decode_and_requantize.4 = bf16[5,128,128]{2,1,0:T(8,128)(2,1)S(1)} custom-call(bf16[8,656,128]{2,1,0:T(8,128)(2,1)S(1)} %all-to-all-done.3.refs_0_.refs_1_, bf16[8,656,128]{2,1,0:T(8,128)(2,1)S(1)} %all-to-all-done.3.refs_0_.refs_1_), custom_call_target="tpu_custom_call" | custom-call | flops 1 | bytes 1 | tf_op jit(solution)/shard_map/decode_and_requantize/pallas_call | solution.py:261
  86.8 0.0 copy-start.2
  86.8 0.7 copy-done.2
  87.5 0.0 copy-start.5
  87.5 21.2 %all-to-all-done.4.refs_0_.refs_1_ = bf16[8,1040,128]{2,1,0:T(8,128)(2,1)S(1)} async-done(((bf16[8,1040,128]{2,1,0:T(8,128)(2,1)}), bf16[8,1040,128]{2,1,0:T(8,128)(2,1)S(1)}, u32[]{:S(2)}, u32[]{:S(2)}) %all-to-all-start.4) | async-done | bytes 2129952 | tf_op jit(solution)/shard_map/all_to_all | solution.py:325
  108.7 0.0 copy-start.3
  108.7 3.6 %decode_and_requantize.5 = bf16[8,128,128]{2,1,0:T(8,128)(2,1)S(1)} custom-call(bf16[8,1040,128]{2,1,0:T(8,128)(2,1)S(1)} %all-to-all-done.4.refs_0_.refs_1_, bf16[8,1040,128]{2,1,0:T(8,128)(2,1)S(1)} %all-to-all-done.4.refs_0_.refs_1_), custom_call_target="tpu_custom_call" | custom-call | flops 1 | bytes 1 | tf_op jit(solution)/shard_map/decode_and_requantize/pallas_call | solution.py:261
  112.3 0.5 slice.7
  113.5 0.0 copy-done.5
  113.5 0.0 copy-done.3
  113.5 0.9 maximum_add_fusion
  114.4 10.9 %all-to-all-start.5 = ((bf16[16,128,128]{2,1,0:T(8,128)(2,1)}), bf16[16,128,128]{2,1,0:T(8,128)(2,1)S(1)}, u32[]{:S(2)}, u32[]{:S(2)}) async-start(bf16[16,128,128]{2,1,0:T(8,128)(2,1)} %maximum_add_fusion), calls=%async_computation.5 | async-start | bytes 1048576 | tf_op jit(solution)/shard_map/all_to_all | solution.py:329
  125.3 17.3 %all-to-all-done.5 = bf16[16,128,128]{2,1,0:T(8,128)(2,1)S(1)} async-done(((bf16[16,128,128]{2,1,0:T(8,128)(2,1)}), bf16[16,128,128]{2,1,0:T(8,128)(2,1)S(1)}, u32[]{:S(2)}, u32[]{:S(2)}) %all-to-all-start.5) | async-done | bytes 524320 | tf_op jit(solution)/shard_map/all_to_all | solution.py:329
  142.5 0.0 copy-start.9
  142.5 0.8 copy-done.9
  143.4 0.0 copy-start.6
  143.4 0.0 copy-start.7
  143.4 0.0 copy-start.8
  143.4 2.1 %while.10 = (bf16[16,128,128]{2,1,0:T(8,128)(2,1)}, s32[]{:T(128)}, bf16[1,4194304]{1,0:T(2,128)(2,1)}, s32[]{:T(128)}) while((bf16[16,128,128]{2,1,0:T(8,128)(2,1)}, s32[]{:T(128)}, bf16[1,4194304]{1,0:T(2,128)(2,1)}, s32[]{:T(128)}) %tuple.25), condition=%wide.region_1.0_spmd, body=%wide.region_0.0_spmd.sunk | while | flops 34 | bytes 20447380 | solution.py:331
  143.4 1.5 compare_reduce_fusion.1
  145.5 0.0 copy-done.6
  145.5 0.0 copy-done.7
  145.5 0.0 copy-done.8
  145.5 1.8 %adamw_update.1 = (f32[128,128]{1,0:T(8,128)}, f32[128,128]{1,0:T(8,128)}, f32[128,128]{1,0:T(8,128)}) custom-call(bf16[16,128,128]{2,1,0:T(8,128)(2,1)} %get-tuple-element.51.refs_0_, f32[128,128]{1,0:T(8,128)S(1)} %bitcast.11, f32[128,128]{1,0:T(8,128)S(1)} %bitcast.12, f32[128,128]{1,0:T(8,128)S(1)} %bitcast.13), custom_call_target="tpu_custom_call" | custom-call | tf_op jit(solution)/shard_map/adamw_update/pallas_call | solution.py:308
  (1 shorter events, 0.0 us)
Async XLA Ops:
  5.7 2.4 %collective-permute-start = (bf16[8,3,128,128]{3,2,1,0:T(8,128)(2,1)S(1)}, bf16[8,3,128,128]{3,2,1,0:T(8,128)(2,1)S(1)}, u32[]{:S(2)}, u32[]{:S(2)}) collective-permute-start(bf16[8,3,128,128]{3,2,1,0:T(8,128)(2,1)S(1)} %get-tuple-element.38), channel_id=1, source_target_pairs={{0,1},{1,0},{2,3},{3,2},{4,5},{5,4},{6,7},{7,6},{8,9},{9,8},{10,11... | collective-permute-start | bytes 2359304 | tf_op jit(solution)/shard_map/ppermute | solution.py:234
  5.8 2.3 %collective-permute-start.1 = (f32[3,8,128]{2,1,0:T(8,128)S(1)}, f32[3,8,128]{2,1,0:T(8,128)S(1)}, u32[]{:S(2)}, u32[]{:S(2)}) collective-permute-start(f32[3,8,128]{2,1,0:T(8,128)S(1)} %get-tuple-element.39.refs_2_), channel_id=1, source_target_pairs={{0,1},{1,0},{2,3},{3,2},{4,5},{5,4},{6,7},{7,6},{8,9},{9,8},{10,11... | collective-permute-start | bytes 36872 | tf_op jit(solution)/shard_map/ppermute | solution.py:233
  17.1 3.2 %collective-permute-start.2 = (bf16[8,5,128,128]{3,2,1,0:T(8,128)(2,1)S(1)}, bf16[8,5,128,128]{3,2,1,0:T(8,128)(2,1)S(1)}, u32[]{:S(2)}, u32[]{:S(2)}) collective-permute-start(bf16[8,5,128,128]{3,2,1,0:T(8,128)(2,1)S(1)} %get-tuple-element.43), channel_id=1, source_target_pairs={{0,1},{1,0},{2,3},{3,2},{4,5},{5,4},{6,7},{7,6},{8,9},{9,8},{10,11... | collective-permute-start | bytes 3932168 | tf_op jit(solution)/shard_map/ppermute | solution.py:234
  17.3 2.9 %collective-permute-start.3 = (f32[5,8,128]{2,1,0:T(8,128)S(1)}, f32[5,8,128]{2,1,0:T(8,128)S(1)}, u32[]{:S(2)}, u32[]{:S(2)}) collective-permute-start(f32[5,8,128]{2,1,0:T(8,128)S(1)} %get-tuple-element.44.refs_2_), channel_id=1, source_target_pairs={{0,1},{1,0},{2,3},{3,2},{4,5},{5,4},{6,7},{7,6},{8,9},{9,8},{10,11... | collective-permute-start | bytes 61448 | tf_op jit(solution)/shard_map/ppermute | solution.py:233
  22.4 1.1 copy-start.1
  35.8 24.5 %collective-permute-start.4 = (bf16[8,8,128,128]{3,2,1,0:T(8,128)(2,1)}, bf16[8,8,128,128]{3,2,1,0:T(8,128)(2,1)}, u32[]{:S(2)}, u32[]{:S(2)}) collective-permute-start(bf16[8,8,128,128]{3,2,1,0:T(8,128)(2,1)} %get-tuple-element.48), channel_id=1, source_target_pairs={{0,1},{1,0},{2,3},{3,2},{4,5},{5,4},{6,7},{7,6},{8,9},{9,8},{10,11... | collective-permute-start | bytes 6291464 | tf_op jit(solution)/shard_map/ppermute | solution.py:234
  54.1 22.1 %all-to-all-start.3 = ((bf16[8,656,128]{2,1,0:T(8,128)(2,1)}), bf16[8,656,128]{2,1,0:T(8,128)(2,1)S(1)}, u32[]{:S(2)}, u32[]{:S(2)}) async-start(bf16[8,656,128]{2,1,0:T(8,128)(2,1)} %copy-done.1), calls=%async_computation.3 | async-start | bytes 2686976 | tf_op jit(solution)/shard_map/all_to_all | solution.py:325
  59.1 1.2 collective-permute-start.5
  76.3 32.5 %all-to-all-start.4 = ((bf16[8,1040,128]{2,1,0:T(8,128)(2,1)}), bf16[8,1040,128]{2,1,0:T(8,128)(2,1)S(1)}, u32[]{:S(2)}, u32[]{:S(2)}) async-start(bf16[8,1040,128]{2,1,0:T(8,128)(2,1)} %get-tuple-element.50), calls=%async_computation.4 | async-start | bytes 4259840 | tf_op jit(solution)/shard_map/all_to_all | solution.py:325
  81.4 1.1 copy-start
  83.9 0.6 copy-start.4
  86.8 0.7 copy-start.2
  87.5 26.0 %copy-start.5 = (bf16[3,128,128]{2,1,0:T(8,128)(2,1)S(1)}, bf16[3,128,128]{2,1,0:T(8,128)(2,1)}, u32[]{:S(2)}) copy-start(bf16[3,128,128]{2,1,0:T(8,128)(2,1)} %copy-done.4) | copy-start | bytes 294916
  108.7 4.8 %copy-start.3 = (bf16[5,128,128]{2,1,0:T(8,128)(2,1)S(1)}, bf16[5,128,128]{2,1,0:T(8,128)(2,1)}, u32[]{:S(2)}) copy-start(bf16[5,128,128]{2,1,0:T(8,128)(2,1)} %copy-done.2) | copy-start | bytes 491524
  114.4 28.2 %all-to-all-start.5 = ((bf16[16,128,128]{2,1,0:T(8,128)(2,1)}), bf16[16,128,128]{2,1,0:T(8,128)(2,1)S(1)}, u32[]{:S(2)}, u32[]{:S(2)}) async-start(bf16[16,128,128]{2,1,0:T(8,128)(2,1)} %maximum_add_fusion), calls=%async_computation.5 | async-start | bytes 1048576 | tf_op jit(solution)/shard_map/all_to_all | solution.py:329
  142.5 0.8 copy-start.9
  143.4 2.1 %copy-start.6 = (f32[16384]{0:T(1024)S(1)}, f32[16384]{0:T(1024)}, u32[]{:S(2)}) copy-start(f32[16384]{0:T(1024)} %param.7) | copy-start | bytes 196612
  143.4 2.1 %copy-start.7 = (f32[16384]{0:T(1024)S(1)}, f32[16384]{0:T(1024)}, u32[]{:S(2)}) copy-start(f32[16384]{0:T(1024)} %param.8) | copy-start | bytes 196612
  143.4 2.1 %copy-start.8 = (f32[16384]{0:T(1024)S(1)}, f32[16384]{0:T(1024)}, u32[]{:S(2)}) copy-start(f32[16384]{0:T(1024)} %param.9) | copy-start | bytes 196612

commit v3 on v2

--- a/solution.py
+++ b/solution.py
@@ -19,7 +19,10 @@
 OFFSET = 113.0
 
 PARTS = (3, 5, 8)
+PIECES = 4
 PARAMS = pltpu.CompilerParams(vmem_limit_bytes=48 << 20)
+PARAMS_Q = pltpu.CompilerParams(vmem_limit_bytes=48 << 20)
+PARAMS_C = pltpu.CompilerParams(vmem_limit_bytes=48 << 20)
 
 
 def scale_of(peak):
@@ -44,8 +47,9 @@
     return [jnp.floor(part * inverse + 0.5) * scale for part in parts]
 
 
-def pair_kernel(chips, groups, core_ref, x_ref, after_ref, own_ref, send_ref, scale_ref, scratch):
+def pair_kernel(chips, groups, core_ref, x_ref, after_ref, own_ref, *refs):
     del after_ref
+    *send_refs, scale_ref, scratch = refs
     core = core_ref[0]
     lane = lax.broadcasted_iota(jnp.int32, (8, LANES), 1)
     where = [(d, half, k) for d in range(chips) for half in range(2) for k in range(groups)]
@@ -74,15 +78,15 @@
         s_col = jnp.broadcast_to(scale[:, at : at + 1], (8, LANES))
         i_col = jnp.broadcast_to(inverse[:, at : at + 1], (8, LANES))
         done = [jnp.floor(part * i_col + 0.5) * s_col for part in parts_of(d, half, k)]
-        o_ref = send_ref if half else own_ref
+        o_ref, slot = (send_refs[d % PIECES], d // PIECES) if half else (own_ref, d)
         at = slice(k * GROUP_ROWS, (k + 1) * GROUP_ROWS)
-        o_ref[d, 0, at, :] = jnp.concatenate(done, axis=0).astype(jnp.bfloat16)
+        o_ref[slot, 0, at, :] = jnp.concatenate(done, axis=0).astype(jnp.bfloat16)
 
 
 def encode_kernel(
-    chips, groups, count, own_ref, peer_ref, mine_ref, theirs_ref, before_ref, m_ref, flag_ref,
-    buffer, aux, packed, bad, sems, aux_sem,
+    chips, groups, count, own_ref, mine_ref, theirs_ref, before_ref, *refs
 ):
+    *peer_refs, m_ref, flag_ref, buffer, aux, packed, bad, sems, aux_sem = refs
     g = pl.program_id(0)
     slot = lax.rem(g, 2)
     rows = groups * GROUP_ROWS
@@ -114,7 +118,8 @@
             tile = jnp.where(lane == g * groups + k, scale[:, column], tile)
             w_col = jnp.broadcast_to(weight[:, column], (8, LANES))
             at = slice(k * GROUP_ROWS, (k + 1) * GROUP_ROWS)
-            total = own_ref[d, 0, at, :].astype(jnp.float32) + peer_ref[d, 0, at, :].astype(jnp.float32)
+            peer = peer_refs[d % PIECES][d // PIECES, 0, at, :].astype(jnp.float32)
+            total = own_ref[d, 0, at, :].astype(jnp.float32) + peer
             out = []
             for s in range(ROWS):
                 part = total[8 * s : 8 * s + 8]
@@ -207,38 +212,47 @@
 COST = pl.CostEstimate(flops=1, bytes_accessed=1, transcendentals=0)
 
 
-def pair_sums(grads, start, count, replicas, chips, shard, before):
+def quantized(grads, after, start, count, chips, shard):
     rows, groups = shard // LANES, shard // GROUP
-    nodes = 2 * chips
     core = lax.axis_index("core").astype(jnp.int32).reshape(1)
-    half = jax.ShapeDtypeStruct((chips, count, rows, LANES), jnp.bfloat16)
-    half_spec = pl.BlockSpec((chips, 1, rows, LANES), lambda g: (0, g, 0, 0))
-    tile_spec = pl.BlockSpec((1, 8, LANES), lambda g: (g, 0, 0))
-    own, send, scales = pl.pallas_call(
+
+    def block(size):
+        shape = jax.ShapeDtypeStruct((size, count, rows, LANES), jnp.bfloat16)
+        return shape, pl.BlockSpec((size, 1, rows, LANES), lambda g: (0, g, 0, 0))
+
+    blocks = [block(chips)] + [block(chips // PIECES)] * PIECES
+    tiles = jax.ShapeDtypeStruct((count, 8, LANES), jnp.float32)
+    own, *send, scales = pl.pallas_call(
         lambda *refs: pair_kernel(chips, groups, *refs),
         name="quantize",
         grid=(count,),
         in_specs=[
             pl.BlockSpec(memory_space=pltpu.SMEM),
-            pl.BlockSpec((1, nodes * shard), lambda g: (0, g + start)),
+            pl.BlockSpec((1, 2 * chips * shard), lambda g: (0, g + start)),
             pl.BlockSpec(memory_space=pl.ANY),
         ],
-        out_specs=[half_spec, half_spec, tile_spec],
-        out_shape=[half, half, jax.ShapeDtypeStruct((count, 8, LANES), jnp.float32)],
+        out_specs=[b for _, b in blocks] + [pl.BlockSpec((1, 8, LANES), lambda g: (g, 0, 0))],
+        out_shape=[a for a, _ in blocks] + [tiles],
         scratch_shapes=[pltpu.VMEM((chips, 2 * groups, GROUP_ROWS, LANES), jnp.float32)],
-        compiler_params=PARAMS,
+        compiler_params=PARAMS_Q,
         cost_estimate=COST,
-    )(core, grads, before)
-    swap = [(0, 1), (1, 0)]
-    peer_scales = lax.ppermute(scales, "core", swap)
-    peer = lax.ppermute(send, "core", swap)
+    )(core, grads, after)
+    peer, peer_scales = jax.tree.map(lambda a: lax.ppermute(a, "core", [(0, 1), (1, 0)]), (send, scales))
+    return own, peer, scales, peer_scales
+
+
+def pair_sums(own, peer, scales, peer_scales, before, after=()):
+    chips, count, rows = own.shape[:3]
+    half_spec = pl.BlockSpec((chips, 1, rows, LANES), lambda g: (0, g, 0, 0))
+    piece_spec = pl.BlockSpec((chips // PIECES, 1, rows, LANES), lambda g: (0, g, 0, 0))
+    tile_spec = pl.BlockSpec((1, 8, LANES), lambda g: (g, 0, 0))
     flag = jax.ShapeDtypeStruct((8, LANES), jnp.float32)
     whole = pl.BlockSpec((8, LANES), lambda g: (0, 0))
     return pl.pallas_call(
-        lambda *refs: encode_kernel(chips, groups, count, *refs),
+        lambda *refs: encode_kernel(chips, rows // GROUP_ROWS, count, *refs),
         name="add_and_encode",
         grid=(count,),
-        in_specs=[half_spec, half_spec, tile_spec, tile_spec, whole],
+        in_specs=[half_spec, tile_spec, tile_spec, whole] + [piece_spec] * PIECES,
         out_specs=[pl.BlockSpec(memory_space=pl.ANY), whole],
         out_shape=[
             jax.ShapeDtypeStruct((chips, count * rows + AUX_ROWS, LANES), jnp.bfloat16), flag,
@@ -251,9 +265,9 @@
             pltpu.SemaphoreType.DMA((2,)),
             pltpu.SemaphoreType.DMA,
         ],
-        compiler_params=PARAMS,
+        compiler_params=PARAMS_C,
         cost_estimate=COST,
-    )(own, peer, scales, peer_scales, before)
+    )(own, scales, peer_scales, before, *peer)
 
 
 def node_sums(received, count, chips, shard):
@@ -321,7 +335,7 @@
     flag = jnp.zeros((8, LANES), jnp.float32)
     partials, start = [], 0
     for count in PARTS:
-        message, flag = pair_sums(grads, start, count, replicas, chips, shard, flag)
+        message, flag = pair_sums(*quantized(grads, flag, start, count, chips, shard), flag)
         received = lax.all_to_all(message, "chip", split_axis=0, concat_axis=0, tiled=True)
         partials.append(node_sums(received, count, chips, shard))
         start += count

time: 149 us -> 133 us (0.89)
  blocking collectives: 18.2 us -> 0 us
  starting transfers between devices: 22.3 us -> 31.8 us
  waiting for transfers between devices: 52.8 us -> 47.5 us
  Pallas kernels: 44.7 us -> 42.9 us
    all_to_all x1 -> x0, blocking collectives: 18.2 us -> none  [body(): lax.all_to_all(message, 'chip', split_axis=0, concat_axis=0, tiled=True)]
    all_to_all x2 -> x3, starting transfers between devices: 10.1 us -> 17.3 us  [body(): lax.all_to_all(message, 'chip', split_axis=0, concat_axis=0, tiled=True)]
    all_to_all x2 -> x3, waiting for transfers between devices: 29.9 us -> 23.3 us  [body(): lax.all_to_all(message, 'chip', split_axis=0, concat_axis=0, tiled=True)]
    ppermute x6 -> x15, starting transfers between devices: 1.33 us -> 3.6 us  [quantized(): lax.ppermute(a, 'core', [(0, 1), (1, 0)])]
    pallas_call x6, Pallas kernels: 35.7 us -> 33.9 us  [the longest x3 24.2 us: quantized(): pl.pallas_call(lambda *refs: pair_kernel(chips, groups, *refs), name='qua...]
    ppermute x6 -> x15, waiting for transfers between devices: 5.56 us -> 6.24 us  [quantized(): lax.ppermute(a, 'core', [(0, 1), (1, 0)])]
    unnamed x20 -> x22, local copies, waits for them, and re-layouts: 4.39 us -> 4.3 us
  transfers between devices with their start and end apart: 9 -> 19, of which waited for: 6 -> 5; matrix products, arithmetic and copies ran while one was open for 0% -> 0% of each run, Pallas kernels for 7% -> 23%
where the time goes in v3:
time: 133 us; the launch traced here: 131 us
  waiting for transfers between devices  47.5 us (36%)
  Pallas kernels  42.9 us (32%)
  starting transfers between devices  31.8 us (24%)
  local copies, waits for them, and re-layouts  4.81 us (4%)
  other arithmetic  2.29 us (2%)
  between operations  1.55 us (1%)
    pallas_call x3, Pallas kernels, quantized(): pl.pallas_call(lambda *refs: pair_kernel(chips, groups, *refs), name='qua...  24.2 us
    all_to_all x3, waiting for transfers between devices, body(): lax.all_to_all(message, 'chip', split_axis=0, concat_axis=0, tiled=True)  23.3 us
    all_to_all x1, waiting for transfers between devices, body(): lax.all_to_all(partial, 'group', split_axis=0, concat_axis=0, tiled=True)  18 us
    all_to_all x3, starting transfers between devices, body(): lax.all_to_all(message, 'chip', split_axis=0, concat_axis=0, tiled=True)  17.3 us
    all_to_all x1, starting transfers between devices, body(): lax.all_to_all(partial, 'group', split_axis=0, concat_axis=0, tiled=True)  10.9 us
    pallas_call x3, Pallas kernels, pair_sums(): pl.pallas_call(lambda *refs: encode_kernel(chips, rows // GROUP_ROWS, cou...  9.78 us
    pallas_call x3, Pallas kernels, node_sums(): pl.pallas_call(lambda *refs: decode_kernel(chips, groups, *refs), name='d...  7.17 us
    ppermute x15, waiting for transfers between devices, quantized(): lax.ppermute(a, 'core', [(0, 1), (1, 0)])  6.24 us
  transfers between devices with their start and end apart: 19, of which 5 were waited for; matrix products, arithmetic and copies ran while one was open for 0% of the time, Pallas kernels for 23%

profile of v3, /device:TPU:2, one launch (start us, length us, event | category | flops | bytes accessed | tf_op | source)
XLA Modules:
  0.0 131.4 jit_solution(16610305084979933440)
XLA Ops:
  0.6 5.1 %quantize.3 = (bf16[8,3,128,128]{3,2,1,0:T(8,128)(2,1)S(1)}, bf16[2,3,128,128]{3,2,1,0:T(8,128)(2,1)S(1)}, bf16[2,3,128,128]{3,2,1,0:T(8,128)(2,1)S(1)}, bf16[2,...) custom-call(s32[1]{0:T(128)} %bitcast.1.refs_0_, ...), custom_call_target="tpu_custom_call" | custom-call | flops 1 | bytes 1 | tf_op jit(solution)/shard_map/quantize/pallas_call | solution.py:225
  5.7 0.1 collective-permute-start.1
  5.8 0.5 collective-permute-start.2
  6.3 0.1 collective-permute-start.3
  6.4 0.4 collective-permute-start.4
  6.8 0.1 collective-permute-start
  6.9 1.2 collective-permute-done.refs_2_
  8.1 0.0 collective-permute-done.1.refs_4_
  8.1 0.0 collective-permute-done.2.refs_5_
  8.1 0.0 collective-permute-done.3.refs_6_
  8.1 0.0 collective-permute-done.4.refs_7_
  8.1 2.2 %add_and_encode.3 = (bf16[8,400,128]{2,1,0:T(8,128)(2,1)}, f32[8,128]{1,0:T(8,128)S(1)}) custom-call(bf16[8,3,128,128]{3,2,1,0:T(8,128)(2,1)S(1)} %get-tuple-element.46.refs_0_, f32[3,8,128]{2,1,0:T(8,128)S(1)} %get-tuple-element.47.refs_1_, f32[3,8,128]{2,1,0:T(8,128)S(1)} %collective-permute-done.refs_2_, f32[8,128]{1,0:T(8,128)S(1)} %broadcast_in_dim.3.refs_2_.refs_3_, ...), custom_call_target="tpu_custom_call" | custom-call | flops 1 | bytes 1 | tf_op jit(solution)/shard_map/add_and_encode/pallas_call | solution.py:251
  10.4 5.9 %all-to-all-start.2 = ((bf16[8,400,128]{2,1,0:T(8,128)(2,1)}), bf16[8,400,128]{2,1,0:T(8,128)(2,1)S(1)}, u32[]{:S(2)}, u32[]{:S(2)}) async-start(bf16[8,400,128]{2,1,0:T(8,128)(2,1)} %get-tuple-element.52), calls=%async_computation.2 | async-start | bytes 1638400 | tf_op jit(solution)/shard_map/all_to_all | solution.py:339
  16.2 7.6 %quantize.4 = (bf16[8,5,128,128]{3,2,1,0:T(8,128)(2,1)S(1)}, bf16[2,5,128,128]{3,2,1,0:T(8,128)(2,1)S(1)}, bf16[2,5,128,128]{3,2,1,0:T(8,128)(2,1)S(1)}, bf16[2,...) custom-call(s32[1]{0:T(128)} %bitcast.1.refs_0_, ...), custom_call_target="tpu_custom_call" | custom-call | flops 1 | bytes 1 | tf_op jit(solution)/shard_map/quantize/pallas_call | solution.py:225
  23.9 0.1 collective-permute-start.6
  24.0 0.5 collective-permute-start.7
  24.5 0.1 collective-permute-start.8
  24.6 0.4 collective-permute-start.9
  25.0 0.1 collective-permute-start.5
  25.1 1.9 %collective-permute-done.5.refs_2_ = f32[5,8,128]{2,1,0:T(8,128)S(1)} collective-permute-done((f32[5,8,128]{2,1,0:T(8,128)S(1)}, f32[5,8,128]{2,1,0:T(8,128)S(1)}, u32[]{:S(2)}, u32[]{:S(2)}) %collective-permute-start.5) | collective-permute-done | bytes 20512 | tf_op jit(solution)/shard_map/ppermute | solution.py:240
  27.0 0.0 collective-permute-done.6.refs_4_
  27.0 0.0 collective-permute-done.7.refs_5_
  27.0 0.0 collective-permute-done.8.refs_6_
  27.0 0.0 collective-permute-done.9.refs_7_
  27.1 2.2 %add_and_encode.4 = (bf16[8,656,128]{2,1,0:T(8,128)(2,1)S(1)}, f32[8,128]{1,0:T(8,128)S(1)}) custom-call(bf16[8,5,128,128]{3,2,1,0:T(8,128)(2,1)S(1)} %get-tuple-element.54.refs_0_, f32[5,8,128]{2,1,0:T(8,128)S(1)} %get-tuple-element.55.refs_1_, f32[5,8,128]{2,1,0:T(8,128)S(1)} %collective-permute-done.5.refs_2_, ...), custom_call_target="tpu_custom_call" | custom-call | flops 1 | bytes 1 | tf_op jit(solution)/shard_map/add_and_encode/pallas_call | solution.py:251
  29.3 0.0 copy-start.2
  29.3 1.1 copy-done.2
  30.3 0.0 all-to-all-done.2.refs_0_.refs_1_
  30.3 5.7 %all-to-all-start.3 = ((bf16[8,656,128]{2,1,0:T(8,128)(2,1)}), bf16[8,656,128]{2,1,0:T(8,128)(2,1)S(1)}, u32[]{:S(2)}, u32[]{:S(2)}) async-start(bf16[8,656,128]{2,1,0:T(8,128)(2,1)} %copy-done.2), calls=%async_computation.3 | async-start | bytes 2686976 | tf_op jit(solution)/shard_map/all_to_all | solution.py:339
  36.0 11.5 %quantize.5 = (bf16[8,8,128,128]{3,2,1,0:T(8,128)(2,1)S(1)}, bf16[2,8,128,128]{3,2,1,0:T(8,128)(2,1)S(1)}, bf16[2,8,128,128]{3,2,1,0:T(8,128)(2,1)S(1)}, bf16[2,...) custom-call(s32[1]{0:T(128)} %bitcast.1.refs_0_, ...), custom_call_target="tpu_custom_call" | custom-call | flops 1 | bytes 1 | tf_op jit(solution)/shard_map/quantize/pallas_call | solution.py:225
  47.5 0.0 copy-done
  47.5 0.1 collective-permute-start.11
  47.6 0.5 collective-permute-start.12
  48.1 0.1 collective-permute-start.13
  48.2 0.4 collective-permute-start.14
  48.6 0.1 collective-permute-start.10
  48.7 3.1 %collective-permute-done.10.refs_2_ = f32[8,8,128]{2,1,0:T(8,128)S(1)} collective-permute-done((f32[8,8,128]{2,1,0:T(8,128)S(1)}, f32[8,8,128]{2,1,0:T(8,128)S(1)}, u32[]{:S(2)}, u32[]{:S(2)}) %collective-permute-start.10) | collective-permute-done | bytes 32800 | tf_op jit(solution)/shard_map/ppermute | solution.py:240
  51.8 0.0 collective-permute-done.11.refs_4_
  51.8 0.0 collective-permute-done.12.refs_5_
  51.8 0.0 collective-permute-done.13.refs_6_
  51.8 0.0 collective-permute-done.14.refs_7_
  51.8 5.3 %add_and_encode.5 = (bf16[8,1040,128]{2,1,0:T(8,128)(2,1)}, f32[8,128]{1,0:T(8,128)}) custom-call(bf16[8,8,128,128]{3,2,1,0:T(8,128)(2,1)S(1)} %get-tuple-element.62.refs_0_, f32[8,8,128]{2,1,0:T(8,128)S(1)} %get-tuple-element.63.refs_1_, f32[8,8,128]{2,1,0:T(8,128)S(1)} %collective-permute-done.10.refs_2_, f32[8,128]{1,0:T(8,128)S(1)} %get-tuple-element.61.refs_2_.refs_3_, ...), custom_call_target="tpu_custom_call" | custom-call | flops 1 | bytes 1 | tf_op jit(solution)/shard_map/add_and_encode/pallas_call | solution.py:251
  57.2 0.0 all-to-all-done.3.refs_0_.refs_1_
  57.2 5.7 %all-to-all-start.4 = ((bf16[8,1040,128]{2,1,0:T(8,128)(2,1)}), bf16[8,1040,128]{2,1,0:T(8,128)(2,1)S(1)}, u32[]{:S(2)}, u32[]{:S(2)}) async-start(bf16[8,1040,128]{2,1,0:T(8,128)(2,1)} %get-tuple-element.68), calls=%async_computation.4 | async-start | bytes 4259840 | tf_op jit(solution)/shard_map/all_to_all | solution.py:339
  62.9 1.1 copy-done.1
  64.1 1.4 %decode_and_requantize.3 = bf16[3,128,128]{2,1,0:T(8,128)(2,1)S(1)} custom-call(bf16[8,400,128]{2,1,0:T(8,128)(2,1)S(1)} %copy-done.1, bf16[8,400,128]{2,1,0:T(8,128)(2,1)S(1)} %copy-done.1), custom_call_target="tpu_custom_call" | custom-call | flops 1 | bytes 1 | tf_op jit(solution)/shard_map/decode_and_requantize/pallas_call | solution.py:275
  65.4 0.0 copy-start.5
  65.4 0.6 copy-done.5
  66.1 2.2 %decode_and_requantize.4 = bf16[5,128,128]{2,1,0:T(8,128)(2,1)S(1)} custom-call(bf16[8,656,128]{2,1,0:T(8,128)(2,1)S(1)} %all-to-all-done.3.refs_0_.refs_1_, bf16[8,656,128]{2,1,0:T(8,128)(2,1)S(1)} %all-to-all-done.3.refs_0_.refs_1_), custom_call_target="tpu_custom_call" | custom-call | flops 1 | bytes 1 | tf_op jit(solution)/shard_map/decode_and_requantize/pallas_call | solution.py:275
  68.3 0.0 copy-start.3
  68.3 0.7 copy-done.3
  69.0 23.3 %all-to-all-done.4.refs_0_.refs_1_ = bf16[8,1040,128]{2,1,0:T(8,128)(2,1)S(1)} async-done(((bf16[8,1040,128]{2,1,0:T(8,128)(2,1)}), bf16[8,1040,128]{2,1,0:T(8,128)(2,1)S(1)}, u32[]{:S(2)}, u32[]{:S(2)}) %all-to-all-start.4) | async-done | bytes 2129952 | tf_op jit(solution)/shard_map/all_to_all | solution.py:339
  92.2 3.6 %decode_and_requantize.5 = bf16[8,128,128]{2,1,0:T(8,128)(2,1)S(1)} custom-call(bf16[8,1040,128]{2,1,0:T(8,128)(2,1)S(1)} %all-to-all-done.4.refs_0_.refs_1_, bf16[8,1040,128]{2,1,0:T(8,128)(2,1)S(1)} %all-to-all-done.4.refs_0_.refs_1_), custom_call_target="tpu_custom_call" | custom-call | flops 1 | bytes 1 | tf_op jit(solution)/shard_map/decode_and_requantize/pallas_call | solution.py:275
  95.8 0.5 slice.7
  97.0 0.0 copy-done.6
  97.0 0.0 copy-done.4
  97.0 0.8 maximum_add_fusion
  97.9 10.9 %all-to-all-start.5 = ((bf16[16,128,128]{2,1,0:T(8,128)(2,1)}), bf16[16,128,128]{2,1,0:T(8,128)(2,1)S(1)}, u32[]{:S(2)}, u32[]{:S(2)}) async-start(bf16[16,128,128]{2,1,0:T(8,128)(2,1)} %maximum_add_fusion), calls=%async_computation.5 | async-start | bytes 1048576 | tf_op jit(solution)/shard_map/all_to_all | solution.py:343
  108.8 18.0 %all-to-all-done.5 = bf16[16,128,128]{2,1,0:T(8,128)(2,1)S(1)} async-done(((bf16[16,128,128]{2,1,0:T(8,128)(2,1)}), bf16[16,128,128]{2,1,0:T(8,128)(2,1)S(1)}, u32[]{:S(2)}, u32[]{:S(2)}) %all-to-all-start.5) | async-done | bytes 524320 | tf_op jit(solution)/shard_map/all_to_all | solution.py:343
  126.7 0.8 copy-done.10
  127.5 2.1 %while.10 = (bf16[16,128,128]{2,1,0:T(8,128)(2,1)}, s32[]{:T(128)}, bf16[1,4194304]{1,0:T(2,128)(2,1)}, s32[]{:T(128)}) while((bf16[16,128,128]{2,1,0:T(8,128)(2,1)}, s32[]{:T(128)}, bf16[1,4194304]{1,0:T(2,128)(2,1)}, s32[]{:T(128)}) %tuple.25), condition=%wide.region_1.0_spmd, body=%wide.region_0.0_spmd.sunk | while | flops 34 | bytes 20447380 | solution.py:345
  127.5 1.5 %compare_reduce_fusion.1 = pred[]{:T(512)} fusion(bf16[16,128,128]{2,1,0:T(8,128)(2,1)} %get-tuple-element.83), kind=kLoop, calls=%fused_computation.clone | loop fusion | flops 31 | bytes 33 | tf_op jit(solution)/shard_map/while/cond/reduce_or | solution.py:346
  129.6 0.0 copy-done.7
  129.6 1.8 %adamw_update.1 = (f32[128,128]{1,0:T(8,128)}, f32[128,128]{1,0:T(8,128)}, f32[128,128]{1,0:T(8,128)}) custom-call(bf16[16,128,128]{2,1,0:T(8,128)(2,1)} %get-tuple-element.69.refs_0_, f32[128,128]{1,0:T(8,128)S(1)} %bitcast.11, f32[128,128]{1,0:T(8,128)S(1)} %bitcast.12, f32[128,128]{1,0:T(8,128)S(1)} %bitcast.13), custom_call_target="tpu_custom_call" | custom-call | tf_op jit(solution)/shard_map/adamw_update/pallas_call | solution.py:322
  (11 shorter events, 0.0 us)
Async XLA Ops:
  5.7 2.4 %collective-permute-start.1 = (bf16[2,3,128,128]{3,2,1,0:T(8,128)(2,1)S(1)}, bf16[2,3,128,128]{3,2,1,0:T(8,128)(2,1)S(1)}, u32[]{:S(2)}, u32[]{:S(2)}) collective-permute-start(bf16[2,3,128,128]{3,2,1,0:T(8,128)(2,1)S(1)} %get-tuple-element.48), channel_id=1, source_target_pairs={{0,1},{1,0},{2,3},{3,2},{4,5},{5,4},{6,7},{7,6},{8,9},{9,8},{10,11... | collective-permute-start | bytes 589832 | tf_op jit(solution)/shard_map/ppermute | solution.py:240
  5.8 2.3 %collective-permute-start.2 = (bf16[2,3,128,128]{3,2,1,0:T(8,128)(2,1)S(1)}, bf16[2,3,128,128]{3,2,1,0:T(8,128)(2,1)S(1)}, u32[]{:S(2)}, u32[]{:S(2)}) collective-permute-start(bf16[2,3,128,128]{3,2,1,0:T(8,128)(2,1)S(1)} %get-tuple-element.49), channel_id=1, source_target_pairs={{0,1},{1,0},{2,3},{3,2},{4,5},{5,4},{6,7},{7,6},{8,9},{9,8},{10,11... | collective-permute-start | bytes 589832 | tf_op jit(solution)/shard_map/ppermute | solution.py:240
  6.3 1.8 %collective-permute-start.3 = (bf16[2,3,128,128]{3,2,1,0:T(8,128)(2,1)S(1)}, bf16[2,3,128,128]{3,2,1,0:T(8,128)(2,1)S(1)}, u32[]{:S(2)}, u32[]{:S(2)}) collective-permute-start(bf16[2,3,128,128]{3,2,1,0:T(8,128)(2,1)S(1)} %get-tuple-element.50), channel_id=1, source_target_pairs={{0,1},{1,0},{2,3},{3,2},{4,5},{5,4},{6,7},{7,6},{8,9},{9,8},{10,11... | collective-permute-start | bytes 589832 | tf_op jit(solution)/shard_map/ppermute | solution.py:240
  6.4 1.7 %collective-permute-start.4 = (bf16[2,3,128,128]{3,2,1,0:T(8,128)(2,1)S(1)}, bf16[2,3,128,128]{3,2,1,0:T(8,128)(2,1)S(1)}, u32[]{:S(2)}, u32[]{:S(2)}) collective-permute-start(bf16[2,3,128,128]{3,2,1,0:T(8,128)(2,1)S(1)} %get-tuple-element.51), channel_id=1, source_target_pairs={{0,1},{1,0},{2,3},{3,2},{4,5},{5,4},{6,7},{7,6},{8,9},{9,8},{10,11... | collective-permute-start | bytes 589832 | tf_op jit(solution)/shard_map/ppermute | solution.py:240
  6.8 1.3 collective-permute-start
  10.4 19.9 %all-to-all-start.2 = ((bf16[8,400,128]{2,1,0:T(8,128)(2,1)}), bf16[8,400,128]{2,1,0:T(8,128)(2,1)S(1)}, u32[]{:S(2)}, u32[]{:S(2)}) async-start(bf16[8,400,128]{2,1,0:T(8,128)(2,1)} %get-tuple-element.52), calls=%async_computation.2 | async-start | bytes 1638400 | tf_op jit(solution)/shard_map/all_to_all | solution.py:339
  23.9 3.2 %collective-permute-start.6 = (bf16[2,5,128,128]{3,2,1,0:T(8,128)(2,1)S(1)}, bf16[2,5,128,128]{3,2,1,0:T(8,128)(2,1)S(1)}, u32[]{:S(2)}, u32[]{:S(2)}) collective-permute-start(bf16[2,5,128,128]{3,2,1,0:T(8,128)(2,1)S(1)} %get-tuple-element.56), channel_id=1, source_target_pairs={{0,1},{1,0},{2,3},{3,2},{4,5},{5,4},{6,7},{7,6},{8,9},{9,8},{10,11... | collective-permute-start | bytes 983048 | tf_op jit(solution)/shard_map/ppermute | solution.py:240
  24.0 3.1 %collective-permute-start.7 = (bf16[2,5,128,128]{3,2,1,0:T(8,128)(2,1)S(1)}, bf16[2,5,128,128]{3,2,1,0:T(8,128)(2,1)S(1)}, u32[]{:S(2)}, u32[]{:S(2)}) collective-permute-start(bf16[2,5,128,128]{3,2,1,0:T(8,128)(2,1)S(1)} %get-tuple-element.57), channel_id=1, source_target_pairs={{0,1},{1,0},{2,3},{3,2},{4,5},{5,4},{6,7},{7,6},{8,9},{9,8},{10,11... | collective-permute-start | bytes 983048 | tf_op jit(solution)/shard_map/ppermute | solution.py:240
  24.5 2.6 %collective-permute-start.8 = (bf16[2,5,128,128]{3,2,1,0:T(8,128)(2,1)S(1)}, bf16[2,5,128,128]{3,2,1,0:T(8,128)(2,1)S(1)}, u32[]{:S(2)}, u32[]{:S(2)}) collective-permute-start(bf16[2,5,128,128]{3,2,1,0:T(8,128)(2,1)S(1)} %get-tuple-element.58), channel_id=1, source_target_pairs={{0,1},{1,0},{2,3},{3,2},{4,5},{5,4},{6,7},{7,6},{8,9},{9,8},{10,11... | collective-permute-start | bytes 983048 | tf_op jit(solution)/shard_map/ppermute | solution.py:240
  24.6 2.5 %collective-permute-start.9 = (bf16[2,5,128,128]{3,2,1,0:T(8,128)(2,1)S(1)}, bf16[2,5,128,128]{3,2,1,0:T(8,128)(2,1)S(1)}, u32[]{:S(2)}, u32[]{:S(2)}) collective-permute-start(bf16[2,5,128,128]{3,2,1,0:T(8,128)(2,1)S(1)} %get-tuple-element.59), channel_id=1, source_target_pairs={{0,1},{1,0},{2,3},{3,2},{4,5},{5,4},{6,7},{7,6},{8,9},{9,8},{10,11... | collective-permute-start | bytes 983048 | tf_op jit(solution)/shard_map/ppermute | solution.py:240
  25.0 2.0 %collective-permute-start.5 = (f32[5,8,128]{2,1,0:T(8,128)S(1)}, f32[5,8,128]{2,1,0:T(8,128)S(1)}, u32[]{:S(2)}, u32[]{:S(2)}) collective-permute-start(f32[5,8,128]{2,1,0:T(8,128)S(1)} %get-tuple-element.55.refs_1_), channel_id=1, source_target_pairs={{0,1},{1,0},{2,3},{3,2},{4,5},{5,4},{6,7},{7,6},{8,9},{9,8},{10,11... | collective-permute-start | bytes 61448 | tf_op jit(solution)/shard_map/ppermute | solution.py:240
  29.3 1.1 copy-start.2
  30.3 17.2 %copy-start = (bf16[8,400,128]{2,1,0:T(8,128)(2,1)}, bf16[8,400,128]{2,1,0:T(8,128)(2,1)S(1)}, u32[]{:S(2)}) copy-start(bf16[8,400,128]{2,1,0:T(8,128)(2,1)S(1)} %all-to-all-done.2.refs_0_.refs_1_) | copy-start | bytes 2457604
  30.3 26.8 %all-to-all-start.3 = ((bf16[8,656,128]{2,1,0:T(8,128)(2,1)}), bf16[8,656,128]{2,1,0:T(8,128)(2,1)S(1)}, u32[]{:S(2)}, u32[]{:S(2)}) async-start(bf16[8,656,128]{2,1,0:T(8,128)(2,1)} %copy-done.2), calls=%async_computation.3 | async-start | bytes 2686976 | tf_op jit(solution)/shard_map/all_to_all | solution.py:339
  47.5 4.3 %collective-permute-start.11 = (bf16[2,8,128,128]{3,2,1,0:T(8,128)(2,1)S(1)}, bf16[2,8,128,128]{3,2,1,0:T(8,128)(2,1)S(1)}, u32[]{:S(2)}, u32[]{:S(2)}) collective-permute-start(bf16[2,8,128,128]{3,2,1,0:T(8,128)(2,1)S(1)} %get-tuple-element.64), channel_id=1, source_target_pairs={{0,1},{1,0},{2,3},{3,2},{4,5},{5,4},{6,7},{7,6},{8,9},{9,8},{10,11... | collective-permute-start | bytes 1572872 | tf_op jit(solution)/shard_map/ppermute | solution.py:240
  47.6 4.2 %collective-permute-start.12 = (bf16[2,8,128,128]{3,2,1,0:T(8,128)(2,1)S(1)}, bf16[2,8,128,128]{3,2,1,0:T(8,128)(2,1)S(1)}, u32[]{:S(2)}, u32[]{:S(2)}) collective-permute-start(bf16[2,8,128,128]{3,2,1,0:T(8,128)(2,1)S(1)} %get-tuple-element.65), channel_id=1, source_target_pairs={{0,1},{1,0},{2,3},{3,2},{4,5},{5,4},{6,7},{7,6},{8,9},{9,8},{10,11... | collective-permute-start | bytes 1572872 | tf_op jit(solution)/shard_map/ppermute | solution.py:240
  48.1 3.7 %collective-permute-start.13 = (bf16[2,8,128,128]{3,2,1,0:T(8,128)(2,1)S(1)}, bf16[2,8,128,128]{3,2,1,0:T(8,128)(2,1)S(1)}, u32[]{:S(2)}, u32[]{:S(2)}) collective-permute-start(bf16[2,8,128,128]{3,2,1,0:T(8,128)(2,1)S(1)} %get-tuple-element.66), channel_id=1, source_target_pairs={{0,1},{1,0},{2,3},{3,2},{4,5},{5,4},{6,7},{7,6},{8,9},{9,8},{10,11... | collective-permute-start | bytes 1572872 | tf_op jit(solution)/shard_map/ppermute | solution.py:240
  48.2 3.6 %collective-permute-start.14 = (bf16[2,8,128,128]{3,2,1,0:T(8,128)(2,1)S(1)}, bf16[2,8,128,128]{3,2,1,0:T(8,128)(2,1)S(1)}, u32[]{:S(2)}, u32[]{:S(2)}) collective-permute-start(bf16[2,8,128,128]{3,2,1,0:T(8,128)(2,1)S(1)} %get-tuple-element.67), channel_id=1, source_target_pairs={{0,1},{1,0},{2,3},{3,2},{4,5},{5,4},{6,7},{7,6},{8,9},{9,8},{10,11... | collective-permute-start | bytes 1572872 | tf_op jit(solution)/shard_map/ppermute | solution.py:240
  48.6 3.2 %collective-permute-start.10 = (f32[8,8,128]{2,1,0:T(8,128)S(1)}, f32[8,8,128]{2,1,0:T(8,128)S(1)}, u32[]{:S(2)}, u32[]{:S(2)}) collective-permute-start(f32[8,8,128]{2,1,0:T(8,128)S(1)} %get-tuple-element.63.refs_1_), channel_id=1, source_target_pairs={{0,1},{1,0},{2,3},{3,2},{4,5},{5,4},{6,7},{7,6},{8,9},{9,8},{10,11... | collective-permute-start | bytes 98312 | tf_op jit(solution)/shard_map/ppermute | solution.py:240
  57.2 35.0 %all-to-all-start.4 = ((bf16[8,1040,128]{2,1,0:T(8,128)(2,1)}), bf16[8,1040,128]{2,1,0:T(8,128)(2,1)S(1)}, u32[]{:S(2)}, u32[]{:S(2)}) async-start(bf16[8,1040,128]{2,1,0:T(8,128)(2,1)} %get-tuple-element.68), calls=%async_computation.4 | async-start | bytes 4259840 | tf_op jit(solution)/shard_map/all_to_all | solution.py:339
  62.9 1.1 copy-start.1
  65.4 0.6 copy-start.5
  68.3 0.7 copy-start.3
  69.0 28.0 %copy-start.6 = (bf16[3,128,128]{2,1,0:T(8,128)(2,1)S(1)}, bf16[3,128,128]{2,1,0:T(8,128)(2,1)}, u32[]{:S(2)}) copy-start(bf16[3,128,128]{2,1,0:T(8,128)(2,1)} %copy-done.5) | copy-start | bytes 294916
  92.2 4.8 %copy-start.4 = (bf16[5,128,128]{2,1,0:T(8,128)(2,1)S(1)}, bf16[5,128,128]{2,1,0:T(8,128)(2,1)}, u32[]{:S(2)}) copy-start(bf16[5,128,128]{2,1,0:T(8,128)(2,1)} %copy-done.3) | copy-start | bytes 491524
  97.9 28.9 %all-to-all-start.5 = ((bf16[16,128,128]{2,1,0:T(8,128)(2,1)}), bf16[16,128,128]{2,1,0:T(8,128)(2,1)S(1)}, u32[]{:S(2)}, u32[]{:S(2)}) async-start(bf16[16,128,128]{2,1,0:T(8,128)(2,1)} %maximum_add_fusion), calls=%async_computation.5 | async-start | bytes 1048576 | tf_op jit(solution)/shard_map/all_to_all | solution.py:343
  126.7 0.8 copy-start.10
  127.5 2.1 %copy-start.7 = (f32[16384]{0:T(1024)S(1)}, f32[16384]{0:T(1024)}, u32[]{:S(2)}) copy-start(f32[16384]{0:T(1024)} %param.7) | copy-start | bytes 196612
  127.5 2.1 %copy-start.8 = (f32[16384]{0:T(1024)S(1)}, f32[16384]{0:T(1024)}, u32[]{:S(2)}) copy-start(f32[16384]{0:T(1024)} %param.8) | copy-start | bytes 196612
  127.5 2.1 %copy-start.9 = (f32[16384]{0:T(1024)S(1)}, f32[16384]{0:T(1024)}, u32[]{:S(2)}) copy-start(f32[16384]{0:T(1024)} %param.9) | copy-start | bytes 196612

commit v4 on v3

--- a/solution.py
+++ b/solution.py
@@ -18,8 +18,8 @@
 STEPS = 72.0
 OFFSET = 113.0
 
-PARTS = (3, 5, 8)
-PIECES = 4
+PARTS = (5, 6, 5)
+PIECES = 2
 PARAMS = pltpu.CompilerParams(vmem_limit_bytes=48 << 20)
 PARAMS_Q = pltpu.CompilerParams(vmem_limit_bytes=48 << 20)
 PARAMS_C = pltpu.CompilerParams(vmem_limit_bytes=48 << 20)
@@ -144,13 +144,22 @@
         copy(g, slot).wait()
 
 
-def decode_kernel(chips, groups, r_ref, aux_ref, o_ref, units):
-    g = pl.program_id(0)
+def decode_kernel(chips, groups, start, final, r_ref, aux_ref, before_ref, o_ref, buffer, units, sems, bad):
+    del before_ref
+    g, count = pl.program_id(0), pl.num_programs(0)
+    slot = lax.rem(g, 2)
+
+    def copy(step, at):
+        return pltpu.make_async_copy(buffer.at[at], o_ref.at[step + start], sems.at[at])
 
     @pl.when(g == 0)
     def _():
         for d in range(chips):
             units[d] = aux_ref[d].astype(jnp.float32)[0:8]
+
+    @pl.when(g >= 2)
+    def _():
+        copy(g - 2, slot).wait()
 
     rolled = [pltpu.roll(units[d], LANES - g * groups, 1) for d in range(chips)]
     for k in range(groups):
@@ -163,7 +172,32 @@
                 part = code[8 * s : 8 * s + 8]
                 size = jnp.floor(jnp.log2(jnp.abs(part)) * STEPS + (OFFSET * STEPS + 0.5))
                 total[s] = total[s] + size * jnp.where(part < 0, -unit, unit)
-        o_ref[0, at, :] = jnp.concatenate(requantized(total), axis=0).astype(jnp.bfloat16)
+        buffer[slot, at, :] = jnp.concatenate(requantized(total), axis=0).astype(jnp.bfloat16)
+    copy(g, slot).start()
+
+    @pl.when(g == count - 1)
+    def _():
+        @pl.when(count >= 2)
+        def _():
+            copy(g - 1, 1 - slot).wait()
+
+        copy(g, slot).wait()
+        if final:
+            total = units[0]
+            for d in range(1, chips):
+                total = total + units[d]
+
+            @pl.when(jnp.max(jnp.where(jnp.isnan(total), 1.0, 0.0)) > 0)
+            def _():
+                buffer[0] = jnp.full(buffer.shape[1:], jnp.nan, jnp.bfloat16)
+
+                def spoil(j, carry):
+                    one = pltpu.make_async_copy(buffer.at[0], o_ref.at[j], bad)
+                    one.start()
+                    one.wait()
+                    return carry
+
+                lax.fori_loop(0, o_ref.shape[0], spoil, 0)
 
 
 def first_kernel(nodes, groups, after_ref, x_ref, o_ref, scratch):
@@ -192,7 +226,7 @@
         o_ref[0, rows, :] = jnp.concatenate(requantized(parts), axis=0).astype(jnp.bfloat16)
 
 
-def update_kernel(replicas, groups, r_ref, p_ref, m_ref, v_ref, po_ref, mo_ref, vo_ref, scratch):
+def update_kernel(replicas, groups, r_ref, p_ref, m_ref, v_ref, po_ref, mo_ref, vo_ref, bad_ref, scratch):
     for k in range(groups):
         rows = slice(k * GROUP_ROWS, (k + 1) * GROUP_ROWS)
         total = r_ref[0, rows, :].astype(jnp.float32)
@@ -207,6 +241,8 @@
     mo_ref[...] = moment
     vo_ref[...] = second
     po_ref[...] = master - 0.02 * (moment / (jnp.sqrt(second) + 1e-08) + 0.1 * master)
+    spoilt = jnp.max(jnp.where(jnp.isnan(gradient[0:8]), 1.0, 0.0))
+    bad_ref[0] = jnp.where(spoilt > 0, 1, 0).astype(jnp.int32)
 
 
 COST = pl.CostEstimate(flops=1, bytes_accessed=1, transcendentals=0)
@@ -270,22 +306,29 @@
     )(own, scales, peer_scales, before, *peer)
 
 
-def node_sums(received, count, chips, shard):
-    rows, groups = shard // LANES, shard // GROUP
+def node_sums(received, partial, start, count, chips, final):
+    rows = partial.shape[1]
     return pl.pallas_call(
-        lambda *refs: decode_kernel(chips, groups, *refs),
+        lambda *refs: decode_kernel(chips, rows // GROUP_ROWS, start, final, *refs),
         name="decode_and_requantize",
         grid=(count,),
         in_specs=[
             pl.BlockSpec((chips, rows, LANES), lambda g: (0, g, 0)),
             pl.BlockSpec((chips, AUX_ROWS, LANES), lambda g: (0, count * rows // AUX_ROWS, 0)),
-        ],
-        out_specs=pl.BlockSpec((1, rows, LANES), lambda g: (g, 0, 0)),
-        out_shape=jax.ShapeDtypeStruct((count, rows, LANES), jnp.bfloat16),
-        scratch_shapes=[pltpu.VMEM((chips, 8, LANES), jnp.float32)],
+            pl.BlockSpec(memory_space=pl.ANY),
+        ],
+        out_specs=pl.BlockSpec(memory_space=pl.ANY),
+        out_shape=jax.ShapeDtypeStruct(partial.shape, partial.dtype),
+        scratch_shapes=[
+            pltpu.VMEM((2, rows, LANES), jnp.bfloat16),
+            pltpu.VMEM((chips, 8, LANES), jnp.float32),
+            pltpu.SemaphoreType.DMA((2,)),
+            pltpu.SemaphoreType.DMA,
+        ],
+        input_output_aliases={2: 0},
         compiler_params=PARAMS,
         cost_estimate=COST,
-    )(received, received)
+    )(received, received, partial)
 
 
 def plain_sums(grads, after, replicas, nodes, shard):
@@ -319,10 +362,12 @@
 def update(owned, master, moment, second):
     replicas, rows = owned.shape[:2]
     state = jax.ShapeDtypeStruct((rows, LANES), jnp.float32)
+    whole = pl.BlockSpec(memory_space=pltpu.VMEM)
     return pl.pallas_call(
         lambda *refs: update_kernel(replicas, rows // GROUP_ROWS, *refs),
         name="adamw_update",
-        out_shape=(state, state, state),
+        out_shape=(state, state, state, jax.ShapeDtypeStruct((1,), jnp.int32)),
+        out_specs=(whole, whole, whole, pl.BlockSpec(memory_space=pltpu.SMEM)),
         scratch_shapes=[pltpu.VMEM((rows, LANES), jnp.float32)],
         compiler_params=PARAMS,
     )(owned, master, moment, second)
@@ -333,23 +378,22 @@
     chips = lax.axis_size("chip")
     shard = master.shape[0]
     flag = jnp.zeros((8, LANES), jnp.float32)
-    partials, start = [], 0
+    partial = jnp.zeros((replicas, shard // LANES, LANES), jnp.bfloat16)
+    start = 0
     for count in PARTS:
         message, flag = pair_sums(*quantized(grads, flag, start, count, chips, shard), flag)
         received = lax.all_to_all(message, "chip", split_axis=0, concat_axis=0, tiled=True)
-        partials.append(node_sums(received, count, chips, shard))
+        partial = node_sums(received, partial, start, count, chips, start + count == replicas)
         start += count
-    partial = jnp.concatenate(partials, axis=0) + partials[-1][0, 0, 0] * 0
     owned = lax.all_to_all(partial, "group", split_axis=0, concat_axis=0, tiled=True)
     state = [a.reshape(shard // LANES, LANES) for a in (master, moment, second)]
-    owned, _ = lax.while_loop(
-        lambda carry: jnp.logical_and(carry[1] == 0, jnp.any(jnp.isnan(carry[0][:, 0, 0]))),
-        lambda carry: (
-            plain_sums(grads, carry[1].reshape(1), replicas, 2 * chips, shard), carry[1] + 1,
-        ),
-        (owned, jnp.int32(0)),
-    )
-    return tuple(a.reshape(shard) for a in update(owned, *state))
+
+    def general(carry):
+        *_, done = update(plain_sums(grads, carry[3], replicas, 2 * chips, shard), *state)
+        return (*_, jnp.zeros_like(done))
+
+    *outs, _ = lax.while_loop(lambda carry: carry[3][0] > 0, general, update(owned, *state))
+    return tuple(a.reshape(shard) for a in outs)
 
 
 def solution(mesh):

time: 133 us -> 124 us (0.932)
  blocking collectives: 0 us -> 27.4 us
  waiting for transfers between devices: 47.5 us -> 28.9 us
  starting transfers between devices: 31.8 us -> 20.1 us
  local copies, waits for them, and re-layouts: 4.81 us -> 2.37 us
  other arithmetic: 2.29 us -> 0 us
    all_to_all x0 -> x1, blocking collectives: none -> 27.4 us  [body(): lax.all_to_all(partial, 'group', split_axis=0, concat_axis=0, tiled=True)]
    all_to_all x1 -> x0, waiting for transfers between devices: 18 us -> none  [body(): lax.all_to_all(partial, 'group', split_axis=0, concat_axis=0, tiled=True)]
    all_to_all x1 -> x0, starting transfers between devices: 10.9 us -> none  [body(): lax.all_to_all(partial, 'group', split_axis=0, concat_axis=0, tiled=True)]
    pallas_call x3, Pallas kernels: 7.17 us -> 9.75 us  [node_sums(): pl.pallas_call(lambda *refs: decode_kernel(chips, rows // GROUP_ROWS, sta...]
    all_to_all x3, waiting for transfers between devices: 23.3 us -> 21.1 us  [body(): lax.all_to_all(message, 'chip', split_axis=0, concat_axis=0, tiled=True)]
    unnamed x22 -> x10, local copies, waits for them, and re-layouts: 4.3 us -> 2.27 us
    ppermute x15 -> x9, starting transfers between devices: 3.6 us -> 2.07 us  [quantized(): lax.ppermute(a, 'core', [(0, 1), (1, 0)])]
    ppermute x15 -> x9, waiting for transfers between devices: 6.24 us -> 7.76 us  [quantized(): lax.ppermute(a, 'core', [(0, 1), (1, 0)])]
  transfers between devices with their start and end apart: 19 -> 12, of which waited for: 5 -> 6; matrix products, arithmetic and copies ran while one was open for 0% -> 0% of each run, Pallas kernels for 23% -> 22%
where the time goes in v4:
time: 124 us; the launch traced here: 123 us
  Pallas kernels  43.2 us (35%)
  waiting for transfers between devices  28.9 us (23%)
  blocking collectives  27.4 us (22%)
  starting transfers between devices  20.1 us (16%)
  local copies, waits for them, and re-layouts  2.37 us (2%)
    all_to_all x1, blocking collectives, body(): lax.all_to_all(partial, 'group', split_axis=0, concat_axis=0, tiled=True)  27.4 us
    pallas_call x3, Pallas kernels, quantized(): pl.pallas_call(lambda *refs: pair_kernel(chips, groups, *refs), name='qua...  24.1 us
    all_to_all x3, waiting for transfers between devices, body(): lax.all_to_all(message, 'chip', split_axis=0, concat_axis=0, tiled=True)  21.1 us
    all_to_all x3, starting transfers between devices, body(): lax.all_to_all(message, 'chip', split_axis=0, concat_axis=0, tiled=True)  18.1 us
    pallas_call x3, Pallas kernels, node_sums(): pl.pallas_call(lambda *refs: decode_kernel(chips, rows // GROUP_ROWS, sta...  9.75 us
    pallas_call x3, Pallas kernels, pair_sums(): pl.pallas_call(lambda *refs: encode_kernel(chips, rows // GROUP_ROWS, cou...  8.57 us
    ppermute x9, waiting for transfers between devices, quantized(): lax.ppermute(a, 'core', [(0, 1), (1, 0)])  7.76 us
  transfers between devices with their start and end apart: 12, of which 6 were waited for; matrix products, arithmetic and copies ran while one was open for 0% of the time, Pallas kernels for 22%

profile of v4, /device:TPU:2, one launch (start us, length us, event | category | flops | bytes accessed | tf_op | source)
XLA Modules:
  0.0 123.3 jit_solution(3167066209360438861)
XLA Ops:
  0.6 7.6 %quantize.3 = (bf16[8,5,128,128]{3,2,1,0:T(8,128)(2,1)S(1)}, bf16[4,5,128,128]{3,2,1,0:T(8,128)(2,1)S(1)}, bf16[4,5,128,128]{3,2,1,0:T(8,128)(2,1)S(1)}, f32[5,8,128]{2,1,0:T(8,128)S(1)}) custom-call(s32[1]{0:T(128)} %bitcast.1.refs_0_, bf16[1,4194304]{1,0:T(2,128)(2,1)} %refs_1_.5, f32[8,128]{1,0:T(8,128)S(1)} %broadcast_in_dim.6.refs_2_.refs_3_), custom_call_target="tpu_custom_call" | custom-call | flops 1 | bytes 1 | tf_op jit(solution)/shard_map/quantize/pallas_call | solution.py:261
  8.3 0.1 collective-permute-start.1
  8.4 0.5 collective-permute-start.2
  8.9 0.1 collective-permute-start
  9.0 2.5 %collective-permute-done.refs_2_ = f32[5,8,128]{2,1,0:T(8,128)S(1)} collective-permute-done((f32[5,8,128]{2,1,0:T(8,128)S(1)}, f32[5,8,128]{2,1,0:T(8,128)S(1)}, u32[]{:S(2)}, u32[]{:S(2)}) %collective-permute-start) | collective-permute-done | bytes 20512 | tf_op jit(solution)/shard_map/ppermute | solution.py:276
  11.4 0.0 collective-permute-done.1.refs_4_
  11.4 0.0 collective-permute-done.2.refs_5_
  11.4 3.2 %add_and_encode.3 = (bf16[8,656,128]{2,1,0:T(8,128)(2,1)}, f32[8,128]{1,0:T(8,128)S(1)}) custom-call(bf16[8,5,128,128]{3,2,1,0:T(8,128)(2,1)S(1)} %get-tuple-element.68.refs_0_, f32[5,8,128]{2,1,0:T(8,128)S(1)} %get-tuple-element.69.refs_1_, f32[5,8,128]{2,1,0:T(8,128)S(1)} %collective-permute-done.refs_2_, f32[8,128]{1,0:T(8,128)S(1)} %broadcast_in_dim.6.refs_2_.refs_3_, ...), custom_call_target="tpu_custom_call" | custom-call | flops 1 | bytes 1 | tf_op jit(solution)/shard_map/add_and_encode/pallas_call | solution.py:287
  14.7 5.9 %all-to-all-start.4 = ((bf16[8,656,128]{2,1,0:T(8,128)(2,1)}), bf16[8,656,128]{2,1,0:T(8,128)(2,1)S(1)}, u32[]{:S(2)}, u32[]{:S(2)}) async-start(bf16[8,656,128]{2,1,0:T(8,128)(2,1)} %get-tuple-element.84), calls=%async_computation.4 | async-start | bytes 2686976 | tf_op jit(solution)/shard_map/all_to_all | solution.py:385
  20.5 8.9 %quantize.4 = (bf16[8,6,128,128]{3,2,1,0:T(8,128)(2,1)S(1)}, bf16[4,6,128,128]{3,2,1,0:T(8,128)(2,1)S(1)}, bf16[4,6,128,128]{3,2,1,0:T(8,128)(2,1)S(1)}, f32[6,8,128]{2,1,0:T(8,128)S(1)}) custom-call(s32[1]{0:T(128)} %bitcast.1.refs_0_, bf16[1,4194304]{1,0:T(2,128)(2,1)} %refs_1_.5, f32[8,128]{1,0:T(8,128)S(1)} %get-tuple-element.72.refs_2_.refs_3_), custom_call_target="tpu_custom_call" | custom-call | flops 1 | bytes 1 | tf_op jit(solution)/shard_map/quantize/pallas_call | solution.py:261
  29.4 0.1 collective-permute-start.4
  29.5 0.5 collective-permute-start.5
  30.0 0.1 collective-permute-start.3
  30.1 2.8 %collective-permute-done.3.refs_2_ = f32[6,8,128]{2,1,0:T(8,128)S(1)} collective-permute-done((f32[6,8,128]{2,1,0:T(8,128)S(1)}, f32[6,8,128]{2,1,0:T(8,128)S(1)}, u32[]{:S(2)}, u32[]{:S(2)}) %collective-permute-start.3) | collective-permute-done | bytes 24608 | tf_op jit(solution)/shard_map/ppermute | solution.py:276
  33.0 0.0 collective-permute-done.4.refs_4_
  33.0 0.0 collective-permute-done.5.refs_5_
  33.0 2.6 %add_and_encode.4 = (bf16[8,784,128]{2,1,0:T(8,128)(2,1)S(1)}, f32[8,128]{1,0:T(8,128)S(1)}) custom-call(bf16[8,6,128,128]{3,2,1,0:T(8,128)(2,1)S(1)} %get-tuple-element.73.refs_0_, f32[6,8,128]{2,1,0:T(8,128)S(1)} %get-tuple-element.74.refs_1_, f32[6,8,128]{2,1,0:T(8,128)S(1)} %collective-permute-done.3.refs_2_, ...), custom_call_target="tpu_custom_call" | custom-call | flops 1 | bytes 1 | tf_op jit(solution)/shard_map/add_and_encode/pallas_call | solution.py:287
  35.5 0.0 copy-start
  35.6 1.2 copy-done
  36.7 2.9 %all-to-all-done.4.refs_0_.refs_1_ = bf16[8,656,128]{2,1,0:T(8,128)(2,1)S(1)} async-done(((bf16[8,656,128]{2,1,0:T(8,128)(2,1)}), bf16[8,656,128]{2,1,0:T(8,128)(2,1)S(1)}, u32[]{:S(2)}, u32[]{:S(2)}) %all-to-all-start.4) | async-done | bytes 1343520 | tf_op jit(solution)/shard_map/all_to_all | solution.py:385
  39.6 5.7 %all-to-all-start.3 = ((bf16[8,784,128]{2,1,0:T(8,128)(2,1)}), bf16[8,784,128]{2,1,0:T(8,128)(2,1)S(1)}, u32[]{:S(2)}, u32[]{:S(2)}) async-start(bf16[8,784,128]{2,1,0:T(8,128)(2,1)} %copy-done), calls=%async_computation.3 | async-start | bytes 3211264 | tf_op jit(solution)/shard_map/all_to_all | solution.py:385
  45.4 7.6 %quantize.5 = (bf16[8,5,128,128]{3,2,1,0:T(8,128)(2,1)S(1)}, bf16[4,5,128,128]{3,2,1,0:T(8,128)(2,1)S(1)}, bf16[4,5,128,128]{3,2,1,0:T(8,128)(2,1)S(1)}, f32[5,8,128]{2,1,0:T(8,128)S(1)}) custom-call(s32[1]{0:T(128)} %bitcast.1.refs_0_, bf16[1,4194304]{1,0:T(2,128)(2,1)} %refs_1_.5, f32[8,128]{1,0:T(8,128)S(1)} %get-tuple-element.77.refs_2_.refs_3_), custom_call_target="tpu_custom_call" | custom-call | flops 1 | bytes 1 | tf_op jit(solution)/shard_map/quantize/pallas_call | solution.py:261
  53.0 0.1 collective-permute-start.7
  53.1 0.5 collective-permute-start.8
  53.6 0.1 collective-permute-start.6
  53.7 2.5 %collective-permute-done.6.refs_2_ = f32[5,8,128]{2,1,0:T(8,128)S(1)} collective-permute-done((f32[5,8,128]{2,1,0:T(8,128)S(1)}, f32[5,8,128]{2,1,0:T(8,128)S(1)}, u32[]{:S(2)}, u32[]{:S(2)}) %collective-permute-start.6) | collective-permute-done | bytes 20512 | tf_op jit(solution)/shard_map/ppermute | solution.py:276
  56.1 0.0 collective-permute-done.7.refs_4_
  56.1 0.0 collective-permute-done.8.refs_5_
  56.1 2.8 %add_and_encode.5 = (bf16[8,656,128]{2,1,0:T(8,128)(2,1)S(1)}, f32[8,128]{1,0:T(8,128)}) custom-call(bf16[8,5,128,128]{3,2,1,0:T(8,128)(2,1)S(1)} %get-tuple-element.78.refs_0_, f32[5,8,128]{2,1,0:T(8,128)S(1)} %get-tuple-element.79.refs_1_, f32[5,8,128]{2,1,0:T(8,128)S(1)} %collective-permute-done.6.refs_2_, ...), custom_call_target="tpu_custom_call" | custom-call | flops 1 | bytes 1 | tf_op jit(solution)/shard_map/add_and_encode/pallas_call | solution.py:287
  58.9 0.0 copy-start.1
  58.9 1.1 copy-done.1
  60.0 6.7 %all-to-all-done.3.refs_0_.refs_1_ = bf16[8,784,128]{2,1,0:T(8,128)(2,1)S(1)} async-done(((bf16[8,784,128]{2,1,0:T(8,128)(2,1)}), bf16[8,784,128]{2,1,0:T(8,128)(2,1)S(1)}, u32[]{:S(2)}, u32[]{:S(2)}) %all-to-all-start.3) | async-done | bytes 1605664 | tf_op jit(solution)/shard_map/all_to_all | solution.py:385
  66.7 6.5 %all-to-all-start.2 = ((bf16[8,656,128]{2,1,0:T(8,128)(2,1)}), bf16[8,656,128]{2,1,0:T(8,128)(2,1)}, u32[]{:S(2)}, u32[]{:S(2)}) async-start(bf16[8,656,128]{2,1,0:T(8,128)(2,1)} %copy-done.1), calls=%async_computation.2 | async-start | bytes 2686976 | tf_op jit(solution)/shard_map/all_to_all | solution.py:385
  73.2 0.1 broadcast_in_dim.7.refs_2_
  73.3 2.5 %decode_and_requantize.3.refs_2_ = bf16[16,128,128]{2,1,0:T(8,128)(2,1)S(1)} custom-call(bf16[8,656,128]{2,1,0:T(8,128)(2,1)S(1)} %all-to-all-done.4.refs_0_.refs_1_, bf16[8,656,128]{2,1,0:T(8,128)(2,1)S(1)} %all-to-all-done.4.refs_0_.refs_1_, bf16[16,128,128]{2,1,0:T(8,128)(2,1)S(1)} %broadcast_in_dim.7.refs_2_), custom_call_target="tpu_custom_call", output_to_operand_aliasing={{}: (2, {})} | custom-call | flops 1 | bytes 1 | tf_op jit(solution)/shard_map/decode_and_requantize/pallas_call | solution.py:311
  75.8 3.0 %decode_and_requantize.4.refs_2_ = bf16[16,128,128]{2,1,0:T(8,128)(2,1)S(1)} custom-call(bf16[8,784,128]{2,1,0:T(8,128)(2,1)S(1)} %all-to-all-done.3.refs_0_.refs_1_, bf16[8,784,128]{2,1,0:T(8,128)(2,1)S(1)} %all-to-all-done.3.refs_0_.refs_1_, bf16[16,128,128]{2,1,0:T(8,128)(2,1)S(1)} %decode_and_requantize.3.refs_2_), custom_call_target="tpu_custom_call", output_to_operand_aliasing={{}: (2, {})} | custom-call | flops 1 | bytes 1 | tf_op jit(solution)/shard_map/decode_and_requantize/pallas_call | solution.py:311
  78.8 0.0 copy-start.2
  78.8 0.0 copy-start.3
  78.8 0.0 copy-start.4
  78.8 11.5 %all-to-all-done.2.refs_0_.refs_1_ = bf16[8,656,128]{2,1,0:T(8,128)(2,1)} async-done(((bf16[8,656,128]{2,1,0:T(8,128)(2,1)}), bf16[8,656,128]{2,1,0:T(8,128)(2,1)}, u32[]{:S(2)}, u32[]{:S(2)}) %all-to-all-start.2) | async-done | bytes 1343520 | tf_op jit(solution)/shard_map/all_to_all | solution.py:385
  90.3 4.3 %decode_and_requantize.5 = bf16[16,128,128]{2,1,0:T(8,128)(2,1)S(1)} custom-call(bf16[8,656,128]{2,1,0:T(8,128)(2,1)} %all-to-all-done.2.refs_0_.refs_1_, bf16[8,656,128]{2,1,0:T(8,128)(2,1)} %all-to-all-done.2.refs_0_.refs_1_, bf16[16,128,128]{2,1,0:T(8,128)(2,1)S(1)} %decode_and_requantize.4.refs_2_), custom_call_target="tpu_custom_call", output_to_operand_aliasing={{}: (2, {})} | custom-call | flops 1 | bytes 1 | tf_op jit(solution)/shard_map/decode_and_requantize/pallas_call | solution.py:311
  94.6 27.4 %all_to_all.29.refs_0_ = bf16[16,128,128]{2,1,0:T(8,128)(2,1)S(1)} all-to-all(bf16[16,128,128]{2,1,0:T(8,128)(2,1)S(1)} %decode_and_requantize.5), channel_id=1, replica_groups=mesh['group'=16,'chip'=8,'core'=2] {'group'}, dimensions={0} | all-to-all | bytes 1048576 | tf_op jit(solution)/shard_map/all_to_all | solution.py:388
  122.0 0.0 copy-done.2
  122.0 0.0 copy-done.3
  122.0 0.0 copy-done.4
  122.0 0.8 adamw_update.3
  122.8 0.6 while.13
  (1 shorter events, 0.0 us)
Async XLA Ops:
  8.3 3.2 %collective-permute-start.1 = (bf16[4,5,128,128]{3,2,1,0:T(8,128)(2,1)S(1)}, bf16[4,5,128,128]{3,2,1,0:T(8,128)(2,1)S(1)}, u32[]{:S(2)}, u32[]{:S(2)}) collective-permute-start(bf16[4,5,128,128]{3,2,1,0:T(8,128)(2,1)S(1)} %get-tuple-element.70), channel_id=1, source_target_pairs={{0,1},{1,0},{2,3},{3,2},{4,5},{5,4},{6,7},{7,6},{8,9},{9,8},{10,11... | collective-permute-start | bytes 1966088 | tf_op jit(solution)/shard_map/ppermute | solution.py:276
  8.4 3.1 %collective-permute-start.2 = (bf16[4,5,128,128]{3,2,1,0:T(8,128)(2,1)S(1)}, bf16[4,5,128,128]{3,2,1,0:T(8,128)(2,1)S(1)}, u32[]{:S(2)}, u32[]{:S(2)}) collective-permute-start(bf16[4,5,128,128]{3,2,1,0:T(8,128)(2,1)S(1)} %get-tuple-element.71), channel_id=1, source_target_pairs={{0,1},{1,0},{2,3},{3,2},{4,5},{5,4},{6,7},{7,6},{8,9},{9,8},{10,11... | collective-permute-start | bytes 1966088 | tf_op jit(solution)/shard_map/ppermute | solution.py:276
  8.9 2.6 %collective-permute-start = (f32[5,8,128]{2,1,0:T(8,128)S(1)}, f32[5,8,128]{2,1,0:T(8,128)S(1)}, u32[]{:S(2)}, u32[]{:S(2)}) collective-permute-start(f32[5,8,128]{2,1,0:T(8,128)S(1)} %get-tuple-element.69.refs_1_), channel_id=1, source_target_pairs={{0,1},{1,0},{2,3},{3,2},{4,5},{5,4},{6,7},{7,6},{8,9},{9,8},{10,11... | collective-permute-start | bytes 61448 | tf_op jit(solution)/shard_map/ppermute | solution.py:276
  14.7 25.0 %all-to-all-start.4 = ((bf16[8,656,128]{2,1,0:T(8,128)(2,1)}), bf16[8,656,128]{2,1,0:T(8,128)(2,1)S(1)}, u32[]{:S(2)}, u32[]{:S(2)}) async-start(bf16[8,656,128]{2,1,0:T(8,128)(2,1)} %get-tuple-element.84), calls=%async_computation.4 | async-start | bytes 2686976 | tf_op jit(solution)/shard_map/all_to_all | solution.py:385
  29.4 3.5 %collective-permute-start.4 = (bf16[4,6,128,128]{3,2,1,0:T(8,128)(2,1)S(1)}, bf16[4,6,128,128]{3,2,1,0:T(8,128)(2,1)S(1)}, u32[]{:S(2)}, u32[]{:S(2)}) collective-permute-start(bf16[4,6,128,128]{3,2,1,0:T(8,128)(2,1)S(1)} %get-tuple-element.75), channel_id=1, source_target_pairs={{0,1},{1,0},{2,3},{3,2},{4,5},{5,4},{6,7},{7,6},{8,9},{9,8},{10,11... | collective-permute-start | bytes 2359304 | tf_op jit(solution)/shard_map/ppermute | solution.py:276
  29.5 3.4 %collective-permute-start.5 = (bf16[4,6,128,128]{3,2,1,0:T(8,128)(2,1)S(1)}, bf16[4,6,128,128]{3,2,1,0:T(8,128)(2,1)S(1)}, u32[]{:S(2)}, u32[]{:S(2)}) collective-permute-start(bf16[4,6,128,128]{3,2,1,0:T(8,128)(2,1)S(1)} %get-tuple-element.76), channel_id=1, source_target_pairs={{0,1},{1,0},{2,3},{3,2},{4,5},{5,4},{6,7},{7,6},{8,9},{9,8},{10,11... | collective-permute-start | bytes 2359304 | tf_op jit(solution)/shard_map/ppermute | solution.py:276
  30.0 2.9 %collective-permute-start.3 = (f32[6,8,128]{2,1,0:T(8,128)S(1)}, f32[6,8,128]{2,1,0:T(8,128)S(1)}, u32[]{:S(2)}, u32[]{:S(2)}) collective-permute-start(f32[6,8,128]{2,1,0:T(8,128)S(1)} %get-tuple-element.74.refs_1_), channel_id=1, source_target_pairs={{0,1},{1,0},{2,3},{3,2},{4,5},{5,4},{6,7},{7,6},{8,9},{9,8},{10,11... | collective-permute-start | bytes 73736 | tf_op jit(solution)/shard_map/ppermute | solution.py:276
  35.5 1.2 copy-start
  39.6 27.1 %all-to-all-start.3 = ((bf16[8,784,128]{2,1,0:T(8,128)(2,1)}), bf16[8,784,128]{2,1,0:T(8,128)(2,1)S(1)}, u32[]{:S(2)}, u32[]{:S(2)}) async-start(bf16[8,784,128]{2,1,0:T(8,128)(2,1)} %copy-done), calls=%async_computation.3 | async-start | bytes 3211264 | tf_op jit(solution)/shard_map/all_to_all | solution.py:385
  53.0 3.2 %collective-permute-start.7 = (bf16[4,5,128,128]{3,2,1,0:T(8,128)(2,1)S(1)}, bf16[4,5,128,128]{3,2,1,0:T(8,128)(2,1)S(1)}, u32[]{:S(2)}, u32[]{:S(2)}) collective-permute-start(bf16[4,5,128,128]{3,2,1,0:T(8,128)(2,1)S(1)} %get-tuple-element.80), channel_id=1, source_target_pairs={{0,1},{1,0},{2,3},{3,2},{4,5},{5,4},{6,7},{7,6},{8,9},{9,8},{10,11... | collective-permute-start | bytes 1966088 | tf_op jit(solution)/shard_map/ppermute | solution.py:276
  53.1 3.1 %collective-permute-start.8 = (bf16[4,5,128,128]{3,2,1,0:T(8,128)(2,1)S(1)}, bf16[4,5,128,128]{3,2,1,0:T(8,128)(2,1)S(1)}, u32[]{:S(2)}, u32[]{:S(2)}) collective-permute-start(bf16[4,5,128,128]{3,2,1,0:T(8,128)(2,1)S(1)} %get-tuple-element.81), channel_id=1, source_target_pairs={{0,1},{1,0},{2,3},{3,2},{4,5},{5,4},{6,7},{7,6},{8,9},{9,8},{10,11... | collective-permute-start | bytes 1966088 | tf_op jit(solution)/shard_map/ppermute | solution.py:276
  53.6 2.6 %collective-permute-start.6 = (f32[5,8,128]{2,1,0:T(8,128)S(1)}, f32[5,8,128]{2,1,0:T(8,128)S(1)}, u32[]{:S(2)}, u32[]{:S(2)}) collective-permute-start(f32[5,8,128]{2,1,0:T(8,128)S(1)} %get-tuple-element.79.refs_1_), channel_id=1, source_target_pairs={{0,1},{1,0},{2,3},{3,2},{4,5},{5,4},{6,7},{7,6},{8,9},{9,8},{10,11... | collective-permute-start | bytes 61448 | tf_op jit(solution)/shard_map/ppermute | solution.py:276
  58.9 1.1 copy-start.1
  66.7 23.6 %all-to-all-start.2 = ((bf16[8,656,128]{2,1,0:T(8,128)(2,1)}), bf16[8,656,128]{2,1,0:T(8,128)(2,1)}, u32[]{:S(2)}, u32[]{:S(2)}) async-start(bf16[8,656,128]{2,1,0:T(8,128)(2,1)} %copy-done.1), calls=%async_computation.2 | async-start | bytes 2686976 | tf_op jit(solution)/shard_map/all_to_all | solution.py:385
  78.8 43.2 %copy-start.2 = (f32[16384]{0:T(1024)S(1)}, f32[16384]{0:T(1024)}, u32[]{:S(2)}) copy-start(f32[16384]{0:T(1024)} %param.7) | copy-start | bytes 196612
  78.8 43.2 %copy-start.3 = (f32[16384]{0:T(1024)S(1)}, f32[16384]{0:T(1024)}, u32[]{:S(2)}) copy-start(f32[16384]{0:T(1024)} %param.8) | copy-start | bytes 196612
  78.8 43.2 %copy-start.4 = (f32[16384]{0:T(1024)S(1)}, f32[16384]{0:T(1024)}, u32[]{:S(2)}) copy-start(f32[16384]{0:T(1024)} %param.9) | copy-start | bytes 196612

commit v5 on v4

--- a/solution.py
+++ b/solution.py
@@ -18,7 +18,7 @@
 STEPS = 72.0
 OFFSET = 113.0
 
-PARTS = (5, 6, 5)
+PARTS = (8, 8)
 PIECES = 2
 PARAMS = pltpu.CompilerParams(vmem_limit_bytes=48 << 20)
 PARAMS_Q = pltpu.CompilerParams(vmem_limit_bytes=48 << 20)
@@ -70,14 +70,14 @@
     tile = tiles[0]
     for k in range(1, groups):
         tile = jnp.maximum(tile, tiles[k])
-    scale, inverse = scale_of(tile)
+    scale, _ = scale_of(tile)
     scale_ref[0] = jnp.where(tile > 0, scale, 0.0)
 
     for d, half, k in where:
         at = half * SEND_LANE + d * groups + k
         s_col = jnp.broadcast_to(scale[:, at : at + 1], (8, LANES))
-        i_col = jnp.broadcast_to(inverse[:, at : at + 1], (8, LANES))
-        done = [jnp.floor(part * i_col + 0.5) * s_col for part in parts_of(d, half, k)]
+        grid, nudge = s_col * (1.5 * 2.0**23), s_col * 2.0**-12
+        done = [((part + nudge) + grid) - grid for part in parts_of(d, half, k)]
         o_ref, slot = (send_refs[d % PIECES], d // PIECES) if half else (own_ref, d)
         at = slice(k * GROUP_ROWS, (k + 1) * GROUP_ROWS)
         o_ref[slot, 0, at, :] = jnp.concatenate(done, axis=0).astype(jnp.bfloat16)
@@ -144,7 +144,9 @@
         copy(g, slot).wait()
 
 
-def decode_kernel(chips, groups, start, final, r_ref, aux_ref, before_ref, o_ref, buffer, units, sems, bad):
+def decode_kernel(
+    chips, groups, start, final, r_ref, aux_ref, before_ref, o_ref, buffer, units, spoilt, sems, bad
+):
     del before_ref
     g, count = pl.program_id(0), pl.num_programs(0)
     slot = lax.rem(g, 2)
@@ -154,8 +156,12 @@
 
     @pl.when(g == 0)
     def _():
+        total = jnp.zeros((8, LANES), jnp.float32)
         for d in range(chips):
             units[d] = aux_ref[d].astype(jnp.float32)[0:8]
+            total = total + units[d]
+        if final:
+            spoilt[0] = jnp.max(jnp.where(jnp.isnan(total), 1, 0)).astype(jnp.int32)
 
     @pl.when(g >= 2)
     def _():
@@ -183,11 +189,7 @@
 
         copy(g, slot).wait()
         if final:
-            total = units[0]
-            for d in range(1, chips):
-                total = total + units[d]
-
-            @pl.when(jnp.max(jnp.where(jnp.isnan(total), 1.0, 0.0)) > 0)
+            @pl.when(spoilt[0] > 0)
             def _():
                 buffer[0] = jnp.full(buffer.shape[1:], jnp.nan, jnp.bfloat16)
 
@@ -322,6 +324,7 @@
         scratch_shapes=[
             pltpu.VMEM((2, rows, LANES), jnp.bfloat16),
             pltpu.VMEM((chips, 8, LANES), jnp.float32),
+            pltpu.SMEM((1,), jnp.int32),
             pltpu.SemaphoreType.DMA((2,)),
             pltpu.SemaphoreType.DMA,
         ],

time: 124 us -> 128 us (1.032)
  waiting for transfers between devices: 28.9 us -> 40.8 us
  starting transfers between devices: 20.1 us -> 14.2 us
  local copies, waits for them, and re-layouts: 2.37 us -> 0.12 us
    all_to_all x3 -> x2, waiting for transfers between devices: 21.1 us -> 33.6 us  [body(): lax.all_to_all(message, 'chip', split_axis=0, concat_axis=0, tiled=True)]
    all_to_all x3 -> x2, starting transfers between devices: 18.1 us -> 12.8 us  [body(): lax.all_to_all(message, 'chip', split_axis=0, concat_axis=0, tiled=True)]
    pallas_call x3 -> x2, Pallas kernels: 24.1 us -> 21.8 us  [quantized(): pl.pallas_call(lambda *refs: pair_kernel(chips, groups, *refs), name='qua...]
    unnamed x10 -> x6, local copies, waits for them, and re-layouts: 2.27 us -> 0.02 us
    pallas_call x3 -> x2, Pallas kernels: 8.57 us -> 10 us  [pair_sums(): pl.pallas_call(lambda *refs: encode_kernel(chips, rows // GROUP_ROWS, cou...]
    ppermute x9 -> x6, waiting for transfers between devices: 7.76 us -> 7.2 us  [quantized(): lax.ppermute(a, 'core', [(0, 1), (1, 0)])]
    pallas_call x3 -> x2, Pallas kernels: 9.75 us -> 10.2 us  [node_sums(): pl.pallas_call(lambda *refs: decode_kernel(chips, rows // GROUP_ROWS, sta...]
  transfers between devices with their start and end apart: 12 -> 8, of which waited for: 6 -> 4; matrix products, arithmetic and copies ran while one was open for 0% -> 0% of each run, Pallas kernels for 22% -> 16%
where the time goes in v5:
time: 128 us; the launch traced here: 127 us
  Pallas kernels  42.8 us (33%)
  waiting for transfers between devices  40.8 us (32%)
  blocking collectives  28 us (22%)
  starting transfers between devices  14.2 us (11%)
    all_to_all x2, waiting for transfers between devices, body(): lax.all_to_all(message, 'chip', split_axis=0, concat_axis=0, tiled=True)  33.6 us
    all_to_all x1, blocking collectives, body(): lax.all_to_all(partial, 'group', split_axis=0, concat_axis=0, tiled=True)  28 us
    pallas_call x2, Pallas kernels, quantized(): pl.pallas_call(lambda *refs: pair_kernel(chips, groups, *refs), name='qua...  21.8 us
    all_to_all x2, starting transfers between devices, body(): lax.all_to_all(message, 'chip', split_axis=0, concat_axis=0, tiled=True)  12.8 us
    pallas_call x2, Pallas kernels, node_sums(): pl.pallas_call(lambda *refs: decode_kernel(chips, rows // GROUP_ROWS, sta...  10.2 us
    pallas_call x2, Pallas kernels, pair_sums(): pl.pallas_call(lambda *refs: encode_kernel(chips, rows // GROUP_ROWS, cou...  10 us
    ppermute x6, waiting for transfers between devices, quantized(): lax.ppermute(a, 'core', [(0, 1), (1, 0)])  7.2 us
  transfers between devices with their start and end apart: 8, of which 4 were waited for; matrix products, arithmetic and copies ran while one was open for 0% of the time, Pallas kernels for 16%

profile of v5, /device:TPU:2, one launch (start us, length us, event | category | flops | bytes accessed | tf_op | source)
XLA Modules:
  0.0 127.3 jit_solution(12624959236832813776)
XLA Ops:
  0.6 10.9 %quantize.2 = (bf16[8,8,128,128]{3,2,1,0:T(8,128)(2,1)S(1)}, bf16[4,8,128,128]{3,2,1,0:T(8,128)(2,1)S(1)}, bf16[4,8,128,128]{3,2,1,0:T(8,128)(2,1)S(1)}, f32[8,8,128]{2,1,0:T(8,128)S(1)}) custom-call(s32[1]{0:T(128)} %bitcast.1.refs_0_, bf16[1,4194304]{1,0:T(2,128)(2,1)} %refs_1_.3, f32[8,128]{1,0:T(8,128)S(1)} %broadcast_in_dim.6.refs_2_.refs_3_), custom_call_target="tpu_custom_call" | custom-call | flops 1 | bytes 1 | tf_op jit(solution)/shard_map/quantize/pallas_call | solution.py:263
  11.5 0.1 collective-permute-start.1
  11.6 0.5 collective-permute-start.2
  12.1 0.1 collective-permute-start
  12.2 3.6 %collective-permute-done.refs_2_ = f32[8,8,128]{2,1,0:T(8,128)S(1)} collective-permute-done((f32[8,8,128]{2,1,0:T(8,128)S(1)}, f32[8,8,128]{2,1,0:T(8,128)S(1)}, u32[]{:S(2)}, u32[]{:S(2)}) %collective-permute-start) | collective-permute-done | bytes 32800 | tf_op jit(solution)/shard_map/ppermute | solution.py:278
  15.8 0.0 collective-permute-done.1.refs_4_
  15.8 0.0 collective-permute-done.2.refs_5_
  15.8 4.7 %add_and_encode.2 = (bf16[8,1040,128]{2,1,0:T(8,128)(2,1)}, f32[8,128]{1,0:T(8,128)S(1)}) custom-call(bf16[8,8,128,128]{3,2,1,0:T(8,128)(2,1)S(1)} %get-tuple-element.62.refs_0_, f32[8,8,128]{2,1,0:T(8,128)S(1)} %get-tuple-element.63.refs_1_, f32[8,8,128]{2,1,0:T(8,128)S(1)} %collective-permute-done.refs_2_, f32[8,128]{1,0:T(8,128)S(1)} %broadcast_in_dim.6.refs_2_.refs_3_, ...), custom_call_target="tpu_custom_call" | custom-call | flops 1 | bytes 1 | tf_op jit(solution)/shard_map/add_and_encode/pallas_call | solution.py:289
  20.6 5.9 %all-to-all-start.3 = ((bf16[8,1040,128]{2,1,0:T(8,128)(2,1)}), bf16[8,1040,128]{2,1,0:T(8,128)(2,1)S(1)}, u32[]{:S(2)}, u32[]{:S(2)}) async-start(bf16[8,1040,128]{2,1,0:T(8,128)(2,1)} %get-tuple-element.72), calls=%async_computation.3 | async-start | bytes 4259840 | tf_op jit(solution)/shard_map/all_to_all | solution.py:388
  26.4 10.9 %quantize.3 = (bf16[8,8,128,128]{3,2,1,0:T(8,128)(2,1)S(1)}, bf16[4,8,128,128]{3,2,1,0:T(8,128)(2,1)S(1)}, bf16[4,8,128,128]{3,2,1,0:T(8,128)(2,1)S(1)}, f32[8,8,128]{2,1,0:T(8,128)S(1)}) custom-call(s32[1]{0:T(128)} %bitcast.1.refs_0_, bf16[1,4194304]{1,0:T(2,128)(2,1)} %refs_1_.3, f32[8,128]{1,0:T(8,128)S(1)} %get-tuple-element.66.refs_2_.refs_3_), custom_call_target="tpu_custom_call" | custom-call | flops 1 | bytes 1 | tf_op jit(solution)/shard_map/quantize/pallas_call | solution.py:263
  37.3 0.1 collective-permute-start.4
  37.4 0.5 collective-permute-start.5
  37.9 0.1 collective-permute-start.3
  38.0 3.6 %collective-permute-done.3.refs_2_ = f32[8,8,128]{2,1,0:T(8,128)S(1)} collective-permute-done((f32[8,8,128]{2,1,0:T(8,128)S(1)}, f32[8,8,128]{2,1,0:T(8,128)S(1)}, u32[]{:S(2)}, u32[]{:S(2)}) %collective-permute-start.3) | collective-permute-done | bytes 32800 | tf_op jit(solution)/shard_map/ppermute | solution.py:278
  41.6 0.0 collective-permute-done.4.refs_4_
  41.6 0.0 collective-permute-done.5.refs_5_
  41.6 5.3 %add_and_encode.3 = (bf16[8,1040,128]{2,1,0:T(8,128)(2,1)}, f32[8,128]{1,0:T(8,128)}) custom-call(bf16[8,8,128,128]{3,2,1,0:T(8,128)(2,1)S(1)} %get-tuple-element.67.refs_0_, f32[8,8,128]{2,1,0:T(8,128)S(1)} %get-tuple-element.68.refs_1_, f32[8,8,128]{2,1,0:T(8,128)S(1)} %collective-permute-done.3.refs_2_, f32[8,128]{1,0:T(8,128)S(1)} %get-tuple-element.66.refs_2_.refs_3_, ...), custom_call_target="tpu_custom_call" | custom-call | flops 1 | bytes 1 | tf_op jit(solution)/shard_map/add_and_encode/pallas_call | solution.py:289
  46.9 9.2 %all-to-all-done.3.refs_0_.refs_1_ = bf16[8,1040,128]{2,1,0:T(8,128)(2,1)S(1)} async-done(((bf16[8,1040,128]{2,1,0:T(8,128)(2,1)}), bf16[8,1040,128]{2,1,0:T(8,128)(2,1)S(1)}, u32[]{:S(2)}, u32[]{:S(2)}) %all-to-all-start.3) | async-done | bytes 2129952 | tf_op jit(solution)/shard_map/all_to_all | solution.py:388
  56.1 6.9 %all-to-all-start.2 = ((bf16[8,1040,128]{2,1,0:T(8,128)(2,1)}), bf16[8,1040,128]{2,1,0:T(8,128)(2,1)}, u32[]{:S(2)}, u32[]{:S(2)}) async-start(bf16[8,1040,128]{2,1,0:T(8,128)(2,1)} %get-tuple-element.71), calls=%async_computation.2 | async-start | bytes 4259840 | tf_op jit(solution)/shard_map/all_to_all | solution.py:388
  63.1 0.1 broadcast_in_dim.7.refs_2_
  63.2 4.0 %decode_and_requantize.2.refs_2_ = bf16[16,128,128]{2,1,0:T(8,128)(2,1)S(1)} custom-call(bf16[8,1040,128]{2,1,0:T(8,128)(2,1)S(1)} %all-to-all-done.3.refs_0_.refs_1_, bf16[8,1040,128]{2,1,0:T(8,128)(2,1)S(1)} %all-to-all-done.3.refs_0_.refs_1_, bf16[16,128,128]{2,1,0:T(8,128)(2,1)S(1)} %broadcast_in_dim.7.refs_2_), custom_call_target="tpu_custom_call", output_to_operand_aliasing={{}: (2, {})} | custom-call | flops 1 | bytes 1 | tf_op jit(solution)/shard_map/decode_and_requantize/pallas_call | solution.py:313
  67.1 0.0 copy-start
  67.1 0.0 copy-start.1
  67.2 0.0 copy-start.2
  67.2 24.4 %all-to-all-done.2.refs_0_.refs_1_ = bf16[8,1040,128]{2,1,0:T(8,128)(2,1)} async-done(((bf16[8,1040,128]{2,1,0:T(8,128)(2,1)}), bf16[8,1040,128]{2,1,0:T(8,128)(2,1)}, u32[]{:S(2)}, u32[]{:S(2)}) %all-to-all-start.2) | async-done | bytes 2129952 | tf_op jit(solution)/shard_map/all_to_all | solution.py:388
  91.6 6.2 %decode_and_requantize.3 = bf16[16,128,128]{2,1,0:T(8,128)(2,1)S(1)} custom-call(bf16[8,1040,128]{2,1,0:T(8,128)(2,1)} %all-to-all-done.2.refs_0_.refs_1_, bf16[8,1040,128]{2,1,0:T(8,128)(2,1)} %all-to-all-done.2.refs_0_.refs_1_, bf16[16,128,128]{2,1,0:T(8,128)(2,1)S(1)} %decode_and_requantize.2.refs_2_), custom_call_target="tpu_custom_call", output_to_operand_aliasing={{}: (2, {})} | custom-call | flops 1 | bytes 1 | tf_op jit(solution)/shard_map/decode_and_requantize/pallas_call | solution.py:313
  97.8 28.0 %all_to_all.24.refs_0_ = bf16[16,128,128]{2,1,0:T(8,128)(2,1)S(1)} all-to-all(bf16[16,128,128]{2,1,0:T(8,128)(2,1)S(1)} %decode_and_requantize.3), channel_id=1, replica_groups=mesh['group'=16,'chip'=8,'core'=2] {'group'}, dimensions={0} | all-to-all | bytes 1048576 | tf_op jit(solution)/shard_map/all_to_all | solution.py:391
  125.8 0.0 copy-done
  125.8 0.0 copy-done.1
  125.8 0.0 copy-done.2
  125.8 0.8 adamw_update.3
  126.6 0.7 while.13
  (1 shorter events, 0.0 us)
Async XLA Ops:
  11.5 4.3 %collective-permute-start.1 = (bf16[4,8,128,128]{3,2,1,0:T(8,128)(2,1)S(1)}, bf16[4,8,128,128]{3,2,1,0:T(8,128)(2,1)S(1)}, u32[]{:S(2)}, u32[]{:S(2)}) collective-permute-start(bf16[4,8,128,128]{3,2,1,0:T(8,128)(2,1)S(1)} %get-tuple-element.64), channel_id=1, source_target_pairs={{0,1},{1,0},{2,3},{3,2},{4,5},{5,4},{6,7},{7,6},{8,9},{9,8},{10,11... | collective-permute-start | bytes 3145736 | tf_op jit(solution)/shard_map/ppermute | solution.py:278
  11.6 4.2 %collective-permute-start.2 = (bf16[4,8,128,128]{3,2,1,0:T(8,128)(2,1)S(1)}, bf16[4,8,128,128]{3,2,1,0:T(8,128)(2,1)S(1)}, u32[]{:S(2)}, u32[]{:S(2)}) collective-permute-start(bf16[4,8,128,128]{3,2,1,0:T(8,128)(2,1)S(1)} %get-tuple-element.65), channel_id=1, source_target_pairs={{0,1},{1,0},{2,3},{3,2},{4,5},{5,4},{6,7},{7,6},{8,9},{9,8},{10,11... | collective-permute-start | bytes 3145736 | tf_op jit(solution)/shard_map/ppermute | solution.py:278
  12.1 3.7 %collective-permute-start = (f32[8,8,128]{2,1,0:T(8,128)S(1)}, f32[8,8,128]{2,1,0:T(8,128)S(1)}, u32[]{:S(2)}, u32[]{:S(2)}) collective-permute-start(f32[8,8,128]{2,1,0:T(8,128)S(1)} %get-tuple-element.63.refs_1_), channel_id=1, source_target_pairs={{0,1},{1,0},{2,3},{3,2},{4,5},{5,4},{6,7},{7,6},{8,9},{9,8},{10,11... | collective-permute-start | bytes 98312 | tf_op jit(solution)/shard_map/ppermute | solution.py:278
  20.6 35.6 %all-to-all-start.3 = ((bf16[8,1040,128]{2,1,0:T(8,128)(2,1)}), bf16[8,1040,128]{2,1,0:T(8,128)(2,1)S(1)}, u32[]{:S(2)}, u32[]{:S(2)}) async-start(bf16[8,1040,128]{2,1,0:T(8,128)(2,1)} %get-tuple-element.72), calls=%async_computation.3 | async-start | bytes 4259840 | tf_op jit(solution)/shard_map/all_to_all | solution.py:388
  37.3 4.3 %collective-permute-start.4 = (bf16[4,8,128,128]{3,2,1,0:T(8,128)(2,1)S(1)}, bf16[4,8,128,128]{3,2,1,0:T(8,128)(2,1)S(1)}, u32[]{:S(2)}, u32[]{:S(2)}) collective-permute-start(bf16[4,8,128,128]{3,2,1,0:T(8,128)(2,1)S(1)} %get-tuple-element.69), channel_id=1, source_target_pairs={{0,1},{1,0},{2,3},{3,2},{4,5},{5,4},{6,7},{7,6},{8,9},{9,8},{10,11... | collective-permute-start | bytes 3145736 | tf_op jit(solution)/shard_map/ppermute | solution.py:278
  37.4 4.2 %collective-permute-start.5 = (bf16[4,8,128,128]{3,2,1,0:T(8,128)(2,1)S(1)}, bf16[4,8,128,128]{3,2,1,0:T(8,128)(2,1)S(1)}, u32[]{:S(2)}, u32[]{:S(2)}) collective-permute-start(bf16[4,8,128,128]{3,2,1,0:T(8,128)(2,1)S(1)} %get-tuple-element.70), channel_id=1, source_target_pairs={{0,1},{1,0},{2,3},{3,2},{4,5},{5,4},{6,7},{7,6},{8,9},{9,8},{10,11... | collective-permute-start | bytes 3145736 | tf_op jit(solution)/shard_map/ppermute | solution.py:278
  37.9 3.7 %collective-permute-start.3 = (f32[8,8,128]{2,1,0:T(8,128)S(1)}, f32[8,8,128]{2,1,0:T(8,128)S(1)}, u32[]{:S(2)}, u32[]{:S(2)}) collective-permute-start(f32[8,8,128]{2,1,0:T(8,128)S(1)} %get-tuple-element.68.refs_1_), channel_id=1, source_target_pairs={{0,1},{1,0},{2,3},{3,2},{4,5},{5,4},{6,7},{7,6},{8,9},{9,8},{10,11... | collective-permute-start | bytes 98312 | tf_op jit(solution)/shard_map/ppermute | solution.py:278
  56.1 35.5 %all-to-all-start.2 = ((bf16[8,1040,128]{2,1,0:T(8,128)(2,1)}), bf16[8,1040,128]{2,1,0:T(8,128)(2,1)}, u32[]{:S(2)}, u32[]{:S(2)}) async-start(bf16[8,1040,128]{2,1,0:T(8,128)(2,1)} %get-tuple-element.71), calls=%async_computation.2 | async-start | bytes 4259840 | tf_op jit(solution)/shard_map/all_to_all | solution.py:388
  67.1 58.7 %copy-start = (f32[16384]{0:T(1024)S(1)}, f32[16384]{0:T(1024)}, u32[]{:S(2)}) copy-start(f32[16384]{0:T(1024)} %param.7) | copy-start | bytes 196612
  67.1 58.7 %copy-start.1 = (f32[16384]{0:T(1024)S(1)}, f32[16384]{0:T(1024)}, u32[]{:S(2)}) copy-start(f32[16384]{0:T(1024)} %param.8) | copy-start | bytes 196612
  67.2 58.7 %copy-start.2 = (f32[16384]{0:T(1024)S(1)}, f32[16384]{0:T(1024)}, u32[]{:S(2)}) copy-start(f32[16384]{0:T(1024)} %param.9) | copy-start | bytes 196612

commit v6 on v5

--- a/solution.py
+++ b/solution.py
@@ -11,6 +11,7 @@
 ROWS = BLOCK // LANES
 GROUP_ROWS = 8 * ROWS
 GROUP = GROUP_ROWS * LANES
+GROUP_AXES = ("group3", "group2", "group1", "group0")
 SEND_LANE = 64
 AUX_ROWS = 16
 
@@ -18,7 +19,7 @@
 STEPS = 72.0
 OFFSET = 113.0
 
-PARTS = (8, 8)
+PARTS = (4, 5, 7)
 PIECES = 2
 PARAMS = pltpu.CompilerParams(vmem_limit_bytes=48 << 20)
 PARAMS_Q = pltpu.CompilerParams(vmem_limit_bytes=48 << 20)
@@ -57,8 +58,8 @@
     for d, half, k in where:
         node = 2 * d + (core if half == 0 else 1 - core)
         at = pl.multiple_of((node * groups + k) * GROUP, GROUP)
-        rows = x_ref[0:1, pl.ds(at, GROUP)].astype(jnp.float32).reshape(GROUP_ROWS, LANES)
-        scratch[d, half * groups + k] = rows
+        rows = x_ref[0:1, pl.ds(at, GROUP)].reshape(GROUP_ROWS, LANES)
+        scratch[d, half * groups + k] = rows.astype(jnp.float32)
 
     def parts_of(d, half, k):
         return [scratch[d, half * groups + k, pl.ds(s, 8, stride=ROWS), :] for s in range(ROWS)]
@@ -144,29 +145,15 @@
         copy(g, slot).wait()
 
 
-def decode_kernel(
-    chips, groups, start, final, r_ref, aux_ref, before_ref, o_ref, buffer, units, spoilt, sems, bad
-):
-    del before_ref
-    g, count = pl.program_id(0), pl.num_programs(0)
-    slot = lax.rem(g, 2)
-
-    def copy(step, at):
-        return pltpu.make_async_copy(buffer.at[at], o_ref.at[step + start], sems.at[at])
-
-    @pl.when(g == 0)
-    def _():
-        total = jnp.zeros((8, LANES), jnp.float32)
-        for d in range(chips):
-            units[d] = aux_ref[d].astype(jnp.float32)[0:8]
-            total = total + units[d]
-        if final:
-            spoilt[0] = jnp.max(jnp.where(jnp.isnan(total), 1, 0)).astype(jnp.int32)
-
-    @pl.when(g >= 2)
-    def _():
-        copy(g - 2, slot).wait()
-
+def slot_of(group):
+    slot = 0
+    for _ in GROUP_AXES:
+        slot = 2 * slot + group % 2
+        group = group // 2
+    return slot
+
+
+def partial_sums(chips, groups, g, r_ref, units):
     rolled = [pltpu.roll(units[d], LANES - g * groups, 1) for d in range(chips)]
     for k in range(groups):
         at = slice(k * GROUP_ROWS, (k + 1) * GROUP_ROWS)
@@ -178,28 +165,73 @@
                 part = code[8 * s : 8 * s + 8]
                 size = jnp.floor(jnp.log2(jnp.abs(part)) * STEPS + (OFFSET * STEPS + 0.5))
                 total[s] = total[s] + size * jnp.where(part < 0, -unit, unit)
-        buffer[slot, at, :] = jnp.concatenate(requantized(total), axis=0).astype(jnp.bfloat16)
+        yield at, jnp.concatenate(requantized(total), axis=0).astype(jnp.bfloat16)
+
+
+def decode_kernel(chips, groups, r_ref, aux_ref, o_ref, units):
+    g = pl.program_id(0)
+
+    @pl.when(g == 0)
+    def _():
+        for d in range(chips):
+            units[d] = aux_ref[d].astype(jnp.float32)[0:8]
+
+    for at, done in partial_sums(chips, groups, g, r_ref, units):
+        o_ref[0, at, :] = done
+
+
+def last_decode_kernel(chips, groups, count, r_ref, aux_ref, *refs):
+    *earlier, o_ref, buffer, units, spoilt, sems, early_sems = refs
+    g = pl.program_id(0)
+    slot = lax.rem(g, 2)
+    start = o_ref.shape[0] - count
+    blocks = [e.at[i] for e in earlier for i in range(e.shape[0])]
+
+    def copy(step, at):
+        return pltpu.make_async_copy(buffer.at[at], o_ref.at[slot_of(step + start)], sems.at[at])
+
+    early = [
+        pltpu.make_async_copy(block, o_ref.at[slot_of(i)], early_sems.at[i])
+        for i, block in enumerate(blocks)
+    ]
+
+    @pl.when(g == 0)
+    def _():
+        for one in early:
+            one.start()
+        total = jnp.zeros((8, LANES), jnp.float32)
+        for d in range(chips):
+            units[d] = aux_ref[d].astype(jnp.float32)[0:8]
+            total = total + units[d]
+        spoilt[0] = jnp.max(jnp.where(jnp.isnan(total), 1, 0)).astype(jnp.int32)
+
+    @pl.when(g >= 2)
+    def _():
+        copy(g - 2, slot).wait()
+
+    for at, done in partial_sums(chips, groups, g, r_ref, units):
+        buffer[slot, at, :] = done
     copy(g, slot).start()
 
     @pl.when(g == count - 1)
     def _():
-        @pl.when(count >= 2)
+        if count >= 2:
+            copy(g - 1, 1 - slot).wait()
+        copy(g, slot).wait()
+        for one in early:
+            one.wait()
+
+        @pl.when(spoilt[0] > 0)
         def _():
-            copy(g - 1, 1 - slot).wait()
-
-        copy(g, slot).wait()
-        if final:
-            @pl.when(spoilt[0] > 0)
-            def _():
-                buffer[0] = jnp.full(buffer.shape[1:], jnp.nan, jnp.bfloat16)
-
-                def spoil(j, carry):
-                    one = pltpu.make_async_copy(buffer.at[0], o_ref.at[j], bad)
-                    one.start()
-                    one.wait()
-                    return carry
-
-                lax.fori_loop(0, o_ref.shape[0], spoil, 0)
+            buffer[0] = jnp.full(buffer.shape[1:], jnp.nan, jnp.bfloat16)
+
+            def spoil(j, carry):
+                one = pltpu.make_async_copy(buffer.at[0], o_ref.at[j], sems.at[0])
+                one.start()
+                one.wait()
+                return carry
+
+            lax.fori_loop(0, o_ref.shape[0], spoil, 0)
 
 
 def first_kernel(nodes, groups, after_ref, x_ref, o_ref, scratch):
@@ -208,7 +240,7 @@
     def step(n, carry):
         for k in range(groups):
             at = pl.multiple_of((n * groups + k) * GROUP, GROUP)
-            scratch[k] = x_ref[0:1, pl.ds(at, GROUP)].astype(jnp.float32).reshape(GROUP_ROWS, LANES)
+            scratch[k] = x_ref[0:1, pl.ds(at, GROUP)].reshape(GROUP_ROWS, LANES).astype(jnp.float32)
         for k in range(groups):
             parts = [scratch[k, pl.ds(s, 8, stride=ROWS), :] for s in range(ROWS)]
             done = jnp.concatenate(requantized(parts), axis=0)
@@ -308,30 +340,43 @@
     )(own, scales, peer_scales, before, *peer)
 
 
-def node_sums(received, partial, start, count, chips, final):
-    rows = partial.shape[1]
+def node_sums(received, count, chips, rows, earlier=None):
+    groups = rows // GROUP_ROWS
+    in_specs = [
+        pl.BlockSpec((chips, rows, LANES), lambda g: (0, g, 0)),
+        pl.BlockSpec((chips, AUX_ROWS, LANES), lambda g: (0, count * rows // AUX_ROWS, 0)),
+    ]
+    units = pltpu.VMEM((chips, 8, LANES), jnp.float32)
+    if earlier is None:
+        return pl.pallas_call(
+            lambda *refs: decode_kernel(chips, groups, *refs),
+            name="decode_and_requantize",
+            grid=(count,),
+            in_specs=in_specs,
+            out_specs=pl.BlockSpec((1, rows, LANES), lambda g: (g, 0, 0)),
+            out_shape=jax.ShapeDtypeStruct((count, rows, LANES), jnp.bfloat16),
+            scratch_shapes=[units],
+            compiler_params=PARAMS,
+            cost_estimate=COST,
+        )(received, received)
+    replicas = count + sum(e.shape[0] for e in earlier)
     return pl.pallas_call(
-        lambda *refs: decode_kernel(chips, rows // GROUP_ROWS, start, final, *refs),
-        name="decode_and_requantize",
+        lambda *refs: last_decode_kernel(chips, groups, count, *refs),
+        name="last_decode_and_requantize",
         grid=(count,),
-        in_specs=[
-            pl.BlockSpec((chips, rows, LANES), lambda g: (0, g, 0)),
-            pl.BlockSpec((chips, AUX_ROWS, LANES), lambda g: (0, count * rows // AUX_ROWS, 0)),
-            pl.BlockSpec(memory_space=pl.ANY),
-        ],
+        in_specs=in_specs + [pl.BlockSpec(memory_space=pl.ANY)] * len(earlier),
         out_specs=pl.BlockSpec(memory_space=pl.ANY),
-        out_shape=jax.ShapeDtypeStruct(partial.shape, partial.dtype),
+        out_shape=jax.ShapeDtypeStruct((replicas, rows, LANES), jnp.bfloat16),
         scratch_shapes=[
             pltpu.VMEM((2, rows, LANES), jnp.bfloat16),
-            pltpu.VMEM((chips, 8, LANES), jnp.float32),
+            units,
             pltpu.SMEM((1,), jnp.int32),
             pltpu.SemaphoreType.DMA((2,)),
-            pltpu.SemaphoreType.DMA,
+            pltpu.SemaphoreType.DMA((replicas - count,)),
         ],
-        input_output_aliases={2: 0},
         compiler_params=PARAMS,
         cost_estimate=COST,
-    )(received, received, partial)
+    )(received, received, *earlier)
 
 
 def plain_sums(grads, after, replicas, nodes, shard):
@@ -359,7 +404,7 @@
         out_shape=jax.ShapeDtypeStruct((replicas, rows, LANES), jnp.bfloat16),
         compiler_params=PARAMS,
     )(received)
-    return lax.all_to_all(partial, "group", split_axis=0, concat_axis=0, tiled=True)
+    return lax.all_to_all(partial, GROUP_AXES, split_axis=0, concat_axis=0, tiled=True)
 
 
 def update(owned, master, moment, second):
@@ -377,18 +422,20 @@
 
 
 def body(grads, master, moment, second):
-    replicas = lax.axis_size("group")
+    replicas = lax.axis_size(GROUP_AXES)
     chips = lax.axis_size("chip")
     shard = master.shape[0]
     flag = jnp.zeros((8, LANES), jnp.float32)
-    partial = jnp.zeros((replicas, shard // LANES, LANES), jnp.bfloat16)
-    start = 0
+    rows = shard // LANES
+    partials, start = [], 0
     for count in PARTS:
         message, flag = pair_sums(*quantized(grads, flag, start, count, chips, shard), flag)
         received = lax.all_to_all(message, "chip", split_axis=0, concat_axis=0, tiled=True)
-        partial = node_sums(received, partial, start, count, chips, start + count == replicas)
         start += count
-    owned = lax.all_to_all(partial, "group", split_axis=0, concat_axis=0, tiled=True)
+        earlier = partials if start == replicas else None
+        partial = node_sums(received, count, chips, rows, earlier)
+        partials.append(partial)
+    owned = lax.all_to_all(partials[-1], GROUP_AXES[::-1], split_axis=0, concat_axis=0, tiled=True)
     state = [a.reshape(shard // LANES, LANES) for a in (master, moment, second)]
 
     def general(carry):
@@ -400,10 +447,11 @@
 
 
 def solution(mesh):
-    groups, nodes = mesh.devices.shape
-    cores = Mesh(mesh.devices.reshape(groups, nodes // 2, 2), ("group", "chip", "core"))
-    split = P(("group", "chip", "core"))
-    in_specs = (P(("group", "chip", "core"), None), split, split, split)
+    nodes = mesh.devices.shape[1]
+    axes = (*GROUP_AXES, "chip", "core")
+    cores = Mesh(mesh.devices.reshape(*[2] * len(GROUP_AXES), nodes // 2, 2), axes)
+    split = P(axes)
+    in_specs = (P(axes, None), split, split, split)
     return jax.shard_map(
         body, mesh=cores, in_specs=in_specs, out_specs=(split, split, split), check_vma=False
     )

time: 128 us -> 117 us (0.914)
  Pallas kernels: 42.8 us -> 33.5 us
  waiting for transfers between devices: 40.8 us -> 32.5 us
  starting transfers between devices: 14.2 us -> 18.7 us
  local copies, waits for them, and re-layouts: 0.12 us -> 3.59 us
  blocking collectives: 28 us -> 26.5 us
    all_to_all x2 -> x3, waiting for transfers between devices: 33.6 us -> 24.7 us  [body(): lax.all_to_all(message, 'chip', split_axis=0, concat_axis=0, tiled=True)]
    pallas_call x2 -> x3, Pallas kernels: 21.8 us -> 16.2 us  [quantized(): pl.pallas_call(lambda *refs: pair_kernel(chips, groups, *refs), name='qua...]
    all_to_all x2 -> x3, starting transfers between devices: 12.8 us -> 16.6 us  [body(): lax.all_to_all(message, 'chip', split_axis=0, concat_axis=0, tiled=True)]
    unnamed x6 -> x14, local copies, waits for them, and re-layouts: 0.02 us -> 3.59 us
    pallas_call x2 -> x3, Pallas kernels: 10.2 us -> 8.2 us  [the longest x1 4.13 us: node_sums(): pl.pallas_call(lambda *refs: last_decode_kernel(chips, groups, count, *re...]
    pallas_call x2 -> x3, Pallas kernels: 10 us -> 8.33 us  [pair_sums(): pl.pallas_call(lambda *refs: encode_kernel(chips, rows // GROUP_ROWS, cou...]
    all_to_all x1, blocking collectives: 28 us -> 26.5 us  [body(): lax.all_to_all(partials[-1], GROUP_AXES[::-1], split_axis=0, concat_axis=...]
    ppermute x6 -> x9, waiting for transfers between devices: 7.2 us -> 7.76 us  [quantized(): lax.ppermute(a, 'core', [(0, 1), (1, 0)])]
  transfers between devices with their start and end apart: 8 -> 12, of which waited for: 4 -> 6; matrix products, arithmetic and copies ran while one was open for 0% -> 0% of each run, Pallas kernels for 16% -> 19%
where the time goes in v6:
time: 117 us; the launch traced here: 116 us
  Pallas kernels  33.5 us (29%)
  waiting for transfers between devices  32.5 us (28%)
  blocking collectives  26.5 us (23%)
  starting transfers between devices  18.7 us (16%)
  local copies, waits for them, and re-layouts  3.59 us (3%)
    all_to_all x1, blocking collectives, body(): lax.all_to_all(partials[-1], GROUP_AXES[::-1], split_axis=0, concat_axis=...  26.5 us
    all_to_all x3, waiting for transfers between devices, body(): lax.all_to_all(message, 'chip', split_axis=0, concat_axis=0, tiled=True)  24.7 us
    all_to_all x3, starting transfers between devices, body(): lax.all_to_all(message, 'chip', split_axis=0, concat_axis=0, tiled=True)  16.6 us
    pallas_call x3, Pallas kernels, quantized(): pl.pallas_call(lambda *refs: pair_kernel(chips, groups, *refs), name='qua...  16.2 us
    pallas_call x3, Pallas kernels, pair_sums(): pl.pallas_call(lambda *refs: encode_kernel(chips, rows // GROUP_ROWS, cou...  8.33 us
    ppermute x9, waiting for transfers between devices, quantized(): lax.ppermute(a, 'core', [(0, 1), (1, 0)])  7.76 us
    pallas_call x1, Pallas kernels, node_sums(): pl.pallas_call(lambda *refs: last_decode_kernel(chips, groups, count, *re...  4.13 us
    pallas_call x2, Pallas kernels, node_sums(): pl.pallas_call(lambda *refs: decode_kernel(chips, groups, *refs), name='d...  4.07 us
  transfers between devices with their start and end apart: 12, of which 6 were waited for; matrix products, arithmetic and copies ran while one was open for 0% of the time, Pallas kernels for 19%

profile of v6, /device:TPU:2, one launch (start us, length us, event | category | flops | bytes accessed | tf_op | source)
XLA Modules:
  0.0 116.1 jit_solution(6547200845896076799)
XLA Ops:
  0.6 4.0 %quantize.3 = (bf16[8,4,128,128]{3,2,1,0:T(8,128)(2,1)S(1)}, bf16[4,4,128,128]{3,2,1,0:T(8,128)(2,1)S(1)}, bf16[4,4,128,128]{3,2,1,0:T(8,128)(2,1)S(1)}, f32[4,8,128]{2,1,0:T(8,128)S(1)}) custom-call(s32[1]{0:T(128)} %bitcast.1.refs_0_, bf16[1,4194304]{1,0:T(2,128)(2,1)} %refs_1_.5, f32[8,128]{1,0:T(8,128)S(1)} %broadcast_in_dim.3.refs_2_.refs_3_), custom_call_target="tpu_custom_call" | custom-call | flops 1 | bytes 1 | tf_op jit(solution)/shard_map/quantize/pallas_call | solution.py:295
  4.7 0.1 collective-permute-start.1
  4.8 0.5 collective-permute-start.2
  5.3 0.1 collective-permute-start
  5.4 2.1 %collective-permute-done.refs_2_ = f32[4,8,128]{2,1,0:T(8,128)S(1)} collective-permute-done((f32[4,8,128]{2,1,0:T(8,128)S(1)}, f32[4,8,128]{2,1,0:T(8,128)S(1)}, u32[]{:S(2)}, u32[]{:S(2)}) %collective-permute-start) | collective-permute-done | bytes 16416 | tf_op jit(solution)/shard_map/ppermute | solution.py:310
  7.5 0.0 collective-permute-done.1.refs_4_
  7.5 0.0 collective-permute-done.2.refs_5_
  7.5 2.6 %add_and_encode.3 = (bf16[8,528,128]{2,1,0:T(8,128)(2,1)}, f32[8,128]{1,0:T(8,128)S(1)}) custom-call(bf16[8,4,128,128]{3,2,1,0:T(8,128)(2,1)S(1)} %get-tuple-element.68.refs_0_, f32[4,8,128]{2,1,0:T(8,128)S(1)} %get-tuple-element.69.refs_1_, f32[4,8,128]{2,1,0:T(8,128)S(1)} %collective-permute-done.refs_2_, f32[8,128]{1,0:T(8,128)S(1)} %broadcast_in_dim.3.refs_2_.refs_3_, ...), custom_call_target="tpu_custom_call" | custom-call | flops 1 | bytes 1 | tf_op jit(solution)/shard_map/add_and_encode/pallas_call | solution.py:321
  10.1 5.9 %all-to-all-start.3 = ((bf16[8,528,128]{2,1,0:T(8,128)(2,1)}), bf16[8,528,128]{2,1,0:T(8,128)(2,1)S(1)}, u32[]{:S(2)}, u32[]{:S(2)}) async-start(bf16[8,528,128]{2,1,0:T(8,128)(2,1)} %get-tuple-element.83), calls=%async_computation.3 | async-start | bytes 2162688 | tf_op jit(solution)/shard_map/all_to_all | solution.py:433
  15.9 5.2 %quantize.4 = (bf16[8,5,128,128]{3,2,1,0:T(8,128)(2,1)S(1)}, bf16[4,5,128,128]{3,2,1,0:T(8,128)(2,1)S(1)}, bf16[4,5,128,128]{3,2,1,0:T(8,128)(2,1)S(1)}, f32[5,8,128]{2,1,0:T(8,128)S(1)}) custom-call(s32[1]{0:T(128)} %bitcast.1.refs_0_, bf16[1,4194304]{1,0:T(2,128)(2,1)} %refs_1_.5, f32[8,128]{1,0:T(8,128)S(1)} %get-tuple-element.72.refs_2_.refs_3_), custom_call_target="tpu_custom_call" | custom-call | flops 1 | bytes 1 | tf_op jit(solution)/shard_map/quantize/pallas_call | solution.py:295
  21.1 0.1 collective-permute-start.4
  21.2 0.5 collective-permute-start.5
  21.7 0.1 collective-permute-start.3
  21.8 2.5 %collective-permute-done.3.refs_2_ = f32[5,8,128]{2,1,0:T(8,128)S(1)} collective-permute-done((f32[5,8,128]{2,1,0:T(8,128)S(1)}, f32[5,8,128]{2,1,0:T(8,128)S(1)}, u32[]{:S(2)}, u32[]{:S(2)}) %collective-permute-start.3) | collective-permute-done | bytes 20512 | tf_op jit(solution)/shard_map/ppermute | solution.py:310
  24.3 0.0 collective-permute-done.4.refs_4_
  24.3 0.0 collective-permute-done.5.refs_5_
  24.3 2.2 %add_and_encode.4 = (bf16[8,656,128]{2,1,0:T(8,128)(2,1)S(1)}, f32[8,128]{1,0:T(8,128)S(1)}) custom-call(bf16[8,5,128,128]{3,2,1,0:T(8,128)(2,1)S(1)} %get-tuple-element.73.refs_0_, f32[5,8,128]{2,1,0:T(8,128)S(1)} %get-tuple-element.74.refs_1_, f32[5,8,128]{2,1,0:T(8,128)S(1)} %collective-permute-done.3.refs_2_, ...), custom_call_target="tpu_custom_call" | custom-call | flops 1 | bytes 1 | tf_op jit(solution)/shard_map/add_and_encode/pallas_call | solution.py:321
  26.5 0.0 copy-start.3
  26.5 1.1 copy-done.3
  27.5 4.0 %all-to-all-done.3.refs_0_.refs_1_ = bf16[8,528,128]{2,1,0:T(8,128)(2,1)S(1)} async-done(((bf16[8,528,128]{2,1,0:T(8,128)(2,1)}), bf16[8,528,128]{2,1,0:T(8,128)(2,1)S(1)}, u32[]{:S(2)}, u32[]{:S(2)}) %all-to-all-start.3) | async-done | bytes 1081376 | tf_op jit(solution)/shard_map/all_to_all | solution.py:433
  31.5 0.0 copy-start
  31.5 5.4 %all-to-all-start.4 = ((bf16[8,656,128]{2,1,0:T(8,128)(2,1)}), bf16[8,656,128]{2,1,0:T(8,128)(2,1)S(1)}, u32[]{:S(2)}, u32[]{:S(2)}) async-start(bf16[8,656,128]{2,1,0:T(8,128)(2,1)} %copy-done.3), calls=%async_computation.4 | async-start | bytes 2686976 | tf_op jit(solution)/shard_map/all_to_all | solution.py:433
  36.9 6.9 %quantize.5 = (bf16[8,7,128,128]{3,2,1,0:T(8,128)(2,1)S(1)}, bf16[4,7,128,128]{3,2,1,0:T(8,128)(2,1)S(1)}, bf16[4,7,128,128]{3,2,1,0:T(8,128)(2,1)S(1)}, f32[7,8,128]{2,1,0:T(8,128)S(1)}) custom-call(s32[1]{0:T(128)} %bitcast.1.refs_0_, bf16[1,4194304]{1,0:T(2,128)(2,1)} %refs_1_.5, f32[8,128]{1,0:T(8,128)S(1)} %get-tuple-element.77.refs_2_.refs_3_), custom_call_target="tpu_custom_call" | custom-call | flops 1 | bytes 1 | tf_op jit(solution)/shard_map/quantize/pallas_call | solution.py:295
  43.8 0.0 copy-done
  43.8 0.1 collective-permute-start.7
  43.9 0.5 collective-permute-start.8
  44.4 0.1 collective-permute-start.6
  44.5 3.2 %collective-permute-done.6.refs_2_ = f32[7,8,128]{2,1,0:T(8,128)S(1)} collective-permute-done((f32[7,8,128]{2,1,0:T(8,128)S(1)}, f32[7,8,128]{2,1,0:T(8,128)S(1)}, u32[]{:S(2)}, u32[]{:S(2)}) %collective-permute-start.6) | collective-permute-done | bytes 28704 | tf_op jit(solution)/shard_map/ppermute | solution.py:310
  47.7 0.0 collective-permute-done.7.refs_4_
  47.7 0.0 collective-permute-done.8.refs_5_
  47.7 3.6 %add_and_encode.5 = (bf16[8,912,128]{2,1,0:T(8,128)(2,1)S(1)}, f32[8,128]{1,0:T(8,128)}) custom-call(bf16[8,7,128,128]{3,2,1,0:T(8,128)(2,1)S(1)} %get-tuple-element.78.refs_0_, f32[7,8,128]{2,1,0:T(8,128)S(1)} %get-tuple-element.79.refs_1_, f32[7,8,128]{2,1,0:T(8,128)S(1)} %collective-permute-done.6.refs_2_, ...), custom_call_target="tpu_custom_call" | custom-call | flops 1 | bytes 1 | tf_op jit(solution)/shard_map/add_and_encode/pallas_call | solution.py:321
  51.3 0.0 copy-start.2
  51.3 1.3 %copy-done.2 = bf16[8,912,128]{2,1,0:T(8,128)(2,1)} copy-done((bf16[8,912,128]{2,1,0:T(8,128)(2,1)}, bf16[8,912,128]{2,1,0:T(8,128)(2,1)S(1)}, u32[]{:S(2)}) %copy-start.2) | copy-done | bytes 1867800
  52.6 2.0 %all-to-all-done.4.refs_0_.refs_1_ = bf16[8,656,128]{2,1,0:T(8,128)(2,1)S(1)} async-done(((bf16[8,656,128]{2,1,0:T(8,128)(2,1)}), bf16[8,656,128]{2,1,0:T(8,128)(2,1)S(1)}, u32[]{:S(2)}, u32[]{:S(2)}) %all-to-all-start.4) | async-done | bytes 1343520 | tf_op jit(solution)/shard_map/all_to_all | solution.py:433
  54.6 5.4 %all-to-all-start.2 = ((bf16[8,912,128]{2,1,0:T(8,128)(2,1)}), bf16[8,912,128]{2,1,0:T(8,128)(2,1)S(1)}, u32[]{:S(2)}, u32[]{:S(2)}) async-start(bf16[8,912,128]{2,1,0:T(8,128)(2,1)} %copy-done.2), calls=%async_computation.2 | async-start | bytes 3735552 | tf_op jit(solution)/shard_map/all_to_all | solution.py:433
  60.0 0.0 copy-start.1
  60.0 1.2 %copy-done.1 = bf16[8,528,128]{2,1,0:T(8,128)(2,1)S(1)} copy-done((bf16[8,528,128]{2,1,0:T(8,128)(2,1)S(1)}, bf16[8,528,128]{2,1,0:T(8,128)(2,1)}, u32[]{:S(2)}) %copy-start.1) | copy-done | bytes 1081368
  61.2 1.8 %decode_and_requantize.2.refs_2_ = bf16[4,128,128]{2,1,0:T(8,128)(2,1)S(1)} custom-call(bf16[8,528,128]{2,1,0:T(8,128)(2,1)S(1)} %copy-done.1, bf16[8,528,128]{2,1,0:T(8,128)(2,1)S(1)} %copy-done.1), custom_call_target="tpu_custom_call" | custom-call | flops 1 | bytes 1 | tf_op jit(solution)/shard_map/decode_and_requantize/pallas_call | solution.py:351
  63.0 2.3 %decode_and_requantize.3.refs_3_ = bf16[5,128,128]{2,1,0:T(8,128)(2,1)S(1)} custom-call(bf16[8,656,128]{2,1,0:T(8,128)(2,1)S(1)} %all-to-all-done.4.refs_0_.refs_1_, bf16[8,656,128]{2,1,0:T(8,128)(2,1)S(1)} %all-to-all-done.4.refs_0_.refs_1_), custom_call_target="tpu_custom_call" | custom-call | flops 1 | bytes 1 | tf_op jit(solution)/shard_map/decode_and_requantize/pallas_call | solution.py:351
  65.3 0.0 copy-start.4
  65.3 0.0 copy-start.5
  65.3 0.0 copy-start.6
  65.3 18.7 %all-to-all-done.2.refs_0_.refs_1_ = bf16[8,912,128]{2,1,0:T(8,128)(2,1)S(1)} async-done(((bf16[8,912,128]{2,1,0:T(8,128)(2,1)}), bf16[8,912,128]{2,1,0:T(8,128)(2,1)S(1)}, u32[]{:S(2)}, u32[]{:S(2)}) %all-to-all-start.2) | async-done | bytes 1867808 | tf_op jit(solution)/shard_map/all_to_all | solution.py:433
  84.1 4.1 %last_decode_and_requantize.1 = bf16[16,128,128]{2,1,0:T(8,128)(2,1)S(1)} custom-call(bf16[8,912,128]{2,1,0:T(8,128)(2,1)S(1)} %all-to-all-done.2.refs_0_.refs_1_, bf16[8,912,128]{2,1,0:T(8,128)(2,1)S(1)} %all-to-all-done.2.refs_0_.refs_1_, bf16[4,128,128]{2,1,0:T(8,128)(2,1)S(1)} %decode_and_requantize.2.refs_2_, ...), custom_call_target="tpu_custom_call" | custom-call | flops 1 | bytes 1 | tf_op jit(solution)/shard_map/last_decode_and_requantize/pallas_call | solution.py:363
  88.2 26.5 %all_to_all.29.refs_0_ = bf16[16,128,128]{2,1,0:T(8,128)(2,1)S(1)} all-to-all(bf16[16,128,128]{2,1,0:T(8,128)(2,1)S(1)} %last_decode_and_requantize.1), channel_id=1, replica_groups=mesh['group3'=2,'group2'=2,'group1'=2,'group0'=2,'chip'=8,'core'=2] {'gr..., dimensions={0} | all-to-all | bytes 1048576 | tf_op jit(solution)/shard_map/all_to_all | solution.py:438
  114.7 0.0 copy-done.4
  114.7 0.0 copy-done.5
  114.7 0.0 copy-done.6
  114.7 0.8 adamw_update.3
  115.5 0.6 while.13
  (1 shorter events, 0.0 us)
Async XLA Ops:
  4.7 2.8 %collective-permute-start.1 = (bf16[4,4,128,128]{3,2,1,0:T(8,128)(2,1)S(1)}, bf16[4,4,128,128]{3,2,1,0:T(8,128)(2,1)S(1)}, u32[]{:S(2)}, u32[]{:S(2)}) collective-permute-start(bf16[4,4,128,128]{3,2,1,0:T(8,128)(2,1)S(1)} %get-tuple-element.70), channel_id=1, source_target_pairs={{0,1},{1,0},{2,3},{3,2},{4,5},{5,4},{6,7},{7,6},{8,9},{9,8},{10,11... | collective-permute-start | bytes 1572872 | tf_op jit(solution)/shard_map/ppermute | solution.py:310
  4.8 2.7 %collective-permute-start.2 = (bf16[4,4,128,128]{3,2,1,0:T(8,128)(2,1)S(1)}, bf16[4,4,128,128]{3,2,1,0:T(8,128)(2,1)S(1)}, u32[]{:S(2)}, u32[]{:S(2)}) collective-permute-start(bf16[4,4,128,128]{3,2,1,0:T(8,128)(2,1)S(1)} %get-tuple-element.71), channel_id=1, source_target_pairs={{0,1},{1,0},{2,3},{3,2},{4,5},{5,4},{6,7},{7,6},{8,9},{9,8},{10,11... | collective-permute-start | bytes 1572872 | tf_op jit(solution)/shard_map/ppermute | solution.py:310
  5.3 2.2 %collective-permute-start = (f32[4,8,128]{2,1,0:T(8,128)S(1)}, f32[4,8,128]{2,1,0:T(8,128)S(1)}, u32[]{:S(2)}, u32[]{:S(2)}) collective-permute-start(f32[4,8,128]{2,1,0:T(8,128)S(1)} %get-tuple-element.69.refs_1_), channel_id=1, source_target_pairs={{0,1},{1,0},{2,3},{3,2},{4,5},{5,4},{6,7},{7,6},{8,9},{9,8},{10,11... | collective-permute-start | bytes 49160 | tf_op jit(solution)/shard_map/ppermute | solution.py:310
  10.1 21.4 %all-to-all-start.3 = ((bf16[8,528,128]{2,1,0:T(8,128)(2,1)}), bf16[8,528,128]{2,1,0:T(8,128)(2,1)S(1)}, u32[]{:S(2)}, u32[]{:S(2)}) async-start(bf16[8,528,128]{2,1,0:T(8,128)(2,1)} %get-tuple-element.83), calls=%async_computation.3 | async-start | bytes 2162688 | tf_op jit(solution)/shard_map/all_to_all | solution.py:433
  21.1 3.2 %collective-permute-start.4 = (bf16[4,5,128,128]{3,2,1,0:T(8,128)(2,1)S(1)}, bf16[4,5,128,128]{3,2,1,0:T(8,128)(2,1)S(1)}, u32[]{:S(2)}, u32[]{:S(2)}) collective-permute-start(bf16[4,5,128,128]{3,2,1,0:T(8,128)(2,1)S(1)} %get-tuple-element.75), channel_id=1, source_target_pairs={{0,1},{1,0},{2,3},{3,2},{4,5},{5,4},{6,7},{7,6},{8,9},{9,8},{10,11... | collective-permute-start | bytes 1966088 | tf_op jit(solution)/shard_map/ppermute | solution.py:310
  21.2 3.1 %collective-permute-start.5 = (bf16[4,5,128,128]{3,2,1,0:T(8,128)(2,1)S(1)}, bf16[4,5,128,128]{3,2,1,0:T(8,128)(2,1)S(1)}, u32[]{:S(2)}, u32[]{:S(2)}) collective-permute-start(bf16[4,5,128,128]{3,2,1,0:T(8,128)(2,1)S(1)} %get-tuple-element.76), channel_id=1, source_target_pairs={{0,1},{1,0},{2,3},{3,2},{4,5},{5,4},{6,7},{7,6},{8,9},{9,8},{10,11... | collective-permute-start | bytes 1966088 | tf_op jit(solution)/shard_map/ppermute | solution.py:310
  21.7 2.6 %collective-permute-start.3 = (f32[5,8,128]{2,1,0:T(8,128)S(1)}, f32[5,8,128]{2,1,0:T(8,128)S(1)}, u32[]{:S(2)}, u32[]{:S(2)}) collective-permute-start(f32[5,8,128]{2,1,0:T(8,128)S(1)} %get-tuple-element.74.refs_1_), channel_id=1, source_target_pairs={{0,1},{1,0},{2,3},{3,2},{4,5},{5,4},{6,7},{7,6},{8,9},{9,8},{10,11... | collective-permute-start | bytes 61448 | tf_op jit(solution)/shard_map/ppermute | solution.py:310
  26.5 1.1 copy-start.3
  31.5 12.3 %copy-start = (bf16[8,528,128]{2,1,0:T(8,128)(2,1)}, bf16[8,528,128]{2,1,0:T(8,128)(2,1)S(1)}, u32[]{:S(2)}) copy-start(bf16[8,528,128]{2,1,0:T(8,128)(2,1)S(1)} %all-to-all-done.3.refs_0_.refs_1_) | copy-start | bytes 3244036
  31.5 23.1 %all-to-all-start.4 = ((bf16[8,656,128]{2,1,0:T(8,128)(2,1)}), bf16[8,656,128]{2,1,0:T(8,128)(2,1)S(1)}, u32[]{:S(2)}, u32[]{:S(2)}) async-start(bf16[8,656,128]{2,1,0:T(8,128)(2,1)} %copy-done.3), calls=%async_computation.4 | async-start | bytes 2686976 | tf_op jit(solution)/shard_map/all_to_all | solution.py:433
  43.8 3.9 %collective-permute-start.7 = (bf16[4,7,128,128]{3,2,1,0:T(8,128)(2,1)S(1)}, bf16[4,7,128,128]{3,2,1,0:T(8,128)(2,1)S(1)}, u32[]{:S(2)}, u32[]{:S(2)}) collective-permute-start(bf16[4,7,128,128]{3,2,1,0:T(8,128)(2,1)S(1)} %get-tuple-element.80), channel_id=1, source_target_pairs={{0,1},{1,0},{2,3},{3,2},{4,5},{5,4},{6,7},{7,6},{8,9},{9,8},{10,11... | collective-permute-start | bytes 2752520 | tf_op jit(solution)/shard_map/ppermute | solution.py:310
  43.9 3.8 %collective-permute-start.8 = (bf16[4,7,128,128]{3,2,1,0:T(8,128)(2,1)S(1)}, bf16[4,7,128,128]{3,2,1,0:T(8,128)(2,1)S(1)}, u32[]{:S(2)}, u32[]{:S(2)}) collective-permute-start(bf16[4,7,128,128]{3,2,1,0:T(8,128)(2,1)S(1)} %get-tuple-element.81), channel_id=1, source_target_pairs={{0,1},{1,0},{2,3},{3,2},{4,5},{5,4},{6,7},{7,6},{8,9},{9,8},{10,11... | collective-permute-start | bytes 2752520 | tf_op jit(solution)/shard_map/ppermute | solution.py:310
  44.4 3.3 %collective-permute-start.6 = (f32[7,8,128]{2,1,0:T(8,128)S(1)}, f32[7,8,128]{2,1,0:T(8,128)S(1)}, u32[]{:S(2)}, u32[]{:S(2)}) collective-permute-start(f32[7,8,128]{2,1,0:T(8,128)S(1)} %get-tuple-element.79.refs_1_), channel_id=1, source_target_pairs={{0,1},{1,0},{2,3},{3,2},{4,5},{5,4},{6,7},{7,6},{8,9},{9,8},{10,11... | collective-permute-start | bytes 86024 | tf_op jit(solution)/shard_map/ppermute | solution.py:310
  51.3 1.3 %copy-start.2 = (bf16[8,912,128]{2,1,0:T(8,128)(2,1)}, bf16[8,912,128]{2,1,0:T(8,128)(2,1)S(1)}, u32[]{:S(2)}) copy-start(bf16[8,912,128]{2,1,0:T(8,128)(2,1)S(1)} %get-tuple-element.82) | copy-start | bytes 5603332
  54.6 29.5 %all-to-all-start.2 = ((bf16[8,912,128]{2,1,0:T(8,128)(2,1)}), bf16[8,912,128]{2,1,0:T(8,128)(2,1)S(1)}, u32[]{:S(2)}, u32[]{:S(2)}) async-start(bf16[8,912,128]{2,1,0:T(8,128)(2,1)} %copy-done.2), calls=%async_computation.2 | async-start | bytes 3735552 | tf_op jit(solution)/shard_map/all_to_all | solution.py:433
  60.0 1.2 %copy-start.1 = (bf16[8,528,128]{2,1,0:T(8,128)(2,1)S(1)}, bf16[8,528,128]{2,1,0:T(8,128)(2,1)}, u32[]{:S(2)}) copy-start(bf16[8,528,128]{2,1,0:T(8,128)(2,1)} %copy-done) | copy-start | bytes 3244036
  65.3 49.4 %copy-start.4 = (f32[16384]{0:T(1024)S(1)}, f32[16384]{0:T(1024)}, u32[]{:S(2)}) copy-start(f32[16384]{0:T(1024)} %param.7) | copy-start | bytes 196612
  65.3 49.4 %copy-start.5 = (f32[16384]{0:T(1024)S(1)}, f32[16384]{0:T(1024)}, u32[]{:S(2)}) copy-start(f32[16384]{0:T(1024)} %param.8) | copy-start | bytes 196612
  65.3 49.4 %copy-start.6 = (f32[16384]{0:T(1024)S(1)}, f32[16384]{0:T(1024)}, u32[]{:S(2)}) copy-start(f32[16384]{0:T(1024)} %param.9) | copy-start | bytes 196612

commit v7 on v6

--- a/solution.py
+++ b/solution.py
@@ -19,8 +19,9 @@
 STEPS = 72.0
 OFFSET = 113.0
 
-PARTS = (4, 5, 7)
-PIECES = 2
+PARTS = (4, 6, 6)
+PIECES = 4
+SHIFTS = ((0, 0), (0, 1), (1, 0), (1, 1), (2, 0), (2, 1), (3, 0), (3, 1))
 PARAMS = pltpu.CompilerParams(vmem_limit_bytes=48 << 20)
 PARAMS_Q = pltpu.CompilerParams(vmem_limit_bytes=48 << 20)
 PARAMS_C = pltpu.CompilerParams(vmem_limit_bytes=48 << 20)
@@ -48,15 +49,15 @@
     return [jnp.floor(part * inverse + 0.5) * scale for part in parts]
 
 
-def pair_kernel(chips, groups, core_ref, x_ref, after_ref, own_ref, *refs):
+def pair_kernel(chips, groups, place_ref, x_ref, after_ref, own_ref, *refs):
     del after_ref
     *send_refs, scale_ref, scratch = refs
-    core = core_ref[0]
+    core = place_ref[chips]
     lane = lax.broadcasted_iota(jnp.int32, (8, LANES), 1)
     where = [(d, half, k) for d in range(chips) for half in range(2) for k in range(groups)]
 
     for d, half, k in where:
-        node = 2 * d + (core if half == 0 else 1 - core)
+        node = 2 * place_ref[d] + (core if half == 0 else 1 - core)
         at = pl.multiple_of((node * groups + k) * GROUP, GROUP)
         rows = x_ref[0:1, pl.ds(at, GROUP)].reshape(GROUP_ROWS, LANES)
         scratch[d, half * groups + k] = rows.astype(jnp.float32)
@@ -85,17 +86,34 @@
 
 
 def encode_kernel(
-    chips, groups, count, own_ref, mine_ref, theirs_ref, before_ref, *refs
+    chips, groups, count, apart, own_ref, mine_ref, theirs_ref, before_ref, *refs
 ):
-    *peer_refs, m_ref, flag_ref, buffer, aux, packed, bad, sems, aux_sem = refs
+    *refs, flag_ref, buffer, aux, packed, bad, sems, aux_sems = refs
+    peer_refs, m_refs = refs[:PIECES], refs[PIECES:]
     g = pl.program_id(0)
     slot = lax.rem(g, 2)
     rows = groups * GROUP_ROWS
     lane = lax.broadcasted_iota(jnp.int32, (8, LANES), 1)
 
+    def copies(source, start, size, sem):
+        where = pl.ds(pl.multiple_of(start, AUX_ROWS), size)
+        if not apart:
+            return [pltpu.make_async_copy(source, m_refs[0].at[:, where, :], sem.at[0])]
+        return [
+            pltpu.make_async_copy(source.at[d], m_refs[d].at[where, :], sem.at[d])
+            for d in range(chips)
+        ]
+
     def copy(step, at):
-        where = m_ref.at[:, pl.ds(pl.multiple_of(step * rows, rows), rows), :]
-        return pltpu.make_async_copy(buffer.at[at], where, sems.at[at])
+        return copies(buffer.at[at], step * rows, rows, sems.at[at])
+
+    def start(several):
+        for one in several:
+            one.start()
+
+    def wait(several):
+        for one in several:
+            one.wait()
 
     @pl.when(g == 0)
     def _():
@@ -104,7 +122,7 @@
 
     @pl.when(g >= 2)
     def _():
-        copy(g - 2, slot).wait()
+        wait(copy(g - 2, slot))
 
     mine, theirs = mine_ref[0], pltpu.roll(theirs_ref[0], SEND_LANE, 1)
     high, low = jnp.maximum(mine, theirs), jnp.minimum(mine, theirs)
@@ -128,7 +146,7 @@
                 out.append(jnp.where(part < 0, -code, code))
             buffer[slot, d, at, :] = jnp.concatenate(out, axis=0).astype(jnp.bfloat16)
         packed[d] = tile
-    copy(g, slot).start()
+    start(copy(g, slot))
 
     @pl.when(g == count - 1)
     def _():
@@ -137,12 +155,12 @@
         for d in range(chips):
             unit = packed[d] * jnp.where(flag > 0, jnp.float32(jnp.nan), 1.0 / RATIO)
             aux[d] = jnp.concatenate([unit, unit], axis=0).astype(jnp.bfloat16)
-        last = pltpu.make_async_copy(aux, m_ref.at[:, pl.ds(count * rows, AUX_ROWS), :], aux_sem)
-        last.start()
-        last.wait()
+        last = copies(aux, count * rows, AUX_ROWS, aux_sems)
+        start(last)
+        wait(last)
         if count >= 2:
-            copy(g - 1, 1 - slot).wait()
-        copy(g, slot).wait()
+            wait(copy(g - 1, 1 - slot))
+        wait(copy(g, slot))
 
 
 def slot_of(group):
@@ -153,14 +171,14 @@
     return slot
 
 
-def partial_sums(chips, groups, g, r_ref, units):
+def partial_sums(chips, groups, g, r_refs, units):
     rolled = [pltpu.roll(units[d], LANES - g * groups, 1) for d in range(chips)]
     for k in range(groups):
         at = slice(k * GROUP_ROWS, (k + 1) * GROUP_ROWS)
         total = [jnp.zeros((8, LANES), jnp.float32)] * ROWS
         for d in range(chips):
             unit = jnp.broadcast_to(rolled[d][:, k : k + 1], (8, LANES))
-            code = r_ref[d, at, :].astype(jnp.float32)
+            code = r_refs[d][at, :].astype(jnp.float32)
             for s in range(ROWS):
                 part = code[8 * s : 8 * s + 8]
                 size = jnp.floor(jnp.log2(jnp.abs(part)) * STEPS + (OFFSET * STEPS + 0.5))
@@ -176,11 +194,13 @@
         for d in range(chips):
             units[d] = aux_ref[d].astype(jnp.float32)[0:8]
 
-    for at, done in partial_sums(chips, groups, g, r_ref, units):
+    codes = [r_ref.at[d] for d in range(chips)]
+    for at, done in partial_sums(chips, groups, g, codes, units):
         o_ref[0, at, :] = done
 
 
-def last_decode_kernel(chips, groups, count, r_ref, aux_ref, *refs):
+def last_decode_kernel(chips, groups, count, *refs):
+    r_refs, aux_refs, refs = refs[:chips], refs[chips : 2 * chips], refs[2 * chips :]
     *earlier, o_ref, buffer, units, spoilt, sems, early_sems = refs
     g = pl.program_id(0)
     slot = lax.rem(g, 2)
@@ -201,7 +221,7 @@
             one.start()
         total = jnp.zeros((8, LANES), jnp.float32)
         for d in range(chips):
-            units[d] = aux_ref[d].astype(jnp.float32)[0:8]
+            units[d] = aux_refs[d][...].astype(jnp.float32)[0:8]
             total = total + units[d]
         spoilt[0] = jnp.max(jnp.where(jnp.isnan(total), 1, 0)).astype(jnp.int32)
 
@@ -209,7 +229,7 @@
     def _():
         copy(g - 2, slot).wait()
 
-    for at, done in partial_sums(chips, groups, g, r_ref, units):
+    for at, done in partial_sums(chips, groups, g, r_refs, units):
         buffer[slot, at, :] = done
     copy(g, slot).start()
 
@@ -282,9 +302,16 @@
 COST = pl.CostEstimate(flops=1, bytes_accessed=1, transcendentals=0)
 
 
-def quantized(grads, after, start, count, chips, shard):
+def other_chip(chip, k):
+    x, y = chip // 2, chip % 2
+    return (x + SHIFTS[k][0]) % 4 * 2 + (y + SHIFTS[k][1]) % 2
+
+
+def quantized(grads, after, start, count, chips, shard, relative=False):
     rows, groups = shard // LANES, shard // GROUP
-    core = lax.axis_index("core").astype(jnp.int32).reshape(1)
+    chip = lax.axis_index("chip")
+    slots = [other_chip(chip, k) if relative else k for k in range(chips)]
+    place = jnp.stack([jnp.asarray(a, jnp.int32) for a in (*slots, lax.axis_index("core"))])
 
     def block(size):
         shape = jax.ShapeDtypeStruct((size, count, rows, LANES), jnp.bfloat16)
@@ -306,38 +333,39 @@
         scratch_shapes=[pltpu.VMEM((chips, 2 * groups, GROUP_ROWS, LANES), jnp.float32)],
         compiler_params=PARAMS_Q,
         cost_estimate=COST,
-    )(core, grads, after)
+    )(place, grads, after)
     peer, peer_scales = jax.tree.map(lambda a: lax.ppermute(a, "core", [(0, 1), (1, 0)]), (send, scales))
     return own, peer, scales, peer_scales
 
 
-def pair_sums(own, peer, scales, peer_scales, before, after=()):
+def pair_sums(own, peer, scales, peer_scales, before, apart=False):
     chips, count, rows = own.shape[:3]
     half_spec = pl.BlockSpec((chips, 1, rows, LANES), lambda g: (0, g, 0, 0))
     piece_spec = pl.BlockSpec((chips // PIECES, 1, rows, LANES), lambda g: (0, g, 0, 0))
     tile_spec = pl.BlockSpec((1, 8, LANES), lambda g: (g, 0, 0))
     flag = jax.ShapeDtypeStruct((8, LANES), jnp.float32)
     whole = pl.BlockSpec((8, LANES), lambda g: (0, 0))
-    return pl.pallas_call(
-        lambda *refs: encode_kernel(chips, rows // GROUP_ROWS, count, *refs),
+    length, copies = count * rows + AUX_ROWS, chips if apart else 1
+    message = jax.ShapeDtypeStruct((length, LANES) if apart else (chips, length, LANES), jnp.bfloat16)
+    *messages, flag = pl.pallas_call(
+        lambda *refs: encode_kernel(chips, rows // GROUP_ROWS, count, apart, *refs),
         name="add_and_encode",
         grid=(count,),
         in_specs=[half_spec, tile_spec, tile_spec, whole] + [piece_spec] * PIECES,
-        out_specs=[pl.BlockSpec(memory_space=pl.ANY), whole],
-        out_shape=[
-            jax.ShapeDtypeStruct((chips, count * rows + AUX_ROWS, LANES), jnp.bfloat16), flag,
-        ],
+        out_specs=[pl.BlockSpec(memory_space=pl.ANY)] * copies + [whole],
+        out_shape=[message] * copies + [flag],
         scratch_shapes=[
             pltpu.VMEM((2, chips, rows, LANES), jnp.bfloat16),
             pltpu.VMEM((chips, AUX_ROWS, LANES), jnp.bfloat16),
             pltpu.VMEM((chips, 8, LANES), jnp.float32),
             pltpu.VMEM((8, LANES), jnp.float32),
-            pltpu.SemaphoreType.DMA((2,)),
-            pltpu.SemaphoreType.DMA,
+            pltpu.SemaphoreType.DMA((2, copies)),
+            pltpu.SemaphoreType.DMA((copies,)),
         ],
         compiler_params=PARAMS_C,
         cost_estimate=COST,
     )(own, scales, peer_scales, before, *peer)
+    return messages, flag
 
 
 def node_sums(received, count, chips, rows, earlier=None):
@@ -364,7 +392,9 @@
         lambda *refs: last_decode_kernel(chips, groups, count, *refs),
         name="last_decode_and_requantize",
         grid=(count,),
-        in_specs=in_specs + [pl.BlockSpec(memory_space=pl.ANY)] * len(earlier),
+        in_specs=[pl.BlockSpec((rows, LANES), lambda g: (g, 0))] * chips
+        + [pl.BlockSpec((AUX_ROWS, LANES), lambda g: (count * rows // AUX_ROWS, 0))] * chips
+        + [pl.BlockSpec(memory_space=pl.ANY)] * len(earlier),
         out_specs=pl.BlockSpec(memory_space=pl.ANY),
         out_shape=jax.ShapeDtypeStruct((replicas, rows, LANES), jnp.bfloat16),
         scratch_shapes=[
@@ -376,7 +406,7 @@
         ],
         compiler_params=PARAMS,
         cost_estimate=COST,
-    )(received, received, *earlier)
+    )(*received, *received, *earlier)
 
 
 def plain_sums(grads, after, replicas, nodes, shard):
@@ -429,12 +459,18 @@
     rows = shard // LANES
     partials, start = [], 0
     for count in PARTS:
-        message, flag = pair_sums(*quantized(grads, flag, start, count, chips, shard), flag)
-        received = lax.all_to_all(message, "chip", split_axis=0, concat_axis=0, tiled=True)
+        last = start + count == replicas
+        ready = quantized(grads, flag, start, count, chips, shard, last)
+        messages, flag = pair_sums(*ready, flag, last)
+        if last:
+            received = [
+                lax.ppermute(m, "chip", [(c, other_chip(c, k)) for c in range(chips)]) if k else m
+                for k, m in enumerate(messages)
+            ]
+        else:
+            received = lax.all_to_all(messages[0], "chip", split_axis=0, concat_axis=0, tiled=True)
+        partials.append(node_sums(received, count, chips, rows, partials if last else None))
         start += count
-        earlier = partials if start == replicas else None
-        partial = node_sums(received, count, chips, rows, earlier)
-        partials.append(partial)
     owned = lax.all_to_all(partials[-1], GROUP_AXES[::-1], split_axis=0, concat_axis=0, tiled=True)
     state = [a.reshape(shard // LANES, LANES) for a in (master, moment, second)]
 

time: 117 us -> 114 us (0.974)
  waiting for transfers between devices: 32.5 us -> 17.9 us
  starting transfers between devices: 18.7 us -> 26.3 us
  Pallas kernels: 33.5 us -> 35.9 us
  blocking collectives: 26.5 us -> 28.4 us
    all_to_all x3 -> x2, waiting for transfers between devices: 24.7 us -> 2.24 us  [body(): lax.all_to_all(messages[0], 'chip', split_axis=0, concat_axis=0, tiled=True)]
    ppermute x0 -> x7, starting transfers between devices: none -> 11.5 us  [body(): lax.ppermute(m, 'chip', [(c, other_chip(c, k)) for c in range(chips)])]
    ppermute x0 -> x7, waiting for transfers between devices: none -> 9.38 us  [body(): lax.ppermute(m, 'chip', [(c, other_chip(c, k)) for c in range(chips)])]
    all_to_all x3 -> x2, starting transfers between devices: 16.6 us -> 11.2 us  [body(): lax.all_to_all(messages[0], 'chip', split_axis=0, concat_axis=0, tiled=True)]
    all_to_all x1, blocking collectives: 26.5 us -> 28.4 us  [body(): lax.all_to_all(partials[-1], GROUP_AXES[::-1], split_axis=0, concat_axis=...]
    ppermute x9 -> x15, starting transfers between devices: 2.07 us -> 3.6 us  [quantized(): lax.ppermute(a, 'core', [(0, 1), (1, 0)])]
    ppermute x9 -> x15, waiting for transfers between devices: 7.76 us -> 6.24 us  [quantized(): lax.ppermute(a, 'core', [(0, 1), (1, 0)])]
  transfers between devices with their start and end apart: 12 -> 24, of which waited for: 6 -> 8; matrix products, arithmetic and copies ran while one was open for 0% -> 0% of each run, Pallas kernels for 19% -> 21%
where the time goes in v7:
time: 114 us; the launch traced here: 113 us
  Pallas kernels  35.9 us (31%)
  blocking collectives  28.4 us (25%)
  starting transfers between devices  26.3 us (23%)
  waiting for transfers between devices  17.9 us (16%)
  local copies, waits for them, and re-layouts  2.97 us (3%)
    all_to_all x1, blocking collectives, body(): lax.all_to_all(partials[-1], GROUP_AXES[::-1], split_axis=0, concat_axis=...  28.4 us
    pallas_call x3, Pallas kernels, quantized(): pl.pallas_call(lambda *refs: pair_kernel(chips, groups, *refs), name='qua...  16.1 us
    ppermute x7, starting transfers between devices, body(): lax.ppermute(m, 'chip', [(c, other_chip(c, k)) for c in range(chips)])  11.5 us
    all_to_all x2, starting transfers between devices, body(): lax.all_to_all(messages[0], 'chip', split_axis=0, concat_axis=0, tiled=True)  11.2 us
    pallas_call x3, Pallas kernels, pair_sums(): pl.pallas_call(lambda *refs: encode_kernel(chips, rows // GROUP_ROWS, cou...  9.41 us
    ppermute x7, waiting for transfers between devices, body(): lax.ppermute(m, 'chip', [(c, other_chip(c, k)) for c in range(chips)])  9.38 us
    ppermute x15, waiting for transfers between devices, quantized(): lax.ppermute(a, 'core', [(0, 1), (1, 0)])  6.24 us
    pallas_call x1, Pallas kernels, node_sums(): pl.pallas_call(lambda *refs: last_decode_kernel(chips, groups, count, *re...  5.12 us
  transfers between devices with their start and end apart: 24, of which 8 were waited for; matrix products, arithmetic and copies ran while one was open for 0% of the time, Pallas kernels for 21%

profile of v7, /device:TPU:2, one launch (start us, length us, event | category | flops | bytes accessed | tf_op | source)
XLA Modules:
  0.0 113.1 jit_solution(18192049162628097653)
XLA Ops:
  0.6 0.1 stack.46.refs_0_
  0.7 4.1 %quantize.3 = (bf16[8,4,128,128]{3,2,1,0:T(8,128)(2,1)S(1)}, bf16[2,4,128,128]{3,2,1,0:T(8,128)(2,1)S(1)}, bf16[2,4,128,128]{3,2,1,0:T(8,128)(2,1)S(1)}, bf16[2,...) custom-call(s32[9]{0:T(128)S(1)} %stack.46.refs_0_, ...), custom_call_target="tpu_custom_call" | custom-call | flops 1 | bytes 1 | tf_op jit(solution)/shard_map/quantize/pallas_call | solution.py:322
  4.9 0.1 collective-permute-start.1
  5.0 0.5 collective-permute-start.2
  5.5 0.1 collective-permute-start.3
  5.6 0.4 collective-permute-start.4
  6.0 0.1 collective-permute-start
  6.1 1.6 %collective-permute-done.refs_2_ = f32[4,8,128]{2,1,0:T(8,128)S(1)} collective-permute-done((f32[4,8,128]{2,1,0:T(8,128)S(1)}, f32[4,8,128]{2,1,0:T(8,128)S(1)}, u32[]{:S(2)}, u32[]{:S(2)}) %collective-permute-start) | collective-permute-done | bytes 16416 | tf_op jit(solution)/shard_map/ppermute | solution.py:337
  7.6 0.0 collective-permute-done.1.refs_4_
  7.6 0.0 collective-permute-done.2.refs_5_
  7.6 0.0 collective-permute-done.3.refs_6_
  7.7 0.0 collective-permute-done.4.refs_7_
  7.7 1.8 %add_and_encode.3 = (bf16[8,528,128]{2,1,0:T(8,128)(2,1)S(1)}, f32[8,128]{1,0:T(8,128)S(1)}) custom-call(bf16[8,4,128,128]{3,2,1,0:T(8,128)(2,1)S(1)} %get-tuple-element.81.refs_0_, f32[4,8,128]{2,1,0:T(8,128)S(1)} %get-tuple-element.82.refs_1_, f32[4,8,128]{2,1,0:T(8,128)S(1)} %collective-permute-done.refs_2_, ...), custom_call_target="tpu_custom_call" | custom-call | flops 1 | bytes 1 | tf_op jit(solution)/shard_map/add_and_encode/pallas_call | solution.py:350
  9.5 1.0 copy-done.1
  10.5 5.8 %all-to-all-start.2 = ((bf16[8,528,128]{2,1,0:T(8,128)(2,1)}), bf16[8,528,128]{2,1,0:T(8,128)(2,1)S(1)}, u32[]{:S(2)}, u32[]{:S(2)}) async-start(bf16[8,528,128]{2,1,0:T(8,128)(2,1)} %copy-done.1), calls=%async_computation.2 | async-start | bytes 2162688 | tf_op jit(solution)/shard_map/all_to_all | solution.py:471
  16.3 6.0 %quantize.4 = (bf16[8,6,128,128]{3,2,1,0:T(8,128)(2,1)S(1)}, bf16[2,6,128,128]{3,2,1,0:T(8,128)(2,1)S(1)}, bf16[2,6,128,128]{3,2,1,0:T(8,128)(2,1)S(1)}, bf16[2,...) custom-call(s32[9]{0:T(128)S(1)} %stack.46.refs_0_, ...), custom_call_target="tpu_custom_call" | custom-call | flops 1 | bytes 1 | tf_op jit(solution)/shard_map/quantize/pallas_call | solution.py:322
  22.3 0.1 collective-permute-start.6
  22.4 0.5 collective-permute-start.7
  22.9 0.1 collective-permute-start.8
  23.0 0.4 collective-permute-start.9
  23.4 0.1 collective-permute-start.5
  23.5 2.3 %collective-permute-done.5.refs_2_ = f32[6,8,128]{2,1,0:T(8,128)S(1)} collective-permute-done((f32[6,8,128]{2,1,0:T(8,128)S(1)}, f32[6,8,128]{2,1,0:T(8,128)S(1)}, u32[]{:S(2)}, u32[]{:S(2)}) %collective-permute-start.5) | collective-permute-done | bytes 24608 | tf_op jit(solution)/shard_map/ppermute | solution.py:337
  25.8 0.0 collective-permute-done.6.refs_4_
  25.8 0.0 collective-permute-done.7.refs_5_
  25.8 0.0 collective-permute-done.8.refs_6_
  25.8 0.0 collective-permute-done.9.refs_7_
  25.8 2.6 %add_and_encode.4 = (bf16[8,784,128]{2,1,0:T(8,128)(2,1)S(1)}, f32[8,128]{1,0:T(8,128)S(1)}) custom-call(bf16[8,6,128,128]{3,2,1,0:T(8,128)(2,1)S(1)} %get-tuple-element.88.refs_0_, f32[6,8,128]{2,1,0:T(8,128)S(1)} %get-tuple-element.89.refs_1_, f32[6,8,128]{2,1,0:T(8,128)S(1)} %collective-permute-done.5.refs_2_, ...), custom_call_target="tpu_custom_call" | custom-call | flops 1 | bytes 1 | tf_op jit(solution)/shard_map/add_and_encode/pallas_call | solution.py:350
  28.5 1.2 %copy-done = bf16[8,784,128]{2,1,0:T(8,128)(2,1)} copy-done((bf16[8,784,128]{2,1,0:T(8,128)(2,1)}, bf16[8,784,128]{2,1,0:T(8,128)(2,1)S(1)}, u32[]{:S(2)}) %copy-start) | copy-done | bytes 1605656
  29.6 2.2 %all-to-all-done.2.refs_0_.refs_1_ = bf16[8,528,128]{2,1,0:T(8,128)(2,1)S(1)} async-done(((bf16[8,528,128]{2,1,0:T(8,128)(2,1)}), bf16[8,528,128]{2,1,0:T(8,128)(2,1)S(1)}, u32[]{:S(2)}, u32[]{:S(2)}) %all-to-all-start.2) | async-done | bytes 1081376 | tf_op jit(solution)/shard_map/all_to_all | solution.py:471
  31.9 5.4 %all-to-all-start.3 = ((bf16[8,784,128]{2,1,0:T(8,128)(2,1)}), bf16[8,784,128]{2,1,0:T(8,128)(2,1)S(1)}, u32[]{:S(2)}, u32[]{:S(2)}) async-start(bf16[8,784,128]{2,1,0:T(8,128)(2,1)} %copy-done), calls=%async_computation.3 | async-start | bytes 3211264 | tf_op jit(solution)/shard_map/all_to_all | solution.py:471
  37.2 0.1 stack.45.refs_0_
  37.3 6.0 %quantize.5 = (bf16[8,6,128,128]{3,2,1,0:T(8,128)(2,1)S(1)}, bf16[2,6,128,128]{3,2,1,0:T(8,128)(2,1)S(1)}, bf16[2,6,128,128]{3,2,1,0:T(8,128)(2,1)S(1)}, bf16[2,...) custom-call(s32[9]{0:T(128)S(1)} %stack.45.refs_0_, ...), custom_call_target="tpu_custom_call" | custom-call | flops 1 | bytes 1 | tf_op jit(solution)/shard_map/quantize/pallas_call | solution.py:322
  43.3 0.1 collective-permute-start.11
  43.4 0.5 collective-permute-start.12
  43.9 0.1 collective-permute-start.13
  44.0 0.4 collective-permute-start.14
  44.4 0.1 collective-permute-start.10
  44.5 2.3 %collective-permute-done.10.refs_2_ = f32[6,8,128]{2,1,0:T(8,128)S(1)} collective-permute-done((f32[6,8,128]{2,1,0:T(8,128)S(1)}, f32[6,8,128]{2,1,0:T(8,128)S(1)}, u32[]{:S(2)}, u32[]{:S(2)}) %collective-permute-start.10) | collective-permute-done | bytes 24608 | tf_op jit(solution)/shard_map/ppermute | solution.py:337
  46.8 0.0 collective-permute-done.11.refs_4_
  46.8 0.0 collective-permute-done.12.refs_5_
  46.8 0.0 collective-permute-done.13.refs_6_
  46.9 0.0 collective-permute-done.14.refs_7_
  46.9 5.0 %add_and_encode.5 = (bf16[784,128]{1,0:T(8,128)(2,1)S(1)}, bf16[784,128]{1,0:T(8,128)(2,1)S(1)}, bf16[784,128]{1,0:T(8,128)(2,1)S(1)}, bf16[784,128]{1,0:T(8,128...) custom-call(bf16[8,6,128,128]{3,2,1,0:T(8,128)(2,1)S(1)} %get-tuple-, ...), custom_call_target="tpu_custom_call" | custom-call | flops 1 | bytes 1 | tf_op jit(solution)/shard_map/add_and_encode/pallas_call | solution.py:350
  51.9 1.6 %collective-permute-start.15 = (bf16[784,128]{1,0:T(8,128)(2,1)S(1)}, bf16[784,128]{1,0:T(8,128)(2,1)S(1)}, u32[]{:S(2)}, u32[]{:S(2)}) collective-permute-start(bf16[784,128]{1,0:T(8,128)(2,1)S(1)} %get-tuple-element.102), channel_id=1, source_target_pairs={{0,2},{2,0},{4,6},{6,4},{8,10},{10,8},{12,14},{14,12},{1,3},{3,1},... | collective-permute-start | bytes 602120 | tf_op jit(solution)/shard_map/ppermute | solution.py:467
  53.4 1.5 %collective-permute-start.16 = (bf16[784,128]{1,0:T(8,128)(2,1)S(1)}, bf16[784,128]{1,0:T(8,128)(2,1)S(1)}, u32[]{:S(2)}, u32[]{:S(2)}) collective-permute-start(bf16[784,128]{1,0:T(8,128)(2,1)S(1)} %get-tuple-element.103), channel_id=1, source_target_pairs={{0,4},{2,6},{4,8},{6,10},{8,12},{10,14},{12,0},{14,2},{1,5},{3,7},... | collective-permute-start | bytes 602120 | tf_op jit(solution)/shard_map/ppermute | solution.py:467
  54.9 1.2 %collective-permute-start.17 = (bf16[784,128]{1,0:T(8,128)(2,1)}, bf16[784,128]{1,0:T(8,128)(2,1)S(1)}, u32[]{:S(2)}, u32[]{:S(2)}) collective-permute-start(bf16[784,128]{1,0:T(8,128)(2,1)} %get-tuple-element.104), channel_id=1, source_target_pairs={{0,6},{2,4},{4,10},{6,8},{8,14},{10,12},{12,2},{14,0},{1,7},{3,5},... | collective-permute-start | bytes 602120 | tf_op jit(solution)/shard_map/ppermute | solution.py:467
  56.1 1.4 %collective-permute-start.18 = (bf16[784,128]{1,0:T(8,128)(2,1)}, bf16[784,128]{1,0:T(8,128)(2,1)}, u32[]{:S(2)}, u32[]{:S(2)}) collective-permute-start(bf16[784,128]{1,0:T(8,128)(2,1)} %get-tuple-element.105), channel_id=1, source_target_pairs={{0,8},{2,10},{4,12},{6,14},{8,0},{10,2},{12,4},{14,6},{1,9},{3,11}... | collective-permute-start | bytes 602120 | tf_op jit(solution)/shard_map/ppermute | solution.py:467
  57.5 3.0 %collective-permute-start.19 = (bf16[784,128]{1,0:T(8,128)(2,1)}, bf16[784,128]{1,0:T(8,128)(2,1)}, u32[]{:S(2)}, u32[]{:S(2)}) collective-permute-start(bf16[784,128]{1,0:T(8,128)(2,1)} %get-tuple-element.106), channel_id=1, source_target_pairs={{0,10},{2,8},{4,14},{6,12},{8,2},{10,0},{12,6},{14,4},{1,11},{3,9}... | collective-permute-start | bytes 602120 | tf_op jit(solution)/shard_map/ppermute | solution.py:467
  60.5 0.6 collective-permute-done.15.refs_1_.refs_9_
  61.1 0.2 collective-permute-start.20
  61.4 0.0 collective-permute-done.16.refs_2_.refs_10_
  61.4 2.6 %collective-permute-start.21 = (bf16[784,128]{1,0:T(8,128)(2,1)}, bf16[784,128]{1,0:T(8,128)(2,1)}, u32[]{:S(2)}, u32[]{:S(2)}) collective-permute-start(bf16[784,128]{1,0:T(8,128)(2,1)} %get-tuple-element.108), channel_id=1, source_target_pairs={{0,14},{2,12},{4,2},{6,0},{8,6},{10,4},{12,10},{14,8},{1,15},{3,13... | collective-permute-start | bytes 602120 | tf_op jit(solution)/shard_map/ppermute | solution.py:467
  64.0 1.8 %decode_and_requantize.2.refs_16_ = bf16[4,128,128]{2,1,0:T(8,128)(2,1)S(1)} custom-call(bf16[8,528,128]{2,1,0:T(8,128)(2,1)S(1)} %all-to-all-done.2.refs_0_.refs_1_, bf16[8,528,128]{2,1,0:T(8,128)(2,1)S(1)} %all-to-all-done.2.refs_0_.refs_1_), custom_call_target="tpu_custom_call" | custom-call | flops 1 | bytes 1 | tf_op jit(solution)/shard_map/decode_and_requantize/pallas_call | solution.py:379
  65.8 0.6 copy-done.2
  66.4 2.7 %decode_and_requantize.3.refs_17_ = bf16[6,128,128]{2,1,0:T(8,128)(2,1)S(1)} custom-call(bf16[8,784,128]{2,1,0:T(8,128)(2,1)S(1)} %all-to-all-done.3.refs_0_.refs_1_, bf16[8,784,128]{2,1,0:T(8,128)(2,1)S(1)} %all-to-all-done.3.refs_0_.refs_1_), custom_call_target="tpu_custom_call" | custom-call | flops 1 | bytes 1 | tf_op jit(solution)/shard_map/decode_and_requantize/pallas_call | solution.py:379
  69.1 0.0 collective-permute-done.17.refs_3_.refs_11_
  69.1 0.0 collective-permute-done.18.refs_4_.refs_12_
  69.1 1.9 %collective-permute-done.19.refs_5_.refs_13_ = bf16[784,128]{1,0:T(8,128)(2,1)} collective-permute-done((bf16[784,128]{1,0:T(8,128)(2,1)}, bf16[784,128]{1,0:T(8,128)(2,1)}, u32[]{:S(2)}, u32[]{:S(2)}) %collective-permute-start.19) | collective-permute-done | bytes 200736 | tf_op jit(solution)/shard_map/ppermute | solution.py:467
  71.1 1.7 %collective-permute-done.20.refs_6_.refs_14_ = bf16[784,128]{1,0:T(8,128)(2,1)} collective-permute-done((bf16[784,128]{1,0:T(8,128)(2,1)}, bf16[784,128]{1,0:T(8,128)(2,1)}, u32[]{:S(2)}, u32[]{:S(2)}) %collective-permute-start.20) | collective-permute-done | bytes 200736 | tf_op jit(solution)/shard_map/ppermute | solution.py:467
  72.8 5.1 %collective-permute-done.21.refs_7_.refs_15_ = bf16[784,128]{1,0:T(8,128)(2,1)} collective-permute-done((bf16[784,128]{1,0:T(8,128)(2,1)}, bf16[784,128]{1,0:T(8,128)(2,1)}, u32[]{:S(2)}, u32[]{:S(2)}) %collective-permute-start.21) | collective-permute-done | bytes 200736 | tf_op jit(solution)/shard_map/ppermute | solution.py:467
  77.9 5.1 %last_decode_and_requantize.1 = bf16[16,128,128]{2,1,0:T(8,128)(2,1)S(1)} custom-call(bf16[784,128]{1,0:T(8,128)(2,1)S(1)} %get-tuple-element.101.refs_0_.refs_8_, bf16[784,128]{1,0:T(8,128)(2,1)S(1)} %collective-permute-done.15.refs_1_.refs_9_, bf16[784,128]{1,0:T(8,128)(2,1)S(1)} %collective-permute-done.16.refs_2_.refs_10_, ...), custom_call_target="tpu_custom_call" | custom-call | flops 1 | bytes 1 | tf_op jit(solution)/shard_map/last_decode_and_requantize/pallas_call | solution.py:391
  83.0 28.4 %all_to_all.24.refs_0_ = bf16[16,128,128]{2,1,0:T(8,128)(2,1)S(1)} all-to-all(bf16[16,128,128]{2,1,0:T(8,128)(2,1)S(1)} %last_decode_and_requantize.1), channel_id=1, replica_groups=mesh['group3'=2,'group2'=2,'group1'=2,'group0'=2,'chip'=8,'core'=2] {'gr..., dimensions={0} | all-to-all | bytes 1048576 | tf_op jit(solution)/shard_map/all_to_all | solution.py:474
  111.4 0.8 adamw_update.3
  112.2 0.7 while.13
  (13 shorter events, 0.0 us)
Async XLA Ops:
  4.9 2.8 %collective-permute-start.1 = (bf16[2,4,128,128]{3,2,1,0:T(8,128)(2,1)S(1)}, bf16[2,4,128,128]{3,2,1,0:T(8,128)(2,1)S(1)}, u32[]{:S(2)}, u32[]{:S(2)}) collective-permute-start(bf16[2,4,128,128]{3,2,1,0:T(8,128)(2,1)S(1)} %get-tuple-element.83), channel_id=1, source_target_pairs={{0,1},{1,0},{2,3},{3,2},{4,5},{5,4},{6,7},{7,6},{8,9},{9,8},{10,11... | collective-permute-start | bytes 786440 | tf_op jit(solution)/shard_map/ppermute | solution.py:337
  5.0 2.7 %collective-permute-start.2 = (bf16[2,4,128,128]{3,2,1,0:T(8,128)(2,1)S(1)}, bf16[2,4,128,128]{3,2,1,0:T(8,128)(2,1)S(1)}, u32[]{:S(2)}, u32[]{:S(2)}) collective-permute-start(bf16[2,4,128,128]{3,2,1,0:T(8,128)(2,1)S(1)} %get-tuple-element.84), channel_id=1, source_target_pairs={{0,1},{1,0},{2,3},{3,2},{4,5},{5,4},{6,7},{7,6},{8,9},{9,8},{10,11... | collective-permute-start | bytes 786440 | tf_op jit(solution)/shard_map/ppermute | solution.py:337
  5.5 2.2 %collective-permute-start.3 = (bf16[2,4,128,128]{3,2,1,0:T(8,128)(2,1)S(1)}, bf16[2,4,128,128]{3,2,1,0:T(8,128)(2,1)S(1)}, u32[]{:S(2)}, u32[]{:S(2)}) collective-permute-start(bf16[2,4,128,128]{3,2,1,0:T(8,128)(2,1)S(1)} %get-tuple-element.85), channel_id=1, source_target_pairs={{0,1},{1,0},{2,3},{3,2},{4,5},{5,4},{6,7},{7,6},{8,9},{9,8},{10,11... | collective-permute-start | bytes 786440 | tf_op jit(solution)/shard_map/ppermute | solution.py:337
  5.6 2.1 %collective-permute-start.4 = (bf16[2,4,128,128]{3,2,1,0:T(8,128)(2,1)S(1)}, bf16[2,4,128,128]{3,2,1,0:T(8,128)(2,1)S(1)}, u32[]{:S(2)}, u32[]{:S(2)}) collective-permute-start(bf16[2,4,128,128]{3,2,1,0:T(8,128)(2,1)S(1)} %get-tuple-element.86), channel_id=1, source_target_pairs={{0,1},{1,0},{2,3},{3,2},{4,5},{5,4},{6,7},{7,6},{8,9},{9,8},{10,11... | collective-permute-start | bytes 786440 | tf_op jit(solution)/shard_map/ppermute | solution.py:337
  6.0 1.7 %collective-permute-start = (f32[4,8,128]{2,1,0:T(8,128)S(1)}, f32[4,8,128]{2,1,0:T(8,128)S(1)}, u32[]{:S(2)}, u32[]{:S(2)}) collective-permute-start(f32[4,8,128]{2,1,0:T(8,128)S(1)} %get-tuple-element.82.refs_1_), channel_id=1, source_target_pairs={{0,1},{1,0},{2,3},{3,2},{4,5},{5,4},{6,7},{7,6},{8,9},{9,8},{10,11... | collective-permute-start | bytes 49160 | tf_op jit(solution)/shard_map/ppermute | solution.py:337
  9.5 1.0 copy-start.1
  10.5 21.4 %all-to-all-start.2 = ((bf16[8,528,128]{2,1,0:T(8,128)(2,1)}), bf16[8,528,128]{2,1,0:T(8,128)(2,1)S(1)}, u32[]{:S(2)}, u32[]{:S(2)}) async-start(bf16[8,528,128]{2,1,0:T(8,128)(2,1)} %copy-done.1), calls=%async_computation.2 | async-start | bytes 2162688 | tf_op jit(solution)/shard_map/all_to_all | solution.py:471
  22.3 3.5 %collective-permute-start.6 = (bf16[2,6,128,128]{3,2,1,0:T(8,128)(2,1)S(1)}, bf16[2,6,128,128]{3,2,1,0:T(8,128)(2,1)S(1)}, u32[]{:S(2)}, u32[]{:S(2)}) collective-permute-start(bf16[2,6,128,128]{3,2,1,0:T(8,128)(2,1)S(1)} %get-tuple-element.90), channel_id=1, source_target_pairs={{0,1},{1,0},{2,3},{3,2},{4,5},{5,4},{6,7},{7,6},{8,9},{9,8},{10,11... | collective-permute-start | bytes 1179656 | tf_op jit(solution)/shard_map/ppermute | solution.py:337
  22.4 3.4 %collective-permute-start.7 = (bf16[2,6,128,128]{3,2,1,0:T(8,128)(2,1)S(1)}, bf16[2,6,128,128]{3,2,1,0:T(8,128)(2,1)S(1)}, u32[]{:S(2)}, u32[]{:S(2)}) collective-permute-start(bf16[2,6,128,128]{3,2,1,0:T(8,128)(2,1)S(1)} %get-tuple-element.91), channel_id=1, source_target_pairs={{0,1},{1,0},{2,3},{3,2},{4,5},{5,4},{6,7},{7,6},{8,9},{9,8},{10,11... | collective-permute-start | bytes 1179656 | tf_op jit(solution)/shard_map/ppermute | solution.py:337
  22.9 2.9 %collective-permute-start.8 = (bf16[2,6,128,128]{3,2,1,0:T(8,128)(2,1)S(1)}, bf16[2,6,128,128]{3,2,1,0:T(8,128)(2,1)S(1)}, u32[]{:S(2)}, u32[]{:S(2)}) collective-permute-start(bf16[2,6,128,128]{3,2,1,0:T(8,128)(2,1)S(1)} %get-tuple-element.92), channel_id=1, source_target_pairs={{0,1},{1,0},{2,3},{3,2},{4,5},{5,4},{6,7},{7,6},{8,9},{9,8},{10,11... | collective-permute-start | bytes 1179656 | tf_op jit(solution)/shard_map/ppermute | solution.py:337
  23.0 2.8 %collective-permute-start.9 = (bf16[2,6,128,128]{3,2,1,0:T(8,128)(2,1)S(1)}, bf16[2,6,128,128]{3,2,1,0:T(8,128)(2,1)S(1)}, u32[]{:S(2)}, u32[]{:S(2)}) collective-permute-start(bf16[2,6,128,128]{3,2,1,0:T(8,128)(2,1)S(1)} %get-tuple-element.93), channel_id=1, source_target_pairs={{0,1},{1,0},{2,3},{3,2},{4,5},{5,4},{6,7},{7,6},{8,9},{9,8},{10,11... | collective-permute-start | bytes 1179656 | tf_op jit(solution)/shard_map/ppermute | solution.py:337
  23.4 2.4 %collective-permute-start.5 = (f32[6,8,128]{2,1,0:T(8,128)S(1)}, f32[6,8,128]{2,1,0:T(8,128)S(1)}, u32[]{:S(2)}, u32[]{:S(2)}) collective-permute-start(f32[6,8,128]{2,1,0:T(8,128)S(1)} %get-tuple-element.89.refs_1_), channel_id=1, source_target_pairs={{0,1},{1,0},{2,3},{3,2},{4,5},{5,4},{6,7},{7,6},{8,9},{9,8},{10,11... | collective-permute-start | bytes 73736 | tf_op jit(solution)/shard_map/ppermute | solution.py:337
  28.5 1.2 %copy-start = (bf16[8,784,128]{2,1,0:T(8,128)(2,1)}, bf16[8,784,128]{2,1,0:T(8,128)(2,1)S(1)}, u32[]{:S(2)}) copy-start(bf16[8,784,128]{2,1,0:T(8,128)(2,1)S(1)} %get-tuple-element.110) | copy-start | bytes 4816900
  31.9 34.5 %all-to-all-start.3 = ((bf16[8,784,128]{2,1,0:T(8,128)(2,1)}), bf16[8,784,128]{2,1,0:T(8,128)(2,1)S(1)}, u32[]{:S(2)}, u32[]{:S(2)}) async-start(bf16[8,784,128]{2,1,0:T(8,128)(2,1)} %copy-done), calls=%async_computation.3 | async-start | bytes 3211264 | tf_op jit(solution)/shard_map/all_to_all | solution.py:471
  43.3 3.5 %collective-permute-start.11 = (bf16[2,6,128,128]{3,2,1,0:T(8,128)(2,1)S(1)}, bf16[2,6,128,128]{3,2,1,0:T(8,128)(2,1)S(1)}, u32[]{:S(2)}, u32[]{:S(2)}) collective-permute-start(bf16[2,6,128,128]{3,2,1,0:T(8,128)(2,1)S(1)} %get-tuple-element.97), channel_id=1, source_target_pairs={{0,1},{1,0},{2,3},{3,2},{4,5},{5,4},{6,7},{7,6},{8,9},{9,8},{10,11... | collective-permute-start | bytes 1179656 | tf_op jit(solution)/shard_map/ppermute | solution.py:337
  43.4 3.4 %collective-permute-start.12 = (bf16[2,6,128,128]{3,2,1,0:T(8,128)(2,1)S(1)}, bf16[2,6,128,128]{3,2,1,0:T(8,128)(2,1)S(1)}, u32[]{:S(2)}, u32[]{:S(2)}) collective-permute-start(bf16[2,6,128,128]{3,2,1,0:T(8,128)(2,1)S(1)} %get-tuple-element.98), channel_id=1, source_target_pairs={{0,1},{1,0},{2,3},{3,2},{4,5},{5,4},{6,7},{7,6},{8,9},{9,8},{10,11... | collective-permute-start | bytes 1179656 | tf_op jit(solution)/shard_map/ppermute | solution.py:337
  43.9 2.9 %collective-permute-start.13 = (bf16[2,6,128,128]{3,2,1,0:T(8,128)(2,1)S(1)}, bf16[2,6,128,128]{3,2,1,0:T(8,128)(2,1)S(1)}, u32[]{:S(2)}, u32[]{:S(2)}) collective-permute-start(bf16[2,6,128,128]{3,2,1,0:T(8,128)(2,1)S(1)} %get-tuple-element.99), channel_id=1, source_target_pairs={{0,1},{1,0},{2,3},{3,2},{4,5},{5,4},{6,7},{7,6},{8,9},{9,8},{10,11... | collective-permute-start | bytes 1179656 | tf_op jit(solution)/shard_map/ppermute | solution.py:337
  44.0 2.8 %collective-permute-start.14 = (bf16[2,6,128,128]{3,2,1,0:T(8,128)(2,1)S(1)}, bf16[2,6,128,128]{3,2,1,0:T(8,128)(2,1)S(1)}, u32[]{:S(2)}, u32[]{:S(2)}) collective-permute-start(bf16[2,6,128,128]{3,2,1,0:T(8,128)(2,1)S(1)} %get-tuple-element.100), channel_id=1, source_target_pairs={{0,1},{1,0},{2,3},{3,2},{4,5},{5,4},{6,7},{7,6},{8,9},{9,8},{10,11... | collective-permute-start | bytes 1179656 | tf_op jit(solution)/shard_map/ppermute | solution.py:337
  44.4 2.4 %collective-permute-start.10 = (f32[6,8,128]{2,1,0:T(8,128)S(1)}, f32[6,8,128]{2,1,0:T(8,128)S(1)}, u32[]{:S(2)}, u32[]{:S(2)}) collective-permute-start(f32[6,8,128]{2,1,0:T(8,128)S(1)} %get-tuple-element.96.refs_1_), channel_id=1, source_target_pairs={{0,1},{1,0},{2,3},{3,2},{4,5},{5,4},{6,7},{7,6},{8,9},{9,8},{10,11... | collective-permute-start | bytes 73736 | tf_op jit(solution)/shard_map/ppermute | solution.py:337
  51.9 9.3 %collective-permute-start.15 = (bf16[784,128]{1,0:T(8,128)(2,1)S(1)}, bf16[784,128]{1,0:T(8,128)(2,1)S(1)}, u32[]{:S(2)}, u32[]{:S(2)}) collective-permute-start(bf16[784,128]{1,0:T(8,128)(2,1)S(1)} %get-tuple-element.102), channel_id=1, source_target_pairs={{0,2},{2,0},{4,6},{6,4},{8,10},{10,8},{12,14},{14,12},{1,3},{3,1},... | collective-permute-start | bytes 602120 | tf_op jit(solution)/shard_map/ppermute | solution.py:467
  53.4 7.9 %collective-permute-start.16 = (bf16[784,128]{1,0:T(8,128)(2,1)S(1)}, bf16[784,128]{1,0:T(8,128)(2,1)S(1)}, u32[]{:S(2)}, u32[]{:S(2)}) collective-permute-start(bf16[784,128]{1,0:T(8,128)(2,1)S(1)} %get-tuple-element.103), channel_id=1, source_target_pairs={{0,4},{2,6},{4,8},{6,10},{8,12},{10,14},{12,0},{14,2},{1,5},{3,7},... | collective-permute-start | bytes 602120 | tf_op jit(solution)/shard_map/ppermute | solution.py:467
  54.9 14.2 %collective-permute-start.17 = (bf16[784,128]{1,0:T(8,128)(2,1)}, bf16[784,128]{1,0:T(8,128)(2,1)S(1)}, u32[]{:S(2)}, u32[]{:S(2)}) collective-permute-start(bf16[784,128]{1,0:T(8,128)(2,1)} %get-tuple-element.104), channel_id=1, source_target_pairs={{0,6},{2,4},{4,10},{6,8},{8,14},{10,12},{12,2},{14,0},{1,7},{3,5},... | collective-permute-start | bytes 602120 | tf_op jit(solution)/shard_map/ppermute | solution.py:467
  56.1 13.1 %collective-permute-start.18 = (bf16[784,128]{1,0:T(8,128)(2,1)}, bf16[784,128]{1,0:T(8,128)(2,1)}, u32[]{:S(2)}, u32[]{:S(2)}) collective-permute-start(bf16[784,128]{1,0:T(8,128)(2,1)} %get-tuple-element.105), channel_id=1, source_target_pairs={{0,8},{2,10},{4,12},{6,14},{8,0},{10,2},{12,4},{14,6},{1,9},{3,11}... | collective-permute-start | bytes 602120 | tf_op jit(solution)/shard_map/ppermute | solution.py:467
  57.5 13.6 %collective-permute-start.19 = (bf16[784,128]{1,0:T(8,128)(2,1)}, bf16[784,128]{1,0:T(8,128)(2,1)}, u32[]{:S(2)}, u32[]{:S(2)}) collective-permute-start(bf16[784,128]{1,0:T(8,128)(2,1)} %get-tuple-element.106), channel_id=1, source_target_pairs={{0,10},{2,8},{4,14},{6,12},{8,2},{10,0},{12,6},{14,4},{1,11},{3,9}... | collective-permute-start | bytes 602120 | tf_op jit(solution)/shard_map/ppermute | solution.py:467
  61.1 11.6 %collective-permute-start.20 = (bf16[784,128]{1,0:T(8,128)(2,1)}, bf16[784,128]{1,0:T(8,128)(2,1)}, u32[]{:S(2)}, u32[]{:S(2)}) collective-permute-start(bf16[784,128]{1,0:T(8,128)(2,1)} %get-tuple-element.107), channel_id=1, source_target_pairs={{0,12},{2,14},{4,0},{6,2},{8,4},{10,6},{12,8},{14,10},{1,13},{3,15... | collective-permute-start | bytes 602120 | tf_op jit(solution)/shard_map/ppermute | solution.py:467
  61.4 16.5 %collective-permute-start.21 = (bf16[784,128]{1,0:T(8,128)(2,1)}, bf16[784,128]{1,0:T(8,128)(2,1)}, u32[]{:S(2)}, u32[]{:S(2)}) collective-permute-start(bf16[784,128]{1,0:T(8,128)(2,1)} %get-tuple-element.108), channel_id=1, source_target_pairs={{0,14},{2,12},{4,2},{6,0},{8,6},{10,4},{12,10},{14,8},{1,15},{3,13... | collective-permute-start | bytes 602120 | tf_op jit(solution)/shard_map/ppermute | solution.py:467
  65.8 0.6 copy-start.2
  66.4 11.5 %copy-start.3 = (bf16[4,128,128]{2,1,0:T(8,128)(2,1)S(1)}, bf16[4,128,128]{2,1,0:T(8,128)(2,1)}, u32[]{:S(2)}) copy-start(bf16[4,128,128]{2,1,0:T(8,128)(2,1)} %copy-done.2) | copy-start | bytes 393220
  77.9 33.5 %copy-start.4 = (f32[16384]{0:T(1024)S(1)}, f32[16384]{0:T(1024)}, u32[]{:S(2)}) copy-start(f32[16384]{0:T(1024)} %param.7) | copy-start | bytes 196612
  77.9 33.5 %copy-start.5 = (f32[16384]{0:T(1024)S(1)}, f32[16384]{0:T(1024)}, u32[]{:S(2)}) copy-start(f32[16384]{0:T(1024)} %param.8) | copy-start | bytes 196612
  77.9 33.5 %copy-start.6 = (f32[16384]{0:T(1024)S(1)}, f32[16384]{0:T(1024)}, u32[]{:S(2)}) copy-start(f32[16384]{0:T(1024)} %param.9) | copy-start | bytes 196612

commit v8 on v7

--- a/solution.py
+++ b/solution.py
@@ -171,14 +171,14 @@
     return slot
 
 
-def partial_sums(chips, groups, g, r_refs, units):
+def partial_sums(chips, groups, g, r_refs, units, first=0):
     rolled = [pltpu.roll(units[d], LANES - g * groups, 1) for d in range(chips)]
     for k in range(groups):
         at = slice(k * GROUP_ROWS, (k + 1) * GROUP_ROWS)
         total = [jnp.zeros((8, LANES), jnp.float32)] * ROWS
         for d in range(chips):
             unit = jnp.broadcast_to(rolled[d][:, k : k + 1], (8, LANES))
-            code = r_refs[d][at, :].astype(jnp.float32)
+            code = r_refs[d][first + at.start : first + at.stop, :].astype(jnp.float32)
             for s in range(ROWS):
                 part = code[8 * s : 8 * s + 8]
                 size = jnp.floor(jnp.log2(jnp.abs(part)) * STEPS + (OFFSET * STEPS + 0.5))
@@ -199,7 +199,7 @@
         o_ref[0, at, :] = done
 
 
-def last_decode_kernel(chips, groups, count, *refs):
+def last_decode_kernel(chips, groups, count, each, *refs):
     r_refs, aux_refs, refs = refs[:chips], refs[chips : 2 * chips], refs[2 * chips :]
     *earlier, o_ref, buffer, units, spoilt, sems, early_sems = refs
     g = pl.program_id(0)
@@ -207,8 +207,19 @@
     start = o_ref.shape[0] - count
     blocks = [e.at[i] for e in earlier for i in range(e.shape[0])]
 
+    steps = count // each
+
     def copy(step, at):
-        return pltpu.make_async_copy(buffer.at[at], o_ref.at[slot_of(step + start)], sems.at[at])
+        return [
+            pltpu.make_async_copy(
+                buffer.at[at, e], o_ref.at[slot_of(step * each + e + start)], sems.at[at, e]
+            )
+            for e in range(each)
+        ]
+
+    def wait(several):
+        for one in several:
+            one.wait()
 
     early = [
         pltpu.make_async_copy(block, o_ref.at[slot_of(i)], early_sems.at[i])
@@ -227,26 +238,28 @@
 
     @pl.when(g >= 2)
     def _():
-        copy(g - 2, slot).wait()
-
-    for at, done in partial_sums(chips, groups, g, r_refs, units):
-        buffer[slot, at, :] = done
-    copy(g, slot).start()
-
-    @pl.when(g == count - 1)
-    def _():
-        if count >= 2:
-            copy(g - 1, 1 - slot).wait()
-        copy(g, slot).wait()
+        wait(copy(g - 2, slot))
+
+    rows = groups * GROUP_ROWS
+    for e in range(each):
+        for at, done in partial_sums(chips, groups, g * each + e, r_refs, units, e * rows):
+            buffer[slot, e, at, :] = done
+        copy(g, slot)[e].start()
+
+    @pl.when(g == steps - 1)
+    def _():
+        if steps >= 2:
+            wait(copy(g - 1, 1 - slot))
+        wait(copy(g, slot))
         for one in early:
             one.wait()
 
         @pl.when(spoilt[0] > 0)
         def _():
-            buffer[0] = jnp.full(buffer.shape[1:], jnp.nan, jnp.bfloat16)
+            buffer[0, 0] = jnp.full(buffer.shape[2:], jnp.nan, jnp.bfloat16)
 
             def spoil(j, carry):
-                one = pltpu.make_async_copy(buffer.at[0], o_ref.at[j], sems.at[0])
+                one = pltpu.make_async_copy(buffer.at[0, 0], o_ref.at[j], sems.at[0, 0])
                 one.start()
                 one.wait()
                 return carry
@@ -388,20 +401,21 @@
             cost_estimate=COST,
         )(received, received)
     replicas = count + sum(e.shape[0] for e in earlier)
+    each = 2 if count % 2 == 0 else 1
     return pl.pallas_call(
-        lambda *refs: last_decode_kernel(chips, groups, count, *refs),
+        lambda *refs: last_decode_kernel(chips, groups, count, each, *refs),
         name="last_decode_and_requantize",
-        grid=(count,),
-        in_specs=[pl.BlockSpec((rows, LANES), lambda g: (g, 0))] * chips
+        grid=(count // each,),
+        in_specs=[pl.BlockSpec((each * rows, LANES), lambda g: (g, 0))] * chips
         + [pl.BlockSpec((AUX_ROWS, LANES), lambda g: (count * rows // AUX_ROWS, 0))] * chips
         + [pl.BlockSpec(memory_space=pl.ANY)] * len(earlier),
         out_specs=pl.BlockSpec(memory_space=pl.ANY),
         out_shape=jax.ShapeDtypeStruct((replicas, rows, LANES), jnp.bfloat16),
         scratch_shapes=[
-            pltpu.VMEM((2, rows, LANES), jnp.bfloat16),
+            pltpu.VMEM((2, each, rows, LANES), jnp.bfloat16),
             units,
             pltpu.SMEM((1,), jnp.int32),
-            pltpu.SemaphoreType.DMA((2,)),
+            pltpu.SemaphoreType.DMA((2, each)),
             pltpu.SemaphoreType.DMA((replicas - count,)),
         ],
         compiler_params=PARAMS,

time: 114 us -> 113 us (level)
  no operation moved by 1% of the time
where the time goes in v8:
time: 113 us; the launch traced here: 112 us
  Pallas kernels  35.2 us (31%)
  blocking collectives  28.4 us (25%)
  starting transfers between devices  26.3 us (23%)
  waiting for transfers between devices  17.9 us (16%)
  local copies, waits for them, and re-layouts  2.97 us (3%)
    all_to_all x1, blocking collectives, body(): lax.all_to_all(partials[-1], GROUP_AXES[::-1], split_axis=0, concat_axis=...  28.4 us
    pallas_call x3, Pallas kernels, quantized(): pl.pallas_call(lambda *refs: pair_kernel(chips, groups, *refs), name='qua...  16.1 us
    ppermute x7, starting transfers between devices, body(): lax.ppermute(m, 'chip', [(c, other_chip(c, k)) for c in range(chips)])  11.5 us
    all_to_all x2, starting transfers between devices, body(): lax.all_to_all(messages[0], 'chip', split_axis=0, concat_axis=0, tiled=True)  11.2 us
    pallas_call x3, Pallas kernels, pair_sums(): pl.pallas_call(lambda *refs: encode_kernel(chips, rows // GROUP_ROWS, cou...  9.41 us
    ppermute x7, waiting for transfers between devices, body(): lax.ppermute(m, 'chip', [(c, other_chip(c, k)) for c in range(chips)])  9.38 us
    ppermute x15, waiting for transfers between devices, quantized(): lax.ppermute(a, 'core', [(0, 1), (1, 0)])  6.24 us
    pallas_call x2, Pallas kernels, node_sums(): pl.pallas_call(lambda *refs: decode_kernel(chips, groups, *refs), name='d...  4.49 us
  transfers between devices with their start and end apart: 24, of which 8 were waited for; matrix products, arithmetic and copies ran while one was open for 0% of the time, Pallas kernels for 21%

profile of v8, /device:TPU:2, one launch (start us, length us, event | category | flops | bytes accessed | tf_op | source)
XLA Modules:
  0.0 112.4 jit_solution(15758182115632216808)
XLA Ops:
  0.6 0.1 stack.46.refs_0_
  0.7 4.1 %quantize.3 = (bf16[8,4,128,128]{3,2,1,0:T(8,128)(2,1)S(1)}, bf16[2,4,128,128]{3,2,1,0:T(8,128)(2,1)S(1)}, bf16[2,4,128,128]{3,2,1,0:T(8,128)(2,1)S(1)}, bf16[2,...) custom-call(s32[9]{0:T(128)S(1)} %stack.46.refs_0_, ...), custom_call_target="tpu_custom_call" | custom-call | flops 1 | bytes 1 | tf_op jit(solution)/shard_map/quantize/pallas_call | solution.py:335
  4.9 0.1 collective-permute-start.1
  5.0 0.5 collective-permute-start.2
  5.5 0.1 collective-permute-start.3
  5.6 0.4 collective-permute-start.4
  6.0 0.1 collective-permute-start
  6.1 1.6 %collective-permute-done.refs_2_ = f32[4,8,128]{2,1,0:T(8,128)S(1)} collective-permute-done((f32[4,8,128]{2,1,0:T(8,128)S(1)}, f32[4,8,128]{2,1,0:T(8,128)S(1)}, u32[]{:S(2)}, u32[]{:S(2)}) %collective-permute-start) | collective-permute-done | bytes 16416 | tf_op jit(solution)/shard_map/ppermute | solution.py:350
  7.6 0.0 collective-permute-done.1.refs_4_
  7.6 0.0 collective-permute-done.2.refs_5_
  7.6 0.0 collective-permute-done.3.refs_6_
  7.7 0.0 collective-permute-done.4.refs_7_
  7.7 1.8 %add_and_encode.3 = (bf16[8,528,128]{2,1,0:T(8,128)(2,1)S(1)}, f32[8,128]{1,0:T(8,128)S(1)}) custom-call(bf16[8,4,128,128]{3,2,1,0:T(8,128)(2,1)S(1)} %get-tuple-element.81.refs_0_, f32[4,8,128]{2,1,0:T(8,128)S(1)} %get-tuple-element.82.refs_1_, f32[4,8,128]{2,1,0:T(8,128)S(1)} %collective-permute-done.refs_2_, ...), custom_call_target="tpu_custom_call" | custom-call | flops 1 | bytes 1 | tf_op jit(solution)/shard_map/add_and_encode/pallas_call | solution.py:363
  9.5 1.0 copy-done.1
  10.5 5.8 %all-to-all-start.2 = ((bf16[8,528,128]{2,1,0:T(8,128)(2,1)}), bf16[8,528,128]{2,1,0:T(8,128)(2,1)S(1)}, u32[]{:S(2)}, u32[]{:S(2)}) async-start(bf16[8,528,128]{2,1,0:T(8,128)(2,1)} %copy-done.1), calls=%async_computation.2 | async-start | bytes 2162688 | tf_op jit(solution)/shard_map/all_to_all | solution.py:485
  16.3 6.0 %quantize.4 = (bf16[8,6,128,128]{3,2,1,0:T(8,128)(2,1)S(1)}, bf16[2,6,128,128]{3,2,1,0:T(8,128)(2,1)S(1)}, bf16[2,6,128,128]{3,2,1,0:T(8,128)(2,1)S(1)}, bf16[2,...) custom-call(s32[9]{0:T(128)S(1)} %stack.46.refs_0_, ...), custom_call_target="tpu_custom_call" | custom-call | flops 1 | bytes 1 | tf_op jit(solution)/shard_map/quantize/pallas_call | solution.py:335
  22.3 0.1 collective-permute-start.6
  22.4 0.5 collective-permute-start.7
  22.9 0.1 collective-permute-start.8
  23.0 0.4 collective-permute-start.9
  23.4 0.1 collective-permute-start.5
  23.5 2.3 %collective-permute-done.5.refs_2_ = f32[6,8,128]{2,1,0:T(8,128)S(1)} collective-permute-done((f32[6,8,128]{2,1,0:T(8,128)S(1)}, f32[6,8,128]{2,1,0:T(8,128)S(1)}, u32[]{:S(2)}, u32[]{:S(2)}) %collective-permute-start.5) | collective-permute-done | bytes 24608 | tf_op jit(solution)/shard_map/ppermute | solution.py:350
  25.8 0.0 collective-permute-done.6.refs_4_
  25.8 0.0 collective-permute-done.7.refs_5_
  25.8 0.0 collective-permute-done.8.refs_6_
  25.8 0.0 collective-permute-done.9.refs_7_
  25.8 2.6 %add_and_encode.4 = (bf16[8,784,128]{2,1,0:T(8,128)(2,1)S(1)}, f32[8,128]{1,0:T(8,128)S(1)}) custom-call(bf16[8,6,128,128]{3,2,1,0:T(8,128)(2,1)S(1)} %get-tuple-element.88.refs_0_, f32[6,8,128]{2,1,0:T(8,128)S(1)} %get-tuple-element.89.refs_1_, f32[6,8,128]{2,1,0:T(8,128)S(1)} %collective-permute-done.5.refs_2_, ...), custom_call_target="tpu_custom_call" | custom-call | flops 1 | bytes 1 | tf_op jit(solution)/shard_map/add_and_encode/pallas_call | solution.py:363
  28.5 1.2 %copy-done = bf16[8,784,128]{2,1,0:T(8,128)(2,1)} copy-done((bf16[8,784,128]{2,1,0:T(8,128)(2,1)}, bf16[8,784,128]{2,1,0:T(8,128)(2,1)S(1)}, u32[]{:S(2)}) %copy-start) | copy-done | bytes 1605656
  29.6 2.2 %all-to-all-done.2.refs_0_.refs_1_ = bf16[8,528,128]{2,1,0:T(8,128)(2,1)S(1)} async-done(((bf16[8,528,128]{2,1,0:T(8,128)(2,1)}), bf16[8,528,128]{2,1,0:T(8,128)(2,1)S(1)}, u32[]{:S(2)}, u32[]{:S(2)}) %all-to-all-start.2) | async-done | bytes 1081376 | tf_op jit(solution)/shard_map/all_to_all | solution.py:485
  31.9 5.4 %all-to-all-start.3 = ((bf16[8,784,128]{2,1,0:T(8,128)(2,1)}), bf16[8,784,128]{2,1,0:T(8,128)(2,1)S(1)}, u32[]{:S(2)}, u32[]{:S(2)}) async-start(bf16[8,784,128]{2,1,0:T(8,128)(2,1)} %copy-done), calls=%async_computation.3 | async-start | bytes 3211264 | tf_op jit(solution)/shard_map/all_to_all | solution.py:485
  37.2 0.1 stack.45.refs_0_
  37.3 6.0 %quantize.5 = (bf16[8,6,128,128]{3,2,1,0:T(8,128)(2,1)S(1)}, bf16[2,6,128,128]{3,2,1,0:T(8,128)(2,1)S(1)}, bf16[2,6,128,128]{3,2,1,0:T(8,128)(2,1)S(1)}, bf16[2,...) custom-call(s32[9]{0:T(128)S(1)} %stack.45.refs_0_, ...), custom_call_target="tpu_custom_call" | custom-call | flops 1 | bytes 1 | tf_op jit(solution)/shard_map/quantize/pallas_call | solution.py:335
  43.3 0.1 collective-permute-start.11
  43.4 0.5 collective-permute-start.12
  43.9 0.1 collective-permute-start.13
  44.0 0.4 collective-permute-start.14
  44.4 0.1 collective-permute-start.10
  44.5 2.3 %collective-permute-done.10.refs_2_ = f32[6,8,128]{2,1,0:T(8,128)S(1)} collective-permute-done((f32[6,8,128]{2,1,0:T(8,128)S(1)}, f32[6,8,128]{2,1,0:T(8,128)S(1)}, u32[]{:S(2)}, u32[]{:S(2)}) %collective-permute-start.10) | collective-permute-done | bytes 24608 | tf_op jit(solution)/shard_map/ppermute | solution.py:350
  46.8 0.0 collective-permute-done.11.refs_4_
  46.8 0.0 collective-permute-done.12.refs_5_
  46.8 0.0 collective-permute-done.13.refs_6_
  46.9 0.0 collective-permute-done.14.refs_7_
  46.9 5.0 %add_and_encode.5 = (bf16[784,128]{1,0:T(8,128)(2,1)S(1)}, bf16[784,128]{1,0:T(8,128)(2,1)S(1)}, bf16[784,128]{1,0:T(8,128)(2,1)S(1)}, bf16[784,128]{1,0:T(8,128...) custom-call(bf16[8,6,128,128]{3,2,1,0:T(8,128)(2,1)S(1)} %get-tuple-, ...), custom_call_target="tpu_custom_call" | custom-call | flops 1 | bytes 1 | tf_op jit(solution)/shard_map/add_and_encode/pallas_call | solution.py:363
  51.9 1.6 %collective-permute-start.15 = (bf16[784,128]{1,0:T(8,128)(2,1)S(1)}, bf16[784,128]{1,0:T(8,128)(2,1)S(1)}, u32[]{:S(2)}, u32[]{:S(2)}) collective-permute-start(bf16[784,128]{1,0:T(8,128)(2,1)S(1)} %get-tuple-element.102), channel_id=1, source_target_pairs={{0,2},{2,0},{4,6},{6,4},{8,10},{10,8},{12,14},{14,12},{1,3},{3,1},... | collective-permute-start | bytes 602120 | tf_op jit(solution)/shard_map/ppermute | solution.py:481
  53.4 1.5 %collective-permute-start.16 = (bf16[784,128]{1,0:T(8,128)(2,1)S(1)}, bf16[784,128]{1,0:T(8,128)(2,1)S(1)}, u32[]{:S(2)}, u32[]{:S(2)}) collective-permute-start(bf16[784,128]{1,0:T(8,128)(2,1)S(1)} %get-tuple-element.103), channel_id=1, source_target_pairs={{0,4},{2,6},{4,8},{6,10},{8,12},{10,14},{12,0},{14,2},{1,5},{3,7},... | collective-permute-start | bytes 602120 | tf_op jit(solution)/shard_map/ppermute | solution.py:481
  54.9 1.2 %collective-permute-start.17 = (bf16[784,128]{1,0:T(8,128)(2,1)}, bf16[784,128]{1,0:T(8,128)(2,1)S(1)}, u32[]{:S(2)}, u32[]{:S(2)}) collective-permute-start(bf16[784,128]{1,0:T(8,128)(2,1)} %get-tuple-element.104), channel_id=1, source_target_pairs={{0,6},{2,4},{4,10},{6,8},{8,14},{10,12},{12,2},{14,0},{1,7},{3,5},... | collective-permute-start | bytes 602120 | tf_op jit(solution)/shard_map/ppermute | solution.py:481
  56.1 1.4 %collective-permute-start.18 = (bf16[784,128]{1,0:T(8,128)(2,1)}, bf16[784,128]{1,0:T(8,128)(2,1)}, u32[]{:S(2)}, u32[]{:S(2)}) collective-permute-start(bf16[784,128]{1,0:T(8,128)(2,1)} %get-tuple-element.105), channel_id=1, source_target_pairs={{0,8},{2,10},{4,12},{6,14},{8,0},{10,2},{12,4},{14,6},{1,9},{3,11}... | collective-permute-start | bytes 602120 | tf_op jit(solution)/shard_map/ppermute | solution.py:481
  57.5 3.0 %collective-permute-start.19 = (bf16[784,128]{1,0:T(8,128)(2,1)}, bf16[784,128]{1,0:T(8,128)(2,1)}, u32[]{:S(2)}, u32[]{:S(2)}) collective-permute-start(bf16[784,128]{1,0:T(8,128)(2,1)} %get-tuple-element.106), channel_id=1, source_target_pairs={{0,10},{2,8},{4,14},{6,12},{8,2},{10,0},{12,6},{14,4},{1,11},{3,9}... | collective-permute-start | bytes 602120 | tf_op jit(solution)/shard_map/ppermute | solution.py:481
  60.5 0.6 collective-permute-done.15.refs_1_.refs_9_
  61.1 0.2 collective-permute-start.20
  61.4 0.0 collective-permute-done.16.refs_2_.refs_10_
  61.4 2.6 %collective-permute-start.21 = (bf16[784,128]{1,0:T(8,128)(2,1)}, bf16[784,128]{1,0:T(8,128)(2,1)}, u32[]{:S(2)}, u32[]{:S(2)}) collective-permute-start(bf16[784,128]{1,0:T(8,128)(2,1)} %get-tuple-element.108), channel_id=1, source_target_pairs={{0,14},{2,12},{4,2},{6,0},{8,6},{10,4},{12,10},{14,8},{1,15},{3,13... | collective-permute-start | bytes 602120 | tf_op jit(solution)/shard_map/ppermute | solution.py:481
  64.0 1.8 %decode_and_requantize.2.refs_16_ = bf16[4,128,128]{2,1,0:T(8,128)(2,1)S(1)} custom-call(bf16[8,528,128]{2,1,0:T(8,128)(2,1)S(1)} %all-to-all-done.2.refs_0_.refs_1_, bf16[8,528,128]{2,1,0:T(8,128)(2,1)S(1)} %all-to-all-done.2.refs_0_.refs_1_), custom_call_target="tpu_custom_call" | custom-call | flops 1 | bytes 1 | tf_op jit(solution)/shard_map/decode_and_requantize/pallas_call | solution.py:392
  65.8 0.6 copy-done.2
  66.4 2.7 %decode_and_requantize.3.refs_17_ = bf16[6,128,128]{2,1,0:T(8,128)(2,1)S(1)} custom-call(bf16[8,784,128]{2,1,0:T(8,128)(2,1)S(1)} %all-to-all-done.3.refs_0_.refs_1_, bf16[8,784,128]{2,1,0:T(8,128)(2,1)S(1)} %all-to-all-done.3.refs_0_.refs_1_), custom_call_target="tpu_custom_call" | custom-call | flops 1 | bytes 1 | tf_op jit(solution)/shard_map/decode_and_requantize/pallas_call | solution.py:392
  69.1 0.0 collective-permute-done.17.refs_3_.refs_11_
  69.1 0.0 collective-permute-done.18.refs_4_.refs_12_
  69.1 1.9 %collective-permute-done.19.refs_5_.refs_13_ = bf16[784,128]{1,0:T(8,128)(2,1)} collective-permute-done((bf16[784,128]{1,0:T(8,128)(2,1)}, bf16[784,128]{1,0:T(8,128)(2,1)}, u32[]{:S(2)}, u32[]{:S(2)}) %collective-permute-start.19) | collective-permute-done | bytes 200736 | tf_op jit(solution)/shard_map/ppermute | solution.py:481
  71.1 1.7 %collective-permute-done.20.refs_6_.refs_14_ = bf16[784,128]{1,0:T(8,128)(2,1)} collective-permute-done((bf16[784,128]{1,0:T(8,128)(2,1)}, bf16[784,128]{1,0:T(8,128)(2,1)}, u32[]{:S(2)}, u32[]{:S(2)}) %collective-permute-start.20) | collective-permute-done | bytes 200736 | tf_op jit(solution)/shard_map/ppermute | solution.py:481
  72.8 5.1 %collective-permute-done.21.refs_7_.refs_15_ = bf16[784,128]{1,0:T(8,128)(2,1)} collective-permute-done((bf16[784,128]{1,0:T(8,128)(2,1)}, bf16[784,128]{1,0:T(8,128)(2,1)}, u32[]{:S(2)}, u32[]{:S(2)}) %collective-permute-start.21) | collective-permute-done | bytes 200736 | tf_op jit(solution)/shard_map/ppermute | solution.py:481
  77.9 4.5 %last_decode_and_requantize.1 = bf16[16,128,128]{2,1,0:T(8,128)(2,1)S(1)} custom-call(bf16[784,128]{1,0:T(8,128)(2,1)S(1)} %get-tuple-element.101.refs_0_.refs_8_, bf16[784,128]{1,0:T(8,128)(2,1)S(1)} %collective-permute-done.15.refs_1_.refs_9_, bf16[784,128]{1,0:T(8,128)(2,1)S(1)} %collective-permute-done.16.refs_2_.refs_10_, ...), custom_call_target="tpu_custom_call" | custom-call | flops 1 | bytes 1 | tf_op jit(solution)/shard_map/last_decode_and_requantize/pallas_call | solution.py:405
  82.4 28.4 %all_to_all.24.refs_0_ = bf16[16,128,128]{2,1,0:T(8,128)(2,1)S(1)} all-to-all(bf16[16,128,128]{2,1,0:T(8,128)(2,1)S(1)} %last_decode_and_requantize.1), channel_id=1, replica_groups=mesh['group3'=2,'group2'=2,'group1'=2,'group0'=2,'chip'=8,'core'=2] {'gr..., dimensions={0} | all-to-all | bytes 1048576 | tf_op jit(solution)/shard_map/all_to_all | solution.py:488
  110.8 0.8 adamw_update.3
  111.6 0.7 while.13
  (13 shorter events, 0.0 us)
Async XLA Ops:
  4.9 2.8 %collective-permute-start.1 = (bf16[2,4,128,128]{3,2,1,0:T(8,128)(2,1)S(1)}, bf16[2,4,128,128]{3,2,1,0:T(8,128)(2,1)S(1)}, u32[]{:S(2)}, u32[]{:S(2)}) collective-permute-start(bf16[2,4,128,128]{3,2,1,0:T(8,128)(2,1)S(1)} %get-tuple-element.83), channel_id=1, source_target_pairs={{0,1},{1,0},{2,3},{3,2},{4,5},{5,4},{6,7},{7,6},{8,9},{9,8},{10,11... | collective-permute-start | bytes 786440 | tf_op jit(solution)/shard_map/ppermute | solution.py:350
  5.0 2.7 %collective-permute-start.2 = (bf16[2,4,128,128]{3,2,1,0:T(8,128)(2,1)S(1)}, bf16[2,4,128,128]{3,2,1,0:T(8,128)(2,1)S(1)}, u32[]{:S(2)}, u32[]{:S(2)}) collective-permute-start(bf16[2,4,128,128]{3,2,1,0:T(8,128)(2,1)S(1)} %get-tuple-element.84), channel_id=1, source_target_pairs={{0,1},{1,0},{2,3},{3,2},{4,5},{5,4},{6,7},{7,6},{8,9},{9,8},{10,11... | collective-permute-start | bytes 786440 | tf_op jit(solution)/shard_map/ppermute | solution.py:350
  5.5 2.2 %collective-permute-start.3 = (bf16[2,4,128,128]{3,2,1,0:T(8,128)(2,1)S(1)}, bf16[2,4,128,128]{3,2,1,0:T(8,128)(2,1)S(1)}, u32[]{:S(2)}, u32[]{:S(2)}) collective-permute-start(bf16[2,4,128,128]{3,2,1,0:T(8,128)(2,1)S(1)} %get-tuple-element.85), channel_id=1, source_target_pairs={{0,1},{1,0},{2,3},{3,2},{4,5},{5,4},{6,7},{7,6},{8,9},{9,8},{10,11... | collective-permute-start | bytes 786440 | tf_op jit(solution)/shard_map/ppermute | solution.py:350
  5.6 2.1 %collective-permute-start.4 = (bf16[2,4,128,128]{3,2,1,0:T(8,128)(2,1)S(1)}, bf16[2,4,128,128]{3,2,1,0:T(8,128)(2,1)S(1)}, u32[]{:S(2)}, u32[]{:S(2)}) collective-permute-start(bf16[2,4,128,128]{3,2,1,0:T(8,128)(2,1)S(1)} %get-tuple-element.86), channel_id=1, source_target_pairs={{0,1},{1,0},{2,3},{3,2},{4,5},{5,4},{6,7},{7,6},{8,9},{9,8},{10,11... | collective-permute-start | bytes 786440 | tf_op jit(solution)/shard_map/ppermute | solution.py:350
  6.0 1.7 %collective-permute-start = (f32[4,8,128]{2,1,0:T(8,128)S(1)}, f32[4,8,128]{2,1,0:T(8,128)S(1)}, u32[]{:S(2)}, u32[]{:S(2)}) collective-permute-start(f32[4,8,128]{2,1,0:T(8,128)S(1)} %get-tuple-element.82.refs_1_), channel_id=1, source_target_pairs={{0,1},{1,0},{2,3},{3,2},{4,5},{5,4},{6,7},{7,6},{8,9},{9,8},{10,11... | collective-permute-start | bytes 49160 | tf_op jit(solution)/shard_map/ppermute | solution.py:350
  9.5 1.0 copy-start.1
  10.5 21.4 %all-to-all-start.2 = ((bf16[8,528,128]{2,1,0:T(8,128)(2,1)}), bf16[8,528,128]{2,1,0:T(8,128)(2,1)S(1)}, u32[]{:S(2)}, u32[]{:S(2)}) async-start(bf16[8,528,128]{2,1,0:T(8,128)(2,1)} %copy-done.1), calls=%async_computation.2 | async-start | bytes 2162688 | tf_op jit(solution)/shard_map/all_to_all | solution.py:485
  22.3 3.5 %collective-permute-start.6 = (bf16[2,6,128,128]{3,2,1,0:T(8,128)(2,1)S(1)}, bf16[2,6,128,128]{3,2,1,0:T(8,128)(2,1)S(1)}, u32[]{:S(2)}, u32[]{:S(2)}) collective-permute-start(bf16[2,6,128,128]{3,2,1,0:T(8,128)(2,1)S(1)} %get-tuple-element.90), channel_id=1, source_target_pairs={{0,1},{1,0},{2,3},{3,2},{4,5},{5,4},{6,7},{7,6},{8,9},{9,8},{10,11... | collective-permute-start | bytes 1179656 | tf_op jit(solution)/shard_map/ppermute | solution.py:350
  22.4 3.4 %collective-permute-start.7 = (bf16[2,6,128,128]{3,2,1,0:T(8,128)(2,1)S(1)}, bf16[2,6,128,128]{3,2,1,0:T(8,128)(2,1)S(1)}, u32[]{:S(2)}, u32[]{:S(2)}) collective-permute-start(bf16[2,6,128,128]{3,2,1,0:T(8,128)(2,1)S(1)} %get-tuple-element.91), channel_id=1, source_target_pairs={{0,1},{1,0},{2,3},{3,2},{4,5},{5,4},{6,7},{7,6},{8,9},{9,8},{10,11... | collective-permute-start | bytes 1179656 | tf_op jit(solution)/shard_map/ppermute | solution.py:350
  22.9 2.9 %collective-permute-start.8 = (bf16[2,6,128,128]{3,2,1,0:T(8,128)(2,1)S(1)}, bf16[2,6,128,128]{3,2,1,0:T(8,128)(2,1)S(1)}, u32[]{:S(2)}, u32[]{:S(2)}) collective-permute-start(bf16[2,6,128,128]{3,2,1,0:T(8,128)(2,1)S(1)} %get-tuple-element.92), channel_id=1, source_target_pairs={{0,1},{1,0},{2,3},{3,2},{4,5},{5,4},{6,7},{7,6},{8,9},{9,8},{10,11... | collective-permute-start | bytes 1179656 | tf_op jit(solution)/shard_map/ppermute | solution.py:350
  23.0 2.8 %collective-permute-start.9 = (bf16[2,6,128,128]{3,2,1,0:T(8,128)(2,1)S(1)}, bf16[2,6,128,128]{3,2,1,0:T(8,128)(2,1)S(1)}, u32[]{:S(2)}, u32[]{:S(2)}) collective-permute-start(bf16[2,6,128,128]{3,2,1,0:T(8,128)(2,1)S(1)} %get-tuple-element.93), channel_id=1, source_target_pairs={{0,1},{1,0},{2,3},{3,2},{4,5},{5,4},{6,7},{7,6},{8,9},{9,8},{10,11... | collective-permute-start | bytes 1179656 | tf_op jit(solution)/shard_map/ppermute | solution.py:350
  23.4 2.4 %collective-permute-start.5 = (f32[6,8,128]{2,1,0:T(8,128)S(1)}, f32[6,8,128]{2,1,0:T(8,128)S(1)}, u32[]{:S(2)}, u32[]{:S(2)}) collective-permute-start(f32[6,8,128]{2,1,0:T(8,128)S(1)} %get-tuple-element.89.refs_1_), channel_id=1, source_target_pairs={{0,1},{1,0},{2,3},{3,2},{4,5},{5,4},{6,7},{7,6},{8,9},{9,8},{10,11... | collective-permute-start | bytes 73736 | tf_op jit(solution)/shard_map/ppermute | solution.py:350
  28.5 1.2 %copy-start = (bf16[8,784,128]{2,1,0:T(8,128)(2,1)}, bf16[8,784,128]{2,1,0:T(8,128)(2,1)S(1)}, u32[]{:S(2)}) copy-start(bf16[8,784,128]{2,1,0:T(8,128)(2,1)S(1)} %get-tuple-element.110) | copy-start | bytes 4816900
  31.9 34.5 %all-to-all-start.3 = ((bf16[8,784,128]{2,1,0:T(8,128)(2,1)}), bf16[8,784,128]{2,1,0:T(8,128)(2,1)S(1)}, u32[]{:S(2)}, u32[]{:S(2)}) async-start(bf16[8,784,128]{2,1,0:T(8,128)(2,1)} %copy-done), calls=%async_computation.3 | async-start | bytes 3211264 | tf_op jit(solution)/shard_map/all_to_all | solution.py:485
  43.3 3.5 %collective-permute-start.11 = (bf16[2,6,128,128]{3,2,1,0:T(8,128)(2,1)S(1)}, bf16[2,6,128,128]{3,2,1,0:T(8,128)(2,1)S(1)}, u32[]{:S(2)}, u32[]{:S(2)}) collective-permute-start(bf16[2,6,128,128]{3,2,1,0:T(8,128)(2,1)S(1)} %get-tuple-element.97), channel_id=1, source_target_pairs={{0,1},{1,0},{2,3},{3,2},{4,5},{5,4},{6,7},{7,6},{8,9},{9,8},{10,11... | collective-permute-start | bytes 1179656 | tf_op jit(solution)/shard_map/ppermute | solution.py:350
  43.4 3.4 %collective-permute-start.12 = (bf16[2,6,128,128]{3,2,1,0:T(8,128)(2,1)S(1)}, bf16[2,6,128,128]{3,2,1,0:T(8,128)(2,1)S(1)}, u32[]{:S(2)}, u32[]{:S(2)}) collective-permute-start(bf16[2,6,128,128]{3,2,1,0:T(8,128)(2,1)S(1)} %get-tuple-element.98), channel_id=1, source_target_pairs={{0,1},{1,0},{2,3},{3,2},{4,5},{5,4},{6,7},{7,6},{8,9},{9,8},{10,11... | collective-permute-start | bytes 1179656 | tf_op jit(solution)/shard_map/ppermute | solution.py:350
  43.9 2.9 %collective-permute-start.13 = (bf16[2,6,128,128]{3,2,1,0:T(8,128)(2,1)S(1)}, bf16[2,6,128,128]{3,2,1,0:T(8,128)(2,1)S(1)}, u32[]{:S(2)}, u32[]{:S(2)}) collective-permute-start(bf16[2,6,128,128]{3,2,1,0:T(8,128)(2,1)S(1)} %get-tuple-element.99), channel_id=1, source_target_pairs={{0,1},{1,0},{2,3},{3,2},{4,5},{5,4},{6,7},{7,6},{8,9},{9,8},{10,11... | collective-permute-start | bytes 1179656 | tf_op jit(solution)/shard_map/ppermute | solution.py:350
  44.0 2.8 %collective-permute-start.14 = (bf16[2,6,128,128]{3,2,1,0:T(8,128)(2,1)S(1)}, bf16[2,6,128,128]{3,2,1,0:T(8,128)(2,1)S(1)}, u32[]{:S(2)}, u32[]{:S(2)}) collective-permute-start(bf16[2,6,128,128]{3,2,1,0:T(8,128)(2,1)S(1)} %get-tuple-element.100), channel_id=1, source_target_pairs={{0,1},{1,0},{2,3},{3,2},{4,5},{5,4},{6,7},{7,6},{8,9},{9,8},{10,11... | collective-permute-start | bytes 1179656 | tf_op jit(solution)/shard_map/ppermute | solution.py:350
  44.4 2.4 %collective-permute-start.10 = (f32[6,8,128]{2,1,0:T(8,128)S(1)}, f32[6,8,128]{2,1,0:T(8,128)S(1)}, u32[]{:S(2)}, u32[]{:S(2)}) collective-permute-start(f32[6,8,128]{2,1,0:T(8,128)S(1)} %get-tuple-element.96.refs_1_), channel_id=1, source_target_pairs={{0,1},{1,0},{2,3},{3,2},{4,5},{5,4},{6,7},{7,6},{8,9},{9,8},{10,11... | collective-permute-start | bytes 73736 | tf_op jit(solution)/shard_map/ppermute | solution.py:350
  51.9 9.3 %collective-permute-start.15 = (bf16[784,128]{1,0:T(8,128)(2,1)S(1)}, bf16[784,128]{1,0:T(8,128)(2,1)S(1)}, u32[]{:S(2)}, u32[]{:S(2)}) collective-permute-start(bf16[784,128]{1,0:T(8,128)(2,1)S(1)} %get-tuple-element.102), channel_id=1, source_target_pairs={{0,2},{2,0},{4,6},{6,4},{8,10},{10,8},{12,14},{14,12},{1,3},{3,1},... | collective-permute-start | bytes 602120 | tf_op jit(solution)/shard_map/ppermute | solution.py:481
  53.4 7.9 %collective-permute-start.16 = (bf16[784,128]{1,0:T(8,128)(2,1)S(1)}, bf16[784,128]{1,0:T(8,128)(2,1)S(1)}, u32[]{:S(2)}, u32[]{:S(2)}) collective-permute-start(bf16[784,128]{1,0:T(8,128)(2,1)S(1)} %get-tuple-element.103), channel_id=1, source_target_pairs={{0,4},{2,6},{4,8},{6,10},{8,12},{10,14},{12,0},{14,2},{1,5},{3,7},... | collective-permute-start | bytes 602120 | tf_op jit(solution)/shard_map/ppermute | solution.py:481
  54.9 14.2 %collective-permute-start.17 = (bf16[784,128]{1,0:T(8,128)(2,1)}, bf16[784,128]{1,0:T(8,128)(2,1)S(1)}, u32[]{:S(2)}, u32[]{:S(2)}) collective-permute-start(bf16[784,128]{1,0:T(8,128)(2,1)} %get-tuple-element.104), channel_id=1, source_target_pairs={{0,6},{2,4},{4,10},{6,8},{8,14},{10,12},{12,2},{14,0},{1,7},{3,5},... | collective-permute-start | bytes 602120 | tf_op jit(solution)/shard_map/ppermute | solution.py:481
  56.1 13.1 %collective-permute-start.18 = (bf16[784,128]{1,0:T(8,128)(2,1)}, bf16[784,128]{1,0:T(8,128)(2,1)}, u32[]{:S(2)}, u32[]{:S(2)}) collective-permute-start(bf16[784,128]{1,0:T(8,128)(2,1)} %get-tuple-element.105), channel_id=1, source_target_pairs={{0,8},{2,10},{4,12},{6,14},{8,0},{10,2},{12,4},{14,6},{1,9},{3,11}... | collective-permute-start | bytes 602120 | tf_op jit(solution)/shard_map/ppermute | solution.py:481
  57.5 13.6 %collective-permute-start.19 = (bf16[784,128]{1,0:T(8,128)(2,1)}, bf16[784,128]{1,0:T(8,128)(2,1)}, u32[]{:S(2)}, u32[]{:S(2)}) collective-permute-start(bf16[784,128]{1,0:T(8,128)(2,1)} %get-tuple-element.106), channel_id=1, source_target_pairs={{0,10},{2,8},{4,14},{6,12},{8,2},{10,0},{12,6},{14,4},{1,11},{3,9}... | collective-permute-start | bytes 602120 | tf_op jit(solution)/shard_map/ppermute | solution.py:481
  61.1 11.6 %collective-permute-start.20 = (bf16[784,128]{1,0:T(8,128)(2,1)}, bf16[784,128]{1,0:T(8,128)(2,1)}, u32[]{:S(2)}, u32[]{:S(2)}) collective-permute-start(bf16[784,128]{1,0:T(8,128)(2,1)} %get-tuple-element.107), channel_id=1, source_target_pairs={{0,12},{2,14},{4,0},{6,2},{8,4},{10,6},{12,8},{14,10},{1,13},{3,15... | collective-permute-start | bytes 602120 | tf_op jit(solution)/shard_map/ppermute | solution.py:481
  61.4 16.5 %collective-permute-start.21 = (bf16[784,128]{1,0:T(8,128)(2,1)}, bf16[784,128]{1,0:T(8,128)(2,1)}, u32[]{:S(2)}, u32[]{:S(2)}) collective-permute-start(bf16[784,128]{1,0:T(8,128)(2,1)} %get-tuple-element.108), channel_id=1, source_target_pairs={{0,14},{2,12},{4,2},{6,0},{8,6},{10,4},{12,10},{14,8},{1,15},{3,13... | collective-permute-start | bytes 602120 | tf_op jit(solution)/shard_map/ppermute | solution.py:481
  65.8 0.6 copy-start.2
  66.4 11.5 %copy-start.3 = (bf16[4,128,128]{2,1,0:T(8,128)(2,1)S(1)}, bf16[4,128,128]{2,1,0:T(8,128)(2,1)}, u32[]{:S(2)}) copy-start(bf16[4,128,128]{2,1,0:T(8,128)(2,1)} %copy-done.2) | copy-start | bytes 393220
  77.9 32.9 %copy-start.4 = (f32[16384]{0:T(1024)S(1)}, f32[16384]{0:T(1024)}, u32[]{:S(2)}) copy-start(f32[16384]{0:T(1024)} %param.7) | copy-start | bytes 196612
  77.9 32.9 %copy-start.5 = (f32[16384]{0:T(1024)S(1)}, f32[16384]{0:T(1024)}, u32[]{:S(2)}) copy-start(f32[16384]{0:T(1024)} %param.8) | copy-start | bytes 196612
  77.9 32.9 %copy-start.6 = (f32[16384]{0:T(1024)S(1)}, f32[16384]{0:T(1024)}, u32[]{:S(2)}) copy-start(f32[16384]{0:T(1024)} %param.9) | copy-start | bytes 196612
